TPU v7x, 128 devices: a whole 4x4x4 slice. The times are simulated.
128 devices in a mesh: row: 16 (over y, x), col: 8 (over z, core).
Axes of the slice: x: 4, y: 4, z: 4, core: 2. Of those that a mesh axis runs over, the one named last changes fastest.
Arguments:
- inputs: bfloat16 [1, 256, 256, 512], P(None, 'row', 'col'), may hold values from -30 to 30, as said below
- out_grad: bfloat16 [1, 256, 256, 512], P(None, 'row', 'col'), may hold values from -6 to 6
- w_expand: bfloat16 [512, 2048], replicated, may hold values from -0.25 to 0.25
- dw_kernel: float32 [3, 3, 2048], replicated, may hold values from -2 to 2
- se_reduce: float32 [2048, 128], replicated, may hold values from -0.125 to 0.125
- se_expand: float32 [128, 2048], replicated, may hold values from -0.5 to 0.5
- w_project: bfloat16 [2048, 512], replicated, may hold values from -0.125 to 0.125
- w_qkv: bfloat16 [512, 1536], replicated, may hold values from -0.25 to 0.25
- w_out: bfloat16 [512, 512], replicated, may hold values from -0.25 to 0.25
- pos_table: float32 [16, 225], replicated, may hold values from -4 to 320
Outputs:
- block_out: bfloat16 [1, 256, 256, 512], P(None, 'row', 'col')
- input_gradient: bfloat16 [1, 256, 256, 512], P(None, 'row', 'col')
- expand_grad: float32 [512, 2048], P(('row', 'col'))
- project_grad: float32 [2048, 512], P(('row', 'col'))
- qkv_grad: float32 [512, 1536], P(('row', 'col'))
- out_proj_grad: float32 [512, 512], P(('row', 'col'))
- kernel_grad: float32 [3, 3, 2048], replicated
- se_reduce_grad: float32 [2048, 128], replicated
- se_expand_grad: float32 [128, 2048], replicated
- table_grad: float32 [16, 225], replicated
Inputs may be any that keep to these rules, and one draw needn't show every extreme that they name: `inputs`: activations of the block's input.
All inputs are finite; a program needn't handle non-finite values.
Results may differ from a plain program's by a relative error of at most 0.015.
Values may be sent and summed in bfloat16 or wider, within the bound.
A program may use at most 192 MiB of HBM per device.

v0:
```python
import functools
import math

import jax
import jax.numpy as jnp
from jax import lax
from jax.experimental import pallas as pl
from jax.experimental.pallas import tpu as pltpu
from jax.sharding import PartitionSpec as P

GRID = 8


EPSILON = 1e-05
GELU_SCALE = math.sqrt(2.0 / math.pi)
HIGHEST = lax.Precision.HIGHEST
MESH = pl.DeviceIdType.MESH
CONTRACT = (((0,), (0,)), ((), ()))
BACKWARD = (((1,), (1,)), ((), ()))


def padded_2(cells, sides, width):
    for axis, dim in sides:
        count = lax.axis_size(axis)
        ends = count - 1
        head = lax.slice_in_dim(cells, 0, width, axis=dim)
        tail = lax.slice_in_dim(cells, cells.shape[dim] - width, cells.shape[dim], axis=dim)
        cells = jnp.concatenate(
            [
                lax.ppermute(tail, axis, [(i, (i + 1) % count) for i in range(ends)]),
                cells,
                lax.ppermute(head, axis, [((i + 1) % count, i) for i in range(ends)]),
            ],
            axis=dim,
        )
    return cells


def gelu_slope(values):
    cubic = values * values * values
    bent = jnp.tanh(GELU_SCALE * (values + 0.044715 * cubic))
    result = 0.5 * values * (1.0 + bent)
    slope = 0.5 * (1.0 + bent) + 0.5 * values * (1.0 - bent * bent) * GELU_SCALE * (
        1.0 + 3.0 * 0.044715 * values * values
    )
    return (result, slope)


def layer_normalize(values):
    values = values.astype(jnp.float32)
    centred = values - jnp.mean(values, axis=-1, keepdims=True)
    inverse = lax.rsqrt(jnp.mean(centred * centred, axis=-1, keepdims=True) + EPSILON)
    return (centred * inverse, inverse)


def norm_backward_pass(normal_values, inverse, grads):
    grads = grads.astype(jnp.float32)
    return inverse * (
        grads
        - jnp.mean(grads, axis=-1, keepdims=True)
        - normal_values * jnp.mean(grads * normal_values, axis=-1, keepdims=True)
    )


def offset_table(side):
    places = jnp.arange(side * side, dtype=jnp.int32)
    place_row = places // side
    place_col = places % side
    offset_index = (
        (place_row[None, :] - place_row[:, None] + side - 1) * (2 * side - 1)
        + place_col[None, :]
        - place_col[:, None]
        + side
        - 1
    )
    table_slots = jnp.arange((2 * side - 1) ** 2, dtype=jnp.int32)
    return (table_slots[:, None] == offset_index.reshape(1, -1)).astype(jnp.float32)


def depthwise(padded, kernel):
    out_rows = padded.shape[1] - 2
    out_cols = padded.shape[2] - 2
    summed = jnp.zeros((padded.shape[0], out_rows, out_cols, padded.shape[3]), jnp.float32)
    for shift_row in range(3):
        for shift_col in range(3):
            window = padded[
                :, shift_row : shift_row + out_rows, shift_col : shift_col + out_cols, :
            ].astype(jnp.float32)
            summed = summed + window * kernel[shift_row, shift_col]
    return summed


def kernel_terms(padded, grads):
    out_rows = grads.shape[1]
    out_cols = grads.shape[2]
    grads_wide = grads.astype(jnp.float32)
    collected = []
    for shift_row in range(3):
        for shift_col in range(3):
            window = padded[
                :, shift_row : shift_row + out_rows, shift_col : shift_col + out_cols, :
            ].astype(jnp.float32)
            collected.append(jnp.sum(window * grads_wide, axis=(0, 1, 2)))
    return jnp.stack(collected).reshape(3, 3, -1)


AXES = ("row", "col")


def exchange_all(parts):
    return lax.all_to_all(parts, AXES, 0, 0, tiled=True)


def gather_sum(values, axis):
    count = lax.axis_size(axis)
    spread = jnp.broadcast_to(values, (count,) + values.shape)
    return jnp.sum(lax.all_to_all(spread, axis, 0, 0, tiled=True), axis=0)


def small_sum_kernel(rows, cols, x_ref, o_ref, row_buf, sum_buf, col_buf, sems):
    row = lax.axis_index("row")
    col = lax.axis_index("col")
    barrier = pltpu.get_barrier_semaphore()

    def row_peer(k):
        return lax.rem(row + k, rows)

    def col_peer(k):
        return lax.rem(col + k, cols)

    @pl.loop(1, rows)
    def _(k):
        pl.semaphore_signal(barrier, inc=1, device_id=(row_peer(k), col), device_id_type=MESH)

    @pl.loop(1, cols)
    def _(k):
        pl.semaphore_signal(barrier, inc=1, device_id=(row, col_peer(k)), device_id_type=MESH)

    row_buf[row] = x_ref[...]
    pl.semaphore_wait(barrier, rows + cols - 2)

    @pl.loop(1, rows)
    def _(k):
        pltpu.make_async_remote_copy(
            src_ref=x_ref,
            dst_ref=row_buf.at[row],
            send_sem=sems.at[0],
            recv_sem=sems.at[1],
            device_id=(row_peer(k), col),
            device_id_type=MESH,
        ).start()

    arrived = row_buf.at[pl.ds(0, rows - 1)]
    pltpu.make_async_copy(arrived, arrived, sems.at[1]).wait()
    total = row_buf[0]
    for k in range(1, rows):
        total = total + row_buf[k]
    sum_buf[...] = total
    col_buf[col] = total

    @pl.loop(1, cols)
    def _(k):
        pltpu.make_async_remote_copy(
            src_ref=sum_buf,
            dst_ref=col_buf.at[col],
            send_sem=sems.at[2],
            recv_sem=sems.at[3],
            device_id=(row, col_peer(k)),
            device_id_type=MESH,
        ).start()

    other = col_buf.at[pl.ds(0, cols - 1)]
    pltpu.make_async_copy(other, other, sems.at[3]).wait()
    total = col_buf[0]
    for k in range(1, cols):
        total = total + col_buf[k]
    o_ref[...] = total
    pltpu.make_async_copy(arrived, arrived, sems.at[0]).wait()
    pltpu.make_async_copy(other, other, sems.at[2]).wait()


def small_sum(values, number):
    rows = lax.axis_size("row")
    cols = lax.axis_size("col")
    shape = values.shape
    return pl.pallas_call(
        functools.partial(small_sum_kernel, rows, cols),
        out_shape=jax.ShapeDtypeStruct(shape, jnp.float32),
        in_specs=[pl.BlockSpec(memory_space=pltpu.VMEM)],
        out_specs=pl.BlockSpec(memory_space=pltpu.VMEM),
        scratch_shapes=[
            pltpu.VMEM((rows,) + shape, jnp.float32),
            pltpu.VMEM(shape, jnp.float32),
            pltpu.VMEM((cols,) + shape, jnp.float32),
            pltpu.SemaphoreType.DMA((4,)),
        ],
        compiler_params=pltpu.CompilerParams(collective_id=number, has_side_effects=True),
    )(values)


def swap_kernel(parity, side, cols, x_ref, o_ref, sems):
    row = lax.axis_index("row")
    col = lax.axis_index("col")
    kind = lax.rem(row, parity)
    count = side * cols
    me = (row // parity) * cols + col
    barrier = pltpu.get_barrier_semaphore()

    def place(k):
        peer = lax.rem(me + k, count)
        return peer, ((peer // cols) * parity + kind, lax.rem(peer, cols))

    @pl.loop(1, count)
    def _(k):
        pl.semaphore_signal(barrier, inc=1, device_id=place(k)[1], device_id_type=MESH)

    own = pltpu.make_async_copy(x_ref.at[me], o_ref.at[me], sems.at[2])
    own.start()
    pl.semaphore_wait(barrier, count - 1)

    @pl.loop(1, count)
    def _(k):
        peer, device = place(k)
        pltpu.make_async_remote_copy(
            src_ref=x_ref.at[peer],
            dst_ref=o_ref.at[me],
            send_sem=sems.at[0],
            recv_sem=sems.at[1],
            device_id=device,
            device_id_type=MESH,
        ).start()

    own.wait()
    sent = x_ref.at[pl.ds(0, count - 1)]
    pltpu.make_async_copy(sent, sent, sems.at[0]).wait()
    arrived = o_ref.at[pl.ds(0, count - 1)]
    pltpu.make_async_copy(arrived, arrived, sems.at[1]).wait()


def swap(parts, number):
    parity = lax.axis_size("row") // GRID
    return pl.pallas_call(
        functools.partial(swap_kernel, parity, GRID, lax.axis_size("col")),
        out_shape=jax.ShapeDtypeStruct(parts.shape, parts.dtype),
        in_specs=[pl.BlockSpec(memory_space=pltpu.VMEM)],
        out_specs=pl.BlockSpec(memory_space=pltpu.VMEM),
        scratch_shapes=[pltpu.SemaphoreType.DMA((3,))],
        compiler_params=pltpu.CompilerParams(collective_id=number, has_side_effects=True),
    )(parts)


def pack_tokens(tokens_in):
    channels = tokens_in.shape[-1]
    shaped = tokens_in.reshape(8, 2, 8, 4, 2, channels // 2)
    return shaped.transpose(0, 2, 4, 1, 3, 5).reshape(64, 16, channels // 2)


def unpack_tokens(blocks):
    half = blocks.shape[-1]
    shaped = blocks.reshape(8, 8, 2, 2, 4, half).transpose(0, 3, 1, 4, 2, 5)
    return shaped.reshape(16 * 32, 2 * half)


def split_sum(values):
    rows = lax.axis_size("row")
    parts = values.reshape(rows, -1, 128)
    own = jnp.sum(lax.all_to_all(parts, "row", 0, 0, tiled=True), axis=0)
    own = gather_sum(own.reshape(-1, 128), "col")
    spread = jnp.broadcast_to(own, (rows,) + own.shape)
    return lax.all_to_all(spread, "row", 0, 0, tiled=True)


def weight_grad(left_side, right_side):
    count = lax.axis_size("row") * lax.axis_size("col")
    partial = lax.dot_general(left_side, right_side, CONTRACT, preferred_element_type=jnp.float32)
    height, width = partial.shape
    parts = partial.astype(jnp.bfloat16).reshape(count, height // count, width)
    return jnp.sum(exchange_all(parts).astype(jnp.float32), axis=0)


HEAD_DIM = 32
QUAD = 4
PLACES = 64
GROUPS = 8


def attention_kernel(
    x_ref,
    wqkv_ref,
    wout_ref,
    bias_ref,
    ret_ref,
    normed_ref,
    proj_ref,
    context_ref,
    cot_ref,
    table_ref,
    spread,
    qkv,
    cgrad,
):
    channels = wout_ref.shape[0]
    factor = HEAD_DIM ** (-0.5)

    def gather(first_row, out_ref):
        for tile in range(2):
            block = x_ref[:, first_row : first_row + 16, tile * 128 : (tile + 1) * 128]
            spread[tile] = block.astype(jnp.float32).reshape(1024, 128)
        for group in range(GROUPS):
            for piece in range(4):
                half, tile = piece // 2, piece % 2
                rows = spread[tile, pl.ds(half * 8 + group, PLACES, stride=16), :]
                out_ref[group * PLACES : (group + 1) * PLACES, piece * 128 : (piece + 1) * 128] = (
                    rows.astype(jnp.bfloat16)
                )

    gather(0, normed_ref)
    gather(16, cot_ref)

    @pl.loop(0, 3 * channels // 256)
    def _(n):
        cols = pl.ds(pl.multiple_of(n * 256, 256), 256)
        qkv[:, cols] = jnp.dot(
            normed_ref[...], wqkv_ref[:, cols], preferred_element_type=jnp.float32
        ).astype(jnp.bfloat16)

    @pl.loop(0, channels // 256)
    def _(n):
        cols = pl.ds(pl.multiple_of(n * 256, 256), 256)
        cgrad[:, cols] = lax.dot_general(
            cot_ref[...], wout_ref[cols, :], BACKWARD, preferred_element_type=jnp.float32
        ).astype(jnp.bfloat16)

    table_ref[...] = jnp.zeros_like(table_ref)
    lane_head = lax.broadcasted_iota(jnp.int32, (PLACES, 128), 1) // HEAD_DIM
    masks = [(lane_head == h).astype(jnp.float32).astype(jnp.bfloat16) for h in range(QUAD)]
    masks_f = [(lane_head == h).astype(jnp.float32) for h in range(QUAD)]

    def widen(block):
        return jnp.concatenate([block * masks[h] for h in range(QUAD)], axis=0)

    def narrow(full):
        total = full[:PLACES] * masks_f[0]
        for h in range(1, QUAD):
            total = total + full[h * PLACES : (h + 1) * PLACES] * masks_f[h]
        return total

    @pl.loop(0, GROUPS)
    def _(group):
        rows = pl.ds(pl.multiple_of(group * PLACES, PLACES), PLACES)
        for quad in range(4):
            low = quad * 128
            queries = qkv[rows, low : low + 128]
            keys_in = qkv[rows, channels + low : channels + low + 128]
            values_in = qkv[rows, 2 * channels + low : 2 * channels + low + 128]
            grads = cgrad[rows, low : low + 128]
            queries_wide = widen(queries)
            grads_wide = widen(grads)
            scores = (
                lax.dot_general(keys_in, queries_wide, BACKWARD, preferred_element_type=jnp.float32)
                * factor
                + bias_ref[quad]
            )
            scores = jnp.exp(scores - jnp.max(scores, axis=0, keepdims=True))
            weights = scores * (1.0 / jnp.sum(scores, axis=0, keepdims=True))
            weights_b = weights.astype(jnp.bfloat16)
            context = narrow(
                lax.dot_general(weights_b, values_in, CONTRACT, preferred_element_type=jnp.float32)
            )
            context_ref[rows, low : low + 128] = context.astype(jnp.bfloat16)
            weights_grad = lax.dot_general(
                values_in, grads_wide, BACKWARD, preferred_element_type=jnp.float32
            )
            values_grad = jnp.dot(weights_b, grads_wide, preferred_element_type=jnp.float32)
            scores_grad = weights * (
                weights_grad - jnp.sum(weights * weights_grad, axis=0, keepdims=True)
            )
            table_ref[quad] += scores_grad
            scores_b = (scores_grad * factor).astype(jnp.bfloat16)
            queries_grad = narrow(
                lax.dot_general(scores_b, keys_in, CONTRACT, preferred_element_type=jnp.float32)
            )
            keys_grad = jnp.dot(scores_b, queries_wide, preferred_element_type=jnp.float32)
            proj_ref[rows, low : low + 128] = queries_grad.astype(jnp.bfloat16)
            proj_ref[rows, channels + low : channels + low + 128] = keys_grad.astype(jnp.bfloat16)
            proj_ref[rows, 2 * channels + low : 2 * channels + low + 128] = values_grad.astype(
                jnp.bfloat16
            )

    def scatter(read, first_row):
        for group in range(GROUPS):
            for piece in range(4):
                half, tile = piece // 2, piece % 2
                spread[tile, pl.ds(half * 8 + group, PLACES, stride=16), :] = read(group, piece)
        for tile in range(2):
            ret_ref[:, first_row : first_row + 16, tile * 128 : (tile + 1) * 128] = (
                spread[tile].reshape(64, 16, 128).astype(jnp.bfloat16)
            )

    def read_context(group, piece):
        return context_ref[
            group * PLACES : (group + 1) * PLACES, piece * 128 : (piece + 1) * 128
        ].astype(jnp.float32)

    scatter(read_context, 0)

    for n in range(channels // 256):
        grads = lax.dot_general(
            proj_ref[...],
            wqkv_ref[n * 256 : (n + 1) * 256, :],
            BACKWARD,
            preferred_element_type=jnp.float32,
        )
        for group in range(GROUPS):
            for tile in range(2):
                spread[tile, pl.ds(n * 8 + group, PLACES, stride=16), :] = grads[
                    group * PLACES : (group + 1) * PLACES, tile * 128 : (tile + 1) * 128
                ]
    for tile in range(2):
        ret_ref[:, 16:32, tile * 128 : (tile + 1) * 128] = (
            spread[tile].reshape(64, 16, 128).astype(jnp.bfloat16)
        )


def attention(blocks, w_qkv, w_out, bias):
    channels = w_out.shape[0]
    tokens = GROUPS * PLACES
    shapes = (
        jax.ShapeDtypeStruct(blocks.shape, jnp.bfloat16),
        jax.ShapeDtypeStruct((tokens, channels), jnp.bfloat16),
        jax.ShapeDtypeStruct((tokens, 3 * channels), jnp.bfloat16),
        jax.ShapeDtypeStruct((tokens, channels), jnp.bfloat16),
        jax.ShapeDtypeStruct((tokens, channels), jnp.bfloat16),
        jax.ShapeDtypeStruct(bias.shape, jnp.float32),
    )
    return pl.pallas_call(
        attention_kernel,
        out_shape=shapes,
        in_specs=[pl.BlockSpec(memory_space=pltpu.VMEM)] * 4,
        out_specs=[pl.BlockSpec(memory_space=pltpu.VMEM)] * 6,
        scratch_shapes=[
            pltpu.VMEM((2, 1024, 128), jnp.float32),
            pltpu.VMEM((tokens, 3 * channels), jnp.bfloat16),
            pltpu.VMEM((tokens, channels), jnp.bfloat16),
        ],
        compiler_params=pltpu.CompilerParams(vmem_limit_bytes=40 * 1024 * 1024),
    )(blocks, w_qkv, w_out, bias)


def on_device(
    inputs, out_grad, w_expand, dw_kernel, se_reduce, se_expand, w_project, w_qkv, w_out, pos_table
):
    images, tile_rows, tile_cols, channels = inputs.shape
    hidden_units = w_expand.shape[1]
    heads = pos_table.shape[0]
    places = GRID * GRID
    full_rows = tile_rows * lax.axis_size("row")
    full_cols = tile_cols * lax.axis_size("col")
    cells = full_rows * full_cols
    factor = (images * cells) ** (-0.5)
    tokens = images * tile_rows * tile_cols
    onehot = offset_table(GRID)
    bias = (
        jnp.dot(pos_table, onehot, precision=HIGHEST)
        .reshape(heads // QUAD, QUAD, places, places)
        .transpose(0, 2, 1, 3)
        .reshape(heads // QUAD, places, QUAD * places)
    )
    first_standardized, inverse_deviation_first = layer_normalize(inputs)
    first_normed_input = first_standardized.astype(jnp.bfloat16)
    pre_expand = jnp.dot(
        first_normed_input.reshape(tokens, channels), w_expand, preferred_element_type=jnp.float32
    )
    expanded_f, slope_expand = gelu_slope(
        pre_expand.reshape(images, tile_rows, tile_cols, hidden_units)
    )
    padded = padded_2(expanded_f.astype(jnp.bfloat16), (("row", 1), ("col", 2)), 1)
    pre_mix = depthwise(padded, dw_kernel)
    mixed, slope_mix = gelu_slope(pre_mix)
    pooled = small_sum(jnp.sum(mixed, axis=(1, 2)).reshape(-1, 128), 3).reshape(images, -1) / cells
    squeeze_pre = jnp.dot(pooled, se_reduce, precision=HIGHEST)
    squeeze_sig = jax.nn.sigmoid(squeeze_pre)
    squeezed = squeeze_pre * squeeze_sig
    gate = jax.nn.sigmoid(jnp.dot(squeezed, se_expand, precision=HIGHEST))
    scaled = (mixed * gate[:, None, None, :]).astype(jnp.bfloat16).reshape(tokens, hidden_units)
    middle_activation = inputs.astype(jnp.float32).reshape(tokens, channels) + jnp.dot(
        scaled, w_project, preferred_element_type=jnp.float32
    )
    second_standardized, inverse_deviation_second = layer_normalize(middle_activation)
    second_normed_input = second_standardized.astype(jnp.bfloat16)
    flattened_cotangent = out_grad.reshape(tokens, channels)
    outgoing = jnp.concatenate(
        [
            pack_tokens(second_normed_input.reshape(tile_rows, tile_cols, channels)),
            pack_tokens(out_grad.reshape(tile_rows, tile_cols, channels)),
        ],
        axis=1,
    )
    returned, grid_normed, grid_proj, grid_context, grid_cotangent, scores_sum = attention(
        swap(outgoing, 1), w_qkv, w_out, bias
    )
    table_part = lax.dot_general(
        scores_sum.reshape(heads // QUAD, places, QUAD, places)
        .transpose(0, 2, 1, 3)
        .reshape(heads, places * places),
        onehot,
        BACKWARD,
        precision=HIGHEST,
    )
    out_proj_grad = weight_grad(grid_context, grid_cotangent) * factor
    qkv_grad = weight_grad(grid_normed, grid_proj) * factor
    returned = swap(returned, 2)
    context_flat = unpack_tokens(returned[:, :16])
    second_normed_gradient = unpack_tokens(returned[:, 16:])
    block_out = (
        middle_activation + jnp.dot(context_flat, w_out, preferred_element_type=jnp.float32)
    ).astype(jnp.bfloat16)
    middle_gradient = flattened_cotangent.astype(jnp.float32) + norm_backward_pass(
        second_standardized, inverse_deviation_second, second_normed_gradient
    )
    middle_b = middle_gradient.astype(jnp.bfloat16)
    project_grad = weight_grad(scaled, middle_b) * factor
    scaled_grad = lax.dot_general(
        middle_b, w_project, BACKWARD, preferred_element_type=jnp.float32
    ).reshape(images, tile_rows, tile_cols, hidden_units)
    gate_grad = small_sum(jnp.sum(scaled_grad * mixed, axis=(1, 2)).reshape(-1, 128), 4).reshape(
        images, -1
    )
    excite_grad = gate_grad * gate * (1.0 - gate)
    squeezed_grad = lax.dot_general(excite_grad, se_expand, BACKWARD, precision=HIGHEST)
    squeeze_grad = squeezed_grad * squeeze_sig * (1.0 + squeeze_pre * (1.0 - squeeze_sig))
    pooled_grad = lax.dot_general(squeeze_grad, se_reduce, BACKWARD, precision=HIGHEST)
    se_reduce_grad = lax.dot_general(pooled, squeeze_grad, CONTRACT, precision=HIGHEST) * factor
    se_expand_grad = lax.dot_general(squeezed, excite_grad, CONTRACT, precision=HIGHEST) * factor
    premix_grad = (
        (scaled_grad * gate[:, None, None, :] + pooled_grad[:, None, None, :] / cells) * slope_mix
    ).astype(jnp.bfloat16)
    grad_padded = padded_2(premix_grad, (("row", 1), ("col", 2)), 1)
    kernel_part = kernel_terms(padded, premix_grad)
    expanded_grad = depthwise(grad_padded, dw_kernel[::-1, ::-1])
    preexp_grad = (expanded_grad * slope_expand).astype(jnp.bfloat16).reshape(tokens, hidden_units)
    expand_grad = weight_grad(first_normed_input.reshape(tokens, channels), preexp_grad) * factor
    first_normed_gradient = lax.dot_general(
        preexp_grad, w_expand, BACKWARD, preferred_element_type=jnp.float32
    ).reshape(images, tile_rows, tile_cols, channels)
    input_gradient = (
        middle_gradient.reshape(images, tile_rows, tile_cols, channels)
        + norm_backward_pass(first_standardized, inverse_deviation_first, first_normed_gradient)
    ).astype(jnp.bfloat16)
    small = jnp.concatenate([kernel_part.reshape(-1), table_part.reshape(-1)])
    unit = lax.axis_size("row") * 1024
    room = -small.shape[0] % unit
    small = split_sum(jnp.pad(small, (0, room))).reshape(-1)
    kernel_size = kernel_part.size
    kernel_sum = small[:kernel_size].reshape(kernel_part.shape)
    table_sum = small[kernel_size : kernel_size + table_part.size].reshape(table_part.shape)
    return (
        block_out.reshape(images, tile_rows, tile_cols, channels),
        input_gradient,
        expand_grad,
        project_grad,
        qkv_grad,
        out_proj_grad,
        kernel_sum * factor,
        se_reduce_grad,
        se_expand_grad,
        table_sum * factor,
    )


def solution(mesh):
    placed = (
        P(None, "row", "col", None),
        P(None, "row", "col", None),
        P(),
        P(),
        P(),
        P(),
        P(),
        P(),
        P(),
        P(),
    )
    return jax.shard_map(
        on_device,
        mesh=mesh,
        in_specs=placed,
        out_specs=(
            P(None, "row", "col", None),
            P(None, "row", "col", None),
            P(("row", "col"), None),
            P(("row", "col"), None),
            P(("row", "col"), None),
            P(("row", "col"), None),
            P(),
            P(),
            P(),
            P(),
        ),
        check_vma=False,
    )
```

profile of v0, /device:TPU:0, one launch (start us, length us, event | category | flops | bytes accessed | tf_op | source)
XLA Modules:
  0.0 384.8 jit_solution(1660211447171538400)
XLA Ops:
  4.6 3.0 fusion.70
  10.4 3.6 collective-permute-start
  16.7 4.1 %collective-permute-done.1 = bf16[1,1,32,2048]{3,2,1,0:T(8,128)(2,1)S(1)} collective-permute-done((bf16[1,1,32,2048]{3,2,1,0:T(8,128)(2,1)S(1)}, bf16[1,1,32,2048]{3,2,1,0:T(8,128)(2,1)S(1)}, u32[]{:S(2)}, u32[]{:S(2)}) %collective-permute-start.1) | collective-permute-done | bytes 131104 | tf_op jit(solution)/shard_map/ppermute | solution.py:32
  20.9 2.1 pad_maximum_fusion.12
  26.2 2.0 convolution_bitcast_fusion
  35.1 3.8 maximum_maximum_fusion
  38.9 8.0 %fusion.62 = (f32[2048]{0:T(1024)}, f32[1,16,32,2048]{3,2,1,0:T(8,128)}) fusion(f32[2048]{0:T(1024)S(1)} %bitcast.163, bf16[1,18,33,2048]{3,2,1,0:T(8,128)(2,1)S(1)} %get-tuple-element.45, f32[2048]{0:T(1024)S(1)} %bitcast.165, bf16[1,1,32,2048]{3,2,1,0:T(8,128)(2,1)S(1)} %collective-permute-done.1, bf16[1,16,32,2048]{3,2,1,0:T(8,128)(2,1)S(1)} %copy-done.16, ...), kind=kLoop, calls=%fused_computation.160 | loop fusion | flops 38795264 | bytes 19218432 | tf_op jit(solution)/shard_map/reduce_sum | solution.py:480
  47.0 20.7 %shard_map.177 = f32[16,128]{1,0:T(8,128)} custom-call(f32[16,128]{1,0:T(8,128)} %bitcast.180), custom_call_target="tpu_custom_call" | custom-call | tf_op jit(solution)/shard_map/pallas_call | solution.py:186
  69.0 2.4 fusion.60
  73.2 3.6 multiply_convert_fusion
  82.1 2.1 copy.55
  86.1 2.3 pad_maximum_fusion.6.x_ref
  88.4 22.2 %shard_map.178.x_ref = bf16[64,32,256]{2,1,0:T(8,128)(2,1)} custom-call(bf16[64,32,256]{2,1,0:T(8,128)(2,1)} %pad_maximum_fusion.6.x_ref), custom_call_target="tpu_custom_call" | custom-call | tf_op jit(solution)/shard_map/pallas_call | solution.py:242
  113.2 21.9 %shard_map.179 = (bf16[64,32,256]{2,1,0:T(8,128)(2,1)S(1)}, bf16[512,512]{1,0:T(8,128)(2,1)S(1)}, bf16[512,1536]{1,0:T(8,128)(2,1)S(1)}, bf16[512,512]{1,0:T(8,1...) custom-call(bf16[64,32,256]{2,1,0:T(8,128)(2,1)S(1)} %copy-done.2, ...), custom_call_target="tpu_custom_call" | custom-call | tf_op jit(solution)/shard_map/pallas_call | solution.py:436
  139.8 23.0 %shard_map.180 = bf16[64,32,256]{2,1,0:T(8,128)(2,1)} custom-call(bf16[64,32,256]{2,1,0:T(8,128)(2,1)} %copy-done.5), custom_call_target="tpu_custom_call" | custom-call | tf_op jit(solution)/shard_map/pallas_call | solution.py:242
  164.1 2.5 slice_convert_fusion
  170.1 2.8 fusion.40
  173.0 2.6 reshape.638
  179.6 4.1 %multiply_reduce_fusion = (f32[2048]{0:T(1024)}, f32[512,2048]{1,0:T(8,128)}) fusion(f32[1,16,32,2048]{3,2,1,0:T(8,128)S(1)} %copy-done.18, bf16[2048,512]{1,0:T(8,128)(2,1)S(1)} %copy-done, f32[512,512]{1,0:T(8,128)S(1)} %convert_add_fusion), kind=kOutput, calls=%fused_computation.67 | convolution fusion | flops 1084487680 | bytes 11542528 | tf_op jit(solution)/shard_map/dot_general | solution.py:523
  183.8 16.1 %shard_map.181 = f32[16,128]{1,0:T(8,128)} custom-call(f32[16,128]{1,0:T(8,128)} %bitcast.182), custom_call_target="tpu_custom_call" | custom-call | tf_op jit(solution)/shard_map/pallas_call | solution.py:186
  200.6 2.1 fusion.46
  202.7 2.2 fusion.55
  204.9 13.8 %fusion.39 = (f32[2048]{0:T(1024)S(1)}, f32[2048]{0:T(1024)S(1)}, f32[2048]{0:T(1024)S(1)}, f32[2048]{0:T(1024)S(1)}, f32[2048]{0:T(1024)S(1)}, /*index=5*/f32[2...) fusion(bf16[1,18,33,2048]{3,2,1,0:T(8,128)(2,1)} %copy-done.14, ...), kind=kLoop, calls=%fused_computation.63 | loop fusion | flops 53458944 | bytes 25518080 | tf_op jit(solution)/shard_map/reduce_sum | solution.py:103
  218.9 12.3 %all_to_all.35 = f32[16,16,128]{2,1,0:T(8,128)S(1)} all-to-all(f32[16,16,128]{2,1,0:T(8,128)S(1)} %bitcast.147), channel_id=1, replica_groups=mesh['row'=16,'col'=8] {'row'}, dimensions={0} | all-to-all | bytes 262144 | tf_op jit(solution)/shard_map/all_to_all | solution.py:267
  231.9 3.4 all-to-all-start.5
  237.0 3.9 %all-to-all-done.5 = f32[8,16,128]{2,1,0:T(8,128)S(1)} async-done(((f32[8,16,128]{2,1,0:T(8,128)}), f32[8,16,128]{2,1,0:T(8,128)S(1)}, u32[]{:S(2)}, u32[]{:S(2)}) %all-to-all-start.5) | async-done | bytes 65568 | tf_op jit(solution)/shard_map/all_to_all | solution.py:117
  241.5 3.5 all-to-all-start.6
  245.0 2.3 convolution_convert_fusion.2
  249.3 3.7 all-to-all-done.6
  253.0 4.8 %all-to-all-start.3 = ((bf16[128,4,512]{2,1,0:T(4,128)(2,1)}), bf16[128,4,512]{2,1,0:T(4,128)(2,1)S(1)}, u32[]{:S(2)}, u32[]{:S(2)}) async-start(bf16[128,4,512]{2,1,0:T(4,128)(2,1)} %reshape.627), calls=%async_computation.3 | async-start | bytes 1048576 | tf_op jit(solution)/shard_map/all_to_all | solution.py:111
  257.8 2.2 convolution_convert_fusion
  260.0 3.9 %reshape.626 = bf16[128,4,1536]{2,1,0:T(4,128)(2,1)} reshape(bf16[512,1536]{1,0:T(8,128)(2,1)} %convolution_convert_fusion) | data formatting | bytes 3145728 | tf_op jit(solution)/shard_map/reshape | solution.py:277
  263.9 3.0 collective-permute-start.4
  268.2 2.0 multiply_multiply_fusion.5
  271.5 10.5 %all-to-all-start.2 = ((bf16[128,4,1536]{2,1,0:T(4,128)(2,1)}), bf16[128,4,1536]{2,1,0:T(4,128)(2,1)}, u32[]{:S(2)}, u32[]{:S(2)}) async-start(bf16[128,4,1536]{2,1,0:T(4,128)(2,1)} %reshape.626), calls=%async_computation.2 | async-start | bytes 3145728 | tf_op jit(solution)/shard_map/all_to_all | solution.py:111
  283.2 4.6 %convolution_convert_fusion.1 = bf16[2048,512]{1,0:T(8,128)(2,1)} fusion(bf16[512,2048]{1,0:T(8,128)(2,1)} %bitcast.138, f32[512,512]{1,0:T(8,128)} %copy-done.25), kind=kOutput, calls=%fused_computation.75 | convolution fusion | flops 1075052544 | bytes 5242880 | tf_op jit(solution)/shard_map/dot_general | solution.py:275
  296.6 3.4 maximum_maximum_fusion.1
  300.1 6.5 %all-to-all-done.2 = bf16[128,4,1536]{2,1,0:T(4,128)(2,1)} async-done(((bf16[128,4,1536]{2,1,0:T(4,128)(2,1)}), bf16[128,4,1536]{2,1,0:T(4,128)(2,1)}, u32[]{:S(2)}, u32[]{:S(2)}) %all-to-all-start.2) | async-done | bytes 1572896 | tf_op jit(solution)/shard_map/all_to_all | solution.py:111
  306.6 8.8 %all-to-all-start.1 = ((bf16[128,16,512]{2,1,0:T(8,128)(2,1)}), bf16[128,16,512]{2,1,0:T(8,128)(2,1)}, u32[]{:S(2)}, u32[]{:S(2)}) async-start(bf16[128,16,512]{2,1,0:T(8,128)(2,1)} %bitcast.139), calls=%async_computation.1 | async-start | bytes 4194304 | tf_op jit(solution)/shard_map/all_to_all | solution.py:111
  315.5 11.3 %fusion.25 = bf16[1,16,32,2048]{3,2,1,0:T(8,128)(2,1)S(1)} fusion(f32[1,16,32,2048]{3,2,1,0:T(8,128)} %bitcast.127, bf16[1,16,32,2048]{3,2,1,0:T(8,128)(2,1)S(1)} %copy-done.19, bf16[1,18,33,2048]{3,2,1,0:T(8,128)(2,1)} %get-tuple-element.41, bf16[1,1,32,2048]{3,2,1,0:T(8,128)(2,1)S(1)} %collective-permute-done.5, ...), kind=kLoop, calls=%fused_computation.49 | loop fusion | flops 49283072 | bytes 21307392 | tf_op jit(solution)/shard_map/convert_element_type | solution.py:541
  328.3 4.5 %bitcast_convert_fusion = bf16[512,2048]{1,0:T(8,128)(2,1)} fusion(bf16[1,16,32,2048]{3,2,1,0:T(8,128)(2,1)} %copy-done.27, bf16[1,16,32,512]{3,2,1,0:T(8,128)(2,1)S(1)} %copy-done.36), kind=kOutput, calls=%fused_computation.64 | convolution fusion | flops 1074790400 | bytes 4718592 | tf_op jit(solution)/shard_map/dot_general | solution.py:275
  332.8 4.2 %reshape.624 = bf16[128,4,2048]{2,1,0:T(4,128)(2,1)} reshape(bf16[512,2048]{1,0:T(8,128)(2,1)} %bitcast_convert_fusion) | data formatting | bytes 4194304 | tf_op jit(solution)/shard_map/reshape | solution.py:277
  337.3 8.1 %all-to-all-done.1 = bf16[128,16,512]{2,1,0:T(8,128)(2,1)} async-done(((bf16[128,16,512]{2,1,0:T(8,128)(2,1)}), bf16[128,16,512]{2,1,0:T(8,128)(2,1)}, u32[]{:S(2)}, u32[]{:S(2)}) %all-to-all-start.1) | async-done | bytes 2097184 | tf_op jit(solution)/shard_map/all_to_all | solution.py:111
  345.4 6.0 %all-to-all-start = ((bf16[128,4,2048]{2,1,0:T(4,128)(2,1)}), bf16[128,4,2048]{2,1,0:T(4,128)(2,1)}, u32[]{:S(2)}, u32[]{:S(2)}) async-start(bf16[128,4,2048]{2,1,0:T(4,128)(2,1)} %reshape.624), calls=%async_computation | async-start | bytes 4194304 | tf_op jit(solution)/shard_map/all_to_all | solution.py:111
  351.5 2.9 add_convert_fusion
  356.6 2.1 convert_reduce_fusion.2
  361.9 19.6 %all-to-all-done = bf16[128,4,2048]{2,1,0:T(4,128)(2,1)} async-done(((bf16[128,4,2048]{2,1,0:T(4,128)(2,1)}), bf16[128,4,2048]{2,1,0:T(4,128)(2,1)}, u32[]{:S(2)}, u32[]{:S(2)}) %all-to-all-start) | async-done | bytes 2097184 | tf_op jit(solution)/shard_map/all_to_all | solution.py:111
  381.5 2.5 convert_reduce_fusion.1
  (215 shorter events, 72.0 us)
Async XLA Ops:
  0.6 76.2 %copy-start = (bf16[2048,512]{1,0:T(8,128)(2,1)S(1)}, bf16[2048,512]{1,0:T(8,128)(2,1)}, u32[]{:S(2)}) copy-start(bf16[2048,512]{1,0:T(8,128)(2,1)} %param.16) | copy-start | bytes 6291460
  7.7 18.5 %copy-start.62 = (f32[16,225]{1,0:T(8,128)S(1)}, f32[16,225]{1,0:T(8,128)}, u32[]{:S(2)}) copy-start(f32[16,225]{1,0:T(8,128)} %param.19) | copy-start | bytes 43204
  10.3 21.6 %copy-start.28 = (bf16[1,16,32,512]{3,2,1,0:T(8,128)(2,1)S(1)}, bf16[1,16,32,512]{3,2,1,0:T(8,128)(2,1)}, u32[]{:S(2)}) copy-start(bf16[1,16,32,512]{3,2,1,0:T(8,128)(2,1)} %param.11) | copy-start | bytes 1572868
  10.4 6.4 %collective-permute-start = (bf16[1,1,32,2048]{3,2,1,0:T(8,128)(2,1)S(1)}, bf16[1,1,32,2048]{3,2,1,0:T(8,128)(2,1)S(1)}, u32[]{:S(2)}, u32[]{:S(2)}) collective-permute-start(bf16[1,1,32,2048]{3,2,1,0:T(8,128)(2,1)S(1)} %get-tuple-element.50), channel_id=1, source_target_pairs={{0,8},{8,16},{16,24},{24,32},{32,40},{40,48},{48,56},{56,64},{64,7... | collective-permute-start | bytes 393224 | tf_op jit(solution)/shard_map/ppermute | solution.py:30
  14.0 6.9 %collective-permute-start.1 = (bf16[1,1,32,2048]{3,2,1,0:T(8,128)(2,1)S(1)}, bf16[1,1,32,2048]{3,2,1,0:T(8,128)(2,1)S(1)}, u32[]{:S(2)}, u32[]{:S(2)}) collective-permute-start(bf16[1,1,32,2048]{3,2,1,0:T(8,128)(2,1)S(1)} %get-tuple-element.51), channel_id=1, source_target_pairs={{8,0},{16,8},{24,16},{32,24},{40,32},{48,40},{56,48},{64,56},{72,6... | collective-permute-start | bytes 393224 | tf_op jit(solution)/shard_map/ppermute | solution.py:32
  15.4 23.5 %copy-start.37 = (f32[1,1,2048]{2,1,0:T(1,128)}, f32[1,1,2048]{2,1,0:T(1,128)S(1)}, u32[]{:S(2)}) copy-start(f32[1,1,2048]{2,1,0:T(1,128)S(1)} %get-tuple-element.54) | copy-start | bytes 24580
  15.4 23.5 %copy-start.39 = (f32[1,1,2048]{2,1,0:T(1,128)}, f32[1,1,2048]{2,1,0:T(1,128)S(1)}, u32[]{:S(2)}) copy-start(f32[1,1,2048]{2,1,0:T(1,128)S(1)} %get-tuple-element.55) | copy-start | bytes 24580
  15.4 23.5 %copy-start.41 = (f32[1,1,2048]{2,1,0:T(1,128)}, f32[1,1,2048]{2,1,0:T(1,128)S(1)}, u32[]{:S(2)}) copy-start(f32[1,1,2048]{2,1,0:T(1,128)S(1)} %get-tuple-element.56) | copy-start | bytes 24580
  15.4 23.5 %copy-start.43 = (f32[1,1,2048]{2,1,0:T(1,128)}, f32[1,1,2048]{2,1,0:T(1,128)S(1)}, u32[]{:S(2)}) copy-start(f32[1,1,2048]{2,1,0:T(1,128)S(1)} %get-tuple-element.57) | copy-start | bytes 24580
  15.4 23.5 %copy-start.45 = (f32[1,1,2048]{2,1,0:T(1,128)}, f32[1,1,2048]{2,1,0:T(1,128)S(1)}, u32[]{:S(2)}) copy-start(f32[1,1,2048]{2,1,0:T(1,128)S(1)} %get-tuple-element.58) | copy-start | bytes 24580
  15.4 23.5 %copy-start.47 = (f32[1,1,2048]{2,1,0:T(1,128)}, f32[1,1,2048]{2,1,0:T(1,128)S(1)}, u32[]{:S(2)}) copy-start(f32[1,1,2048]{2,1,0:T(1,128)S(1)} %get-tuple-element.59) | copy-start | bytes 24580
  15.4 23.5 %copy-start.49 = (f32[1,1,2048]{2,1,0:T(1,128)}, f32[1,1,2048]{2,1,0:T(1,128)S(1)}, u32[]{:S(2)}) copy-start(f32[1,1,2048]{2,1,0:T(1,128)S(1)} %get-tuple-element.60) | copy-start | bytes 24580
  15.4 23.5 %copy-start.51 = (f32[1,1,2048]{2,1,0:T(1,128)}, f32[1,1,2048]{2,1,0:T(1,128)S(1)}, u32[]{:S(2)}) copy-start(f32[1,1,2048]{2,1,0:T(1,128)S(1)} %get-tuple-element.61) | copy-start | bytes 24580
  15.5 23.5 %copy-start.53 = (f32[1,1,2048]{2,1,0:T(1,128)}, f32[1,1,2048]{2,1,0:T(1,128)S(1)}, u32[]{:S(2)}) copy-start(f32[1,1,2048]{2,1,0:T(1,128)S(1)} %get-tuple-element.62) | copy-start | bytes 24580
  23.0 12.1 %collective-permute-start.2 = (bf16[1,18,1,2048]{3,2,1,0:T(2,128)(2,1)}, bf16[1,18,1,2048]{3,2,1,0:T(2,128)(2,1)}, u32[]{:S(2)}, u32[]{:S(2)}) collective-permute-start(bf16[1,18,1,2048]{3,2,1,0:T(2,128)(2,1)} %get-tuple-element.46), channel_id=1, source_target_pairs={{0,1},{1,2},{2,3},{3,4},{4,5},{5,6},{6,7},{8,9},{9,10},{10,11},{11... | collective-permute-start | bytes 221192 | tf_op jit(solution)/shard_map/ppermute | solution.py:30
  24.9 10.1 %collective-permute-start.3 = (bf16[1,18,1,2048]{3,2,1,0:T(2,128)(2,1)}, bf16[1,18,1,2048]{3,2,1,0:T(2,128)(2,1)}, u32[]{:S(2)}, u32[]{:S(2)}) collective-permute-start(bf16[1,18,1,2048]{3,2,1,0:T(2,128)(2,1)} %get-tuple-element.47), channel_id=1, source_target_pairs={{1,0},{2,1},{3,2},{4,3},{5,4},{6,5},{7,6},{9,8},{10,9},{11,10},{12... | collective-permute-start | bytes 221192 | tf_op jit(solution)/shard_map/ppermute | solution.py:32
  79.2 31.4 %copy-start.3 = (bf16[512,512]{1,0:T(8,128)(2,1)S(1)}, bf16[512,512]{1,0:T(8,128)(2,1)}, u32[]{:S(2)}) copy-start(bf16[512,512]{1,0:T(8,128)(2,1)} %wout_ref.1) | copy-start | bytes 1572868
  179.6 20.9 %copy-start.59 = (f32[128]{0:T(128)S(1)}, f32[128]{0:T(128)}, u32[]{:S(2)}) copy-start(f32[128]{0:T(128)} %copy-done.58) | copy-start | bytes 1540
  200.6 18.2 %copy-start.55 = (f32[2048]{0:T(1024)}, f32[2048]{0:T(1024)S(1)}, u32[]{:S(2)}) copy-start(f32[2048]{0:T(1024)S(1)} %fusion.54) | copy-start | bytes 24580
  204.9 40.1 %copy-start.11 = (bf16[512,512]{1,0:T(8,128)(2,1)S(1)}, bf16[512,512]{1,0:T(8,128)(2,1)}, u32[]{:S(2)}) copy-start(bf16[512,512]{1,0:T(8,128)(2,1)} %copy-done.10) | copy-start | bytes 1572868
  218.7 39.1 %copy-start.7 = (bf16[512,1536]{1,0:T(8,128)(2,1)S(1)}, bf16[512,1536]{1,0:T(8,128)(2,1)}, u32[]{:S(2)}) copy-start(bf16[512,1536]{1,0:T(8,128)(2,1)} %copy-done.6) | copy-start | bytes 4718596
  218.7 39.1 %copy-start.9 = (bf16[512,512]{1,0:T(8,128)(2,1)S(1)}, bf16[512,512]{1,0:T(8,128)(2,1)}, u32[]{:S(2)}) copy-start(bf16[512,512]{1,0:T(8,128)(2,1)} %copy-done.8) | copy-start | bytes 1572868
  231.9 8.9 %all-to-all-start.5 = ((f32[8,16,128]{2,1,0:T(8,128)}), f32[8,16,128]{2,1,0:T(8,128)S(1)}, u32[]{:S(2)}, u32[]{:S(2)}) async-start(f32[8,16,128]{2,1,0:T(8,128)} %broadcast_in_dim.4), calls=%async_computation.5 | async-start | bytes 131072 | tf_op jit(solution)/shard_map/all_to_all | solution.py:117
  241.5 11.5 %all-to-all-start.6 = ((f32[16,16,128]{2,1,0:T(8,128)}), f32[16,16,128]{2,1,0:T(8,128)S(1)}, u32[]{:S(2)}, u32[]{:S(2)}) async-start(f32[16,16,128]{2,1,0:T(8,128)} %broadcast_in_dim.5), calls=%async_computation.6 | async-start | bytes 262144 | tf_op jit(solution)/shard_map/all_to_all | solution.py:270
  253.0 18.6 %all-to-all-start.3 = ((bf16[128,4,512]{2,1,0:T(4,128)(2,1)}), bf16[128,4,512]{2,1,0:T(4,128)(2,1)S(1)}, u32[]{:S(2)}, u32[]{:S(2)}) async-start(bf16[128,4,512]{2,1,0:T(4,128)(2,1)} %reshape.627), calls=%async_computation.3 | async-start | bytes 1048576 | tf_op jit(solution)/shard_map/all_to_all | solution.py:111
  260.0 22.1 %copy-start.56 = (f32[2048]{0:T(1024)S(1)}, f32[2048]{0:T(1024)}, u32[]{:S(2)}) copy-start(f32[2048]{0:T(1024)} %copy-done.55) | copy-start | bytes 24580
  260.0 22.1 %copy-start.61 = (f32[128]{0:T(128)S(1)}, f32[128]{0:T(128)}, u32[]{:S(2)}) copy-start(f32[128]{0:T(128)} %get-tuple-element.71) | copy-start | bytes 1540
  263.9 26.6 %collective-permute-start.4 = (bf16[1,1,32,2048]{3,2,1,0:T(8,128)(2,1)}, bf16[1,1,32,2048]{3,2,1,0:T(8,128)(2,1)S(1)}, u32[]{:S(2)}, u32[]{:S(2)}) collective-permute-start(bf16[1,1,32,2048]{3,2,1,0:T(8,128)(2,1)} %get-tuple-element.48), channel_id=1, source_target_pairs={{0,8},{8,16},{16,24},{24,32},{32,40},{40,48},{48,56},{56,64},{64,7... | collective-permute-start | bytes 393224 | tf_op jit(solution)/shard_map/ppermute | solution.py:30
  266.9 23.6 %collective-permute-start.5 = (bf16[1,1,32,2048]{3,2,1,0:T(8,128)(2,1)}, bf16[1,1,32,2048]{3,2,1,0:T(8,128)(2,1)S(1)}, u32[]{:S(2)}, u32[]{:S(2)}) collective-permute-start(bf16[1,1,32,2048]{3,2,1,0:T(8,128)(2,1)} %get-tuple-element.49), channel_id=1, source_target_pairs={{8,0},{16,8},{24,16},{32,24},{40,32},{48,40},{56,48},{64,56},{72,6... | collective-permute-start | bytes 393224 | tf_op jit(solution)/shard_map/ppermute | solution.py:32
  271.5 10.6 %copy-start.33 = (bf16[128,4,512]{2,1,0:T(4,128)(2,1)}, bf16[128,4,512]{2,1,0:T(4,128)(2,1)S(1)}, u32[]{:S(2)}) copy-start(bf16[128,4,512]{2,1,0:T(4,128)(2,1)S(1)} %all-to-all-done.3) | copy-start | bytes 1572868
  271.5 35.0 %all-to-all-start.2 = ((bf16[128,4,1536]{2,1,0:T(4,128)(2,1)}), bf16[128,4,1536]{2,1,0:T(4,128)(2,1)}, u32[]{:S(2)}, u32[]{:S(2)}) async-start(bf16[128,4,1536]{2,1,0:T(4,128)(2,1)} %reshape.626), calls=%async_computation.2 | async-start | bytes 3145728 | tf_op jit(solution)/shard_map/all_to_all | solution.py:111
  290.8 3.9 %collective-permute-start.6 = (bf16[1,18,1,2048]{3,2,1,0:T(2,128)(2,1)S(1)}, bf16[1,18,1,2048]{3,2,1,0:T(2,128)(2,1)S(1)}, u32[]{:S(2)}, u32[]{:S(2)}) collective-permute-start(bf16[1,18,1,2048]{3,2,1,0:T(2,128)(2,1)S(1)} %get-tuple-element.42), channel_id=1, source_target_pairs={{0,1},{1,2},{2,3},{3,4},{4,5},{5,6},{6,7},{8,9},{9,10},{10,11},{11... | collective-permute-start | bytes 221192 | tf_op jit(solution)/shard_map/ppermute | solution.py:30
  292.1 4.5 %collective-permute-start.7 = (bf16[1,18,1,2048]{3,2,1,0:T(2,128)(2,1)S(1)}, bf16[1,18,1,2048]{3,2,1,0:T(2,128)(2,1)S(1)}, u32[]{:S(2)}, u32[]{:S(2)}) collective-permute-start(bf16[1,18,1,2048]{3,2,1,0:T(2,128)(2,1)S(1)} %get-tuple-element.43), channel_id=1, source_target_pairs={{1,0},{2,1},{3,2},{4,3},{5,4},{6,5},{7,6},{9,8},{10,9},{11,10},{12... | collective-permute-start | bytes 221192 | tf_op jit(solution)/shard_map/ppermute | solution.py:32
  300.0 15.4 %copy-start.38 = (f32[1,1,2048]{2,1,0:T(1,128)S(1)}, f32[1,1,2048]{2,1,0:T(1,128)}, u32[]{:S(2)}) copy-start(f32[1,1,2048]{2,1,0:T(1,128)} %copy-done.37) | copy-start | bytes 24580
  300.0 15.4 %copy-start.40 = (f32[1,1,2048]{2,1,0:T(1,128)S(1)}, f32[1,1,2048]{2,1,0:T(1,128)}, u32[]{:S(2)}) copy-start(f32[1,1,2048]{2,1,0:T(1,128)} %copy-done.39) | copy-start | bytes 24580
  300.0 15.5 %copy-start.42 = (f32[1,1,2048]{2,1,0:T(1,128)S(1)}, f32[1,1,2048]{2,1,0:T(1,128)}, u32[]{:S(2)}) copy-start(f32[1,1,2048]{2,1,0:T(1,128)} %copy-done.41) | copy-start | bytes 24580
  300.0 15.5 %copy-start.44 = (f32[1,1,2048]{2,1,0:T(1,128)S(1)}, f32[1,1,2048]{2,1,0:T(1,128)}, u32[]{:S(2)}) copy-start(f32[1,1,2048]{2,1,0:T(1,128)} %copy-done.43) | copy-start | bytes 24580
  300.0 15.5 %copy-start.46 = (f32[1,1,2048]{2,1,0:T(1,128)S(1)}, f32[1,1,2048]{2,1,0:T(1,128)}, u32[]{:S(2)}) copy-start(f32[1,1,2048]{2,1,0:T(1,128)} %copy-done.45) | copy-start | bytes 24580
  300.0 15.5 %copy-start.48 = (f32[1,1,2048]{2,1,0:T(1,128)S(1)}, f32[1,1,2048]{2,1,0:T(1,128)}, u32[]{:S(2)}) copy-start(f32[1,1,2048]{2,1,0:T(1,128)} %copy-done.47) | copy-start | bytes 24580
  300.0 15.5 %copy-start.50 = (f32[1,1,2048]{2,1,0:T(1,128)S(1)}, f32[1,1,2048]{2,1,0:T(1,128)}, u32[]{:S(2)}) copy-start(f32[1,1,2048]{2,1,0:T(1,128)} %copy-done.49) | copy-start | bytes 24580
  300.0 15.5 %copy-start.52 = (f32[1,1,2048]{2,1,0:T(1,128)S(1)}, f32[1,1,2048]{2,1,0:T(1,128)}, u32[]{:S(2)}) copy-start(f32[1,1,2048]{2,1,0:T(1,128)} %copy-done.51) | copy-start | bytes 24580
  300.0 15.5 %copy-start.54 = (f32[1,1,2048]{2,1,0:T(1,128)S(1)}, f32[1,1,2048]{2,1,0:T(1,128)}, u32[]{:S(2)}) copy-start(f32[1,1,2048]{2,1,0:T(1,128)} %copy-done.53) | copy-start | bytes 24580
  306.6 38.8 %all-to-all-start.1 = ((bf16[128,16,512]{2,1,0:T(8,128)(2,1)}), bf16[128,16,512]{2,1,0:T(8,128)(2,1)}, u32[]{:S(2)}, u32[]{:S(2)}) async-start(bf16[128,16,512]{2,1,0:T(8,128)(2,1)} %bitcast.139), calls=%async_computation.1 | async-start | bytes 4194304 | tf_op jit(solution)/shard_map/all_to_all | solution.py:111
  315.5 11.3 %copy-start.31 = (bf16[512,2048]{1,0:T(8,128)(2,1)S(1)}, bf16[512,2048]{1,0:T(8,128)(2,1)}, u32[]{:S(2)}) copy-start(bf16[512,2048]{1,0:T(8,128)(2,1)} %param.12) | copy-start | bytes 6291460
  328.2 8.8 %copy-start.26 = (f32[512,512]{1,0:T(8,128)}, f32[512,512]{1,0:T(8,128)S(1)}, u32[]{:S(2)}) copy-start(f32[512,512]{1,0:T(8,128)S(1)} %get-tuple-element.70) | copy-start | bytes 3145732
  337.3 18.4 %copy-start.34 = (bf16[128,4,512]{2,1,0:T(4,128)(2,1)S(1)}, bf16[128,4,512]{2,1,0:T(4,128)(2,1)}, u32[]{:S(2)}) copy-start(bf16[128,4,512]{2,1,0:T(4,128)(2,1)} %copy-done.33) | copy-start | bytes 1572868
  345.4 36.0 %all-to-all-start = ((bf16[128,4,2048]{2,1,0:T(4,128)(2,1)}), bf16[128,4,2048]{2,1,0:T(4,128)(2,1)}, u32[]{:S(2)}, u32[]{:S(2)}) async-start(bf16[128,4,2048]{2,1,0:T(4,128)(2,1)} %reshape.624), calls=%async_computation | async-start | bytes 4194304 | tf_op jit(solution)/shard_map/all_to_all | solution.py:111
  351.5 33.1 %copy-start.1 = (bf16[2048,512]{1,0:T(8,128)(2,1)S(1)}, bf16[2048,512]{1,0:T(8,128)(2,1)}, u32[]{:S(2)}) copy-start(bf16[2048,512]{1,0:T(8,128)(2,1)} %param.16) | copy-start | bytes 6291460
  (29 other events, 98.5 us)
where the time goes:
time: 392 us; the launch traced here: 385 us
  Pallas kernels  104 us (27%)
  other arithmetic  77.3 us (20%)
  starting transfers between devices  52.1 us (13%)
  waiting for transfers between devices  50.3 us (13%)
  local copies, waits for them, and re-layouts  49.1 us (13%)
  matrix products  38 us (10%)
  blocking collectives  12.3 us (3%)
    pallas_call x2, Pallas kernels, swap(): pl.pallas_call(functools.partial(swap_kernel, parity, GRID, lax.axis_size...  45.2 us
    pallas_call x2, Pallas kernels, small_sum(): pl.pallas_call(functools.partial(small_sum_kernel, rows, cols), out_shape...  36.7 us
    all_to_all x4, waiting for transfers between devices, exchange_all(): return lax.all_to_all(parts, AXES, 0, 0, tiled=True)  35.6 us
    all_to_all x4, starting transfers between devices, exchange_all(): return lax.all_to_all(parts, AXES, 0, 0, tiled=True)  30.2 us
    pallas_call x1, Pallas kernels, attention(): pl.pallas_call(attention_kernel, out_shape=shapes, in_specs=[pl.BlockSpec...  21.9 us
    reduce_sum x1, other arithmetic, kernel_terms(): collected.append(jnp.sum(window * grads_wide, axis=(0, 1, 2)))  13.8 us
    dot_general x4, matrix products, weight_grad(): lax.dot_general(left_side, right_side, CONTRACT, preferred_element_type=j...  13.5 us
    all_to_all x1, blocking collectives, split_sum(): own = jnp.sum(lax.all_to_all(parts, 'row', 0, 0, tiled=True), axis=0)  12.3 us
  transfers between devices with their start and end apart: 14, of which 9 were waited for; matrix products, arithmetic and copies ran while one was open for 18% of the time, Pallas kernels for 0%

commit v1 on v0

--- a/solution.py
+++ b/solution.py
@@ -17,23 +17,6 @@
 MESH = pl.DeviceIdType.MESH
 CONTRACT = (((0,), (0,)), ((), ()))
 BACKWARD = (((1,), (1,)), ((), ()))
-
-
-def padded_2(cells, sides, width):
-    for axis, dim in sides:
-        count = lax.axis_size(axis)
-        ends = count - 1
-        head = lax.slice_in_dim(cells, 0, width, axis=dim)
-        tail = lax.slice_in_dim(cells, cells.shape[dim] - width, cells.shape[dim], axis=dim)
-        cells = jnp.concatenate(
-            [
-                lax.ppermute(tail, axis, [(i, (i + 1) % count) for i in range(ends)]),
-                cells,
-                lax.ppermute(head, axis, [((i + 1) % count, i) for i in range(ends)]),
-            ],
-            axis=dim,
-        )
-    return cells
 
 
 def gelu_slope(values):
@@ -77,44 +60,223 @@
     return (table_slots[:, None] == offset_index.reshape(1, -1)).astype(jnp.float32)
 
 
-def depthwise(padded, kernel):
-    out_rows = padded.shape[1] - 2
-    out_cols = padded.shape[2] - 2
-    summed = jnp.zeros((padded.shape[0], out_rows, out_cols, padded.shape[3]), jnp.float32)
-    for shift_row in range(3):
-        for shift_col in range(3):
-            window = padded[
-                :, shift_row : shift_row + out_rows, shift_col : shift_col + out_cols, :
-            ].astype(jnp.float32)
-            summed = summed + window * kernel[shift_row, shift_col]
-    return summed
-
-
-def kernel_terms(padded, grads):
-    out_rows = grads.shape[1]
-    out_cols = grads.shape[2]
-    grads_wide = grads.astype(jnp.float32)
-    collected = []
-    for shift_row in range(3):
-        for shift_col in range(3):
-            window = padded[
-                :, shift_row : shift_row + out_rows, shift_col : shift_col + out_cols, :
-            ].astype(jnp.float32)
-            collected.append(jnp.sum(window * grads_wide, axis=(0, 1, 2)))
-    return jnp.stack(collected).reshape(3, 3, -1)
-
-
 AXES = ("row", "col")
 
 
-def exchange_all(parts):
-    return lax.all_to_all(parts, AXES, 0, 0, tiled=True)
-
-
-def gather_sum(values, axis):
-    count = lax.axis_size(axis)
-    spread = jnp.broadcast_to(values, (count,) + values.shape)
-    return jnp.sum(lax.all_to_all(spread, axis, 0, 0, tiled=True), axis=0)
+def halo_kernel(rows, cols, height, width, top_ref, down_ref, left_ref, right_ref, o_ref, sems):
+    row = lax.axis_index("row")
+    col = lax.axis_index("col")
+    barrier = pltpu.get_barrier_semaphore()
+    up, down = lax.rem(row + rows - 1, rows), lax.rem(row + 1, rows)
+    left, right = lax.rem(col + cols - 1, cols), lax.rem(col + 1, cols)
+    last = width - 16
+    sends = (
+        (down_ref, 0, width, (down, col)),
+        (top_ref, width, width, (up, col)),
+        (right_ref, 2 * width, height, (row, right)),
+        (left_ref, 2 * width + height, height, (row, left)),
+        (down_ref.at[pl.ds(last, 16)], 2 * (width + height), 16, (down, right)),
+        (down_ref.at[pl.ds(0, 16)], 2 * (width + height) + 16, 16, (down, left)),
+        (top_ref.at[pl.ds(last, 16)], 2 * (width + height) + 32, 16, (up, right)),
+        (top_ref.at[pl.ds(0, 16)], 2 * (width + height) + 48, 16, (up, left)),
+    )
+    for _, _, _, device in sends:
+        pl.semaphore_signal(barrier, inc=1, device_id=device, device_id_type=MESH)
+    pl.semaphore_wait(barrier, len(sends))
+    copies = []
+    for number, (source, start, size, device) in enumerate(sends):
+        copies.append(
+            pltpu.make_async_remote_copy(
+                src_ref=source,
+                dst_ref=o_ref.at[pl.ds(start, size)],
+                send_sem=sems.at[0, number],
+                recv_sem=sems.at[1, number],
+                device_id=device,
+                device_id_type=MESH,
+            )
+        )
+        copies[-1].start()
+    for copy in copies:
+        copy.wait()
+
+
+def halo(cells, number):
+    height, width, features = cells.shape
+    rows, cols = lax.axis_size("row"), lax.axis_size("col")
+    total = 2 * (width + height) + 64
+
+    def body(*refs):
+        halo_kernel(rows, cols, height, width, *refs)
+
+    return pl.pallas_call(
+        body,
+        out_shape=jax.ShapeDtypeStruct((total, features), cells.dtype),
+        in_specs=[pl.BlockSpec(memory_space=pltpu.VMEM)] * 4,
+        out_specs=pl.BlockSpec(memory_space=pltpu.VMEM),
+        scratch_shapes=[pltpu.SemaphoreType.DMA((2, 8))],
+        compiler_params=pltpu.CompilerParams(collective_id=number, has_side_effects=True),
+    )(cells[0], cells[-1], cells[:, 0], cells[:, -1])
+
+
+def reduce_kernel(rows, cols, w_ref, s_ref, o_ref, so_ref, half, got, rs_buf, own_buf, col_buf, sems):
+    row = lax.axis_index("row")
+    col = lax.axis_index("col")
+    depth = cols // 2
+    core = lax.rem(col, 2)
+    count = rows * depth
+    me = row * depth + col // 2
+    steps = 4
+    span = count // steps
+    barrier = pltpu.get_barrier_semaphore()
+    pair = (row, col - core + (1 - core))
+
+    def place(k):
+        peer = lax.rem(me + k, count)
+        return peer, (peer // depth, lax.rem(peer, depth) * 2 + core)
+
+    def signal(device):
+        pl.semaphore_signal(barrier, inc=1, device_id=device, device_id_type=MESH)
+
+    def wait_like(ref, sem):
+        pltpu.make_async_copy(ref, ref, sem).wait()
+
+    @pl.loop(1, count)
+    def _(k):
+        signal(place(k)[1])
+
+    @pl.loop(0, depth)
+    def _(k):
+        signal((row, lax.rem(col // 2 + k, depth) * 2 + (1 - core)))
+
+    rs_buf[row] = s_ref[row]
+    pl.semaphore_wait(barrier, count - 1 + depth)
+
+    for step in range(steps):
+
+        @pl.loop(step * span, (step + 1) * span)
+        def _(k):
+            peer = lax.rem(me + k, count)
+            pltpu.make_async_remote_copy(
+                src_ref=w_ref.at[peer, 1 - core],
+                dst_ref=half.at[step, k - step * span],
+                send_sem=sems.at[0],
+                recv_sem=sems.at[1 + step],
+                device_id=pair,
+                device_id_type=MESH,
+            ).start()
+
+    @pl.loop(1, rows)
+    def _(k):
+        other = lax.rem(row + k, rows)
+        pltpu.make_async_remote_copy(
+            src_ref=s_ref.at[other],
+            dst_ref=rs_buf.at[row],
+            send_sem=sems.at[5],
+            recv_sem=sems.at[6],
+            device_id=(other, col),
+            device_id_type=MESH,
+        ).start()
+
+    for step in range(steps):
+        wait_like(half.at[step], sems.at[1 + step])
+
+        @pl.loop(0, span)
+        def _(k):
+            peer, device = place(k + step * span)
+            mine = w_ref[peer, core].astype(jnp.float32) + half[step, k].astype(jnp.float32)
+            half[step, k] = mine.astype(jnp.bfloat16)
+
+            @pl.when(k + step * span > 0)
+            def _():
+                pltpu.make_async_remote_copy(
+                    src_ref=half.at[step, k],
+                    dst_ref=got.at[me],
+                    send_sem=sems.at[7],
+                    recv_sem=sems.at[8],
+                    device_id=device,
+                    device_id_type=MESH,
+                ).start()
+
+        if step == 0:
+            got[me] = half[0, 0]
+            wait_like(rs_buf.at[pl.ds(0, rows - 1)], sems.at[6])
+            total = rs_buf[0]
+            for k in range(1, rows):
+                total = total + rs_buf[k]
+            own_buf[...] = total
+            col_buf[col] = total
+
+            @pl.loop(1, cols)
+            def _(k):
+                pltpu.make_async_remote_copy(
+                    src_ref=own_buf,
+                    dst_ref=col_buf.at[col],
+                    send_sem=sems.at[9],
+                    recv_sem=sems.at[10],
+                    device_id=(row, lax.rem(col + k, cols)),
+                    device_id_type=MESH,
+                ).start()
+
+        if step == 2:
+            wait_like(col_buf.at[pl.ds(0, cols - 1)], sems.at[10])
+            total = col_buf[0]
+            for k in range(1, cols):
+                total = total + col_buf[k]
+            so_ref[row] = total
+
+            @pl.loop(1, rows)
+            def _(k):
+                pltpu.make_async_remote_copy(
+                    src_ref=so_ref.at[row],
+                    dst_ref=so_ref.at[row],
+                    send_sem=sems.at[11],
+                    recv_sem=sems.at[12],
+                    device_id=(lax.rem(row + k, rows), col),
+                    device_id_type=MESH,
+                ).start()
+
+    wait_like(got.at[pl.ds(0, count - 1)], sems.at[8])
+    height = o_ref.shape[0]
+    for low in range(0, height, 16):
+
+        def add(k, total):
+            return total + got[k, low : low + 16, :].astype(jnp.float32)
+
+        o_ref[low : low + 16, :] = lax.fori_loop(
+            0, count, add, jnp.zeros((16, o_ref.shape[1]), jnp.float32)
+        )
+    wait_like(so_ref.at[pl.ds(0, rows - 1)], sems.at[12])
+    wait_like(so_ref.at[pl.ds(0, rows - 1)], sems.at[11])
+    wait_like(col_buf.at[pl.ds(0, cols - 1)], sems.at[9])
+    wait_like(rs_buf.at[pl.ds(0, rows - 1)], sems.at[5])
+    wait_like(half, sems.at[0])
+    wait_like(got.at[pl.ds(0, count - 1)], sems.at[7])
+
+
+def reduce_all(parts, small, number):
+    rows, cols = lax.axis_size("row"), lax.axis_size("col")
+    count, _, height, width = parts.shape
+    block = small.shape[1:]
+    return pl.pallas_call(
+        functools.partial(reduce_kernel, rows, cols),
+        out_shape=(
+            jax.ShapeDtypeStruct((height, width), jnp.float32),
+            jax.ShapeDtypeStruct(small.shape, jnp.float32),
+        ),
+        in_specs=[pl.BlockSpec(memory_space=pltpu.VMEM)] * 2,
+        out_specs=[pl.BlockSpec(memory_space=pltpu.VMEM)] * 2,
+        scratch_shapes=[
+            pltpu.VMEM((4, count // 4, height, width), jnp.bfloat16),
+            pltpu.VMEM((count, height, width), jnp.bfloat16),
+            pltpu.VMEM(small.shape, jnp.float32),
+            pltpu.VMEM(block, jnp.float32),
+            pltpu.VMEM((cols,) + block, jnp.float32),
+            pltpu.SemaphoreType.DMA((13,)),
+        ],
+        compiler_params=pltpu.CompilerParams(
+            collective_id=number, has_side_effects=True, vmem_limit_bytes=40 * 1024 * 1024
+        ),
+    )(parts, small)
 
 
 def small_sum_kernel(rows, cols, x_ref, o_ref, row_buf, sum_buf, col_buf, sems):
@@ -249,33 +411,457 @@
     )(parts)
 
 
-def pack_tokens(tokens_in):
-    channels = tokens_in.shape[-1]
-    shaped = tokens_in.reshape(8, 2, 8, 4, 2, channels // 2)
-    return shaped.transpose(0, 2, 4, 1, 3, 5).reshape(64, 16, channels // 2)
-
-
-def unpack_tokens(blocks):
-    half = blocks.shape[-1]
-    shaped = blocks.reshape(8, 8, 2, 2, 4, half).transpose(0, 3, 1, 4, 2, 5)
-    return shaped.reshape(16 * 32, 2 * half)
-
-
-def split_sum(values):
-    rows = lax.axis_size("row")
-    parts = values.reshape(rows, -1, 128)
-    own = jnp.sum(lax.all_to_all(parts, "row", 0, 0, tiled=True), axis=0)
-    own = gather_sum(own.reshape(-1, 128), "col")
-    spread = jnp.broadcast_to(own, (rows,) + own.shape)
-    return lax.all_to_all(spread, "row", 0, 0, tiled=True)
-
-
-def weight_grad(left_side, right_side):
-    count = lax.axis_size("row") * lax.axis_size("col")
-    partial = lax.dot_general(left_side, right_side, CONTRACT, preferred_element_type=jnp.float32)
-    height, width = partial.shape
-    parts = partial.astype(jnp.bfloat16).reshape(count, height // count, width)
-    return jnp.sum(exchange_all(parts).astype(jnp.float32), axis=0)
+ROWS = 16
+COLS = 32
+MAIN = (ROWS + 2) * COLS
+SIDE = (ROWS + 2) * 8
+
+
+def edge_masks():
+    row, col = lax.axis_index("row"), lax.axis_index("col")
+    rows, cols = lax.axis_size("row"), lax.axis_size("col")
+    return tuple(
+        jnp.where(present, 1.0, 0.0).astype(jnp.float32)
+        for present in (row > 0, row < rows - 1, col > 0, col < cols - 1)
+    )
+
+
+def fill_sides(got_ref, side_ref, masks, tiles):
+    up, down, left, right = masks
+    start = 2 * COLS
+    corner = 2 * (COLS + ROWS)
+    for tile in range(tiles):
+        lanes = slice(tile * 128, (tile + 1) * 128)
+        before = got_ref[start : start + ROWS, lanes].astype(jnp.float32)
+        after = got_ref[start + ROWS : start + 2 * ROWS, lanes].astype(jnp.float32)
+        side_ref[tile, pl.ds(8, ROWS, stride=8), :] = after * right
+        side_ref[tile, pl.ds(15, ROWS, stride=8), :] = before * left
+        corners = got_ref[corner : corner + 64, lanes].astype(jnp.float32)
+        side_ref[tile, 7:8, :] = corners[15:16] * (up * left)
+        side_ref[tile, 0:1, :] = corners[16:17] * (up * right)
+        side_ref[tile, SIDE - 1 : SIDE, :] = corners[47:48] * (down * left)
+        side_ref[tile, SIDE - 8 : SIDE - 7, :] = corners[48:49] * (down * right)
+
+
+def expand_kernel(
+    x_ref, got_ref, w_ref, taps_ref, mixed_ref, slope_mix_ref, slope_ref, main_ref, side_out_ref,
+    pooled_ref, normed, normed_side, side, pre, pre_side, padded
+):
+    step = pl.program_id(0)
+
+    @pl.when(step == 0)
+    def _():
+        masks = edge_masks()
+        side[...] = jnp.zeros_like(side)
+        fill_sides(got_ref, side, masks, 4)
+        values = jnp.concatenate([side[tile] for tile in range(4)], axis=-1)
+        present = jnp.max(jnp.abs(values), axis=-1, keepdims=True) > 0.0
+        standard = layer_normalize(values)[0]
+        normed_side[...] = jnp.where(present, standard, 0.0).astype(jnp.bfloat16)
+        normed[0:COLS, :] = (layer_normalize(got_ref[0:COLS, :])[0] * masks[0]).astype(jnp.bfloat16)
+        normed[MAIN - COLS : MAIN, :] = (
+            layer_normalize(got_ref[COLS : 2 * COLS, :])[0] * masks[1]
+        ).astype(jnp.bfloat16)
+
+        @pl.loop(0, ROWS)
+        def _(y):
+            rows = pl.ds(pl.multiple_of(y * COLS, COLS), COLS)
+            after = pl.ds(pl.multiple_of((y + 1) * COLS, COLS), COLS)
+            normed[after, :] = layer_normalize(x_ref[rows, :])[0].astype(jnp.bfloat16)
+
+    width = w_ref.shape[1]
+    pre[...] = jnp.dot(normed[...], w_ref[...], preferred_element_type=jnp.float32)
+    pre_side[...] = jnp.dot(normed_side[...], w_ref[...], preferred_element_type=jnp.float32)
+
+    @pl.loop(0, ROWS + 2)
+    def _(y):
+        rows = pl.ds(pl.multiple_of(y * COLS, COLS), COLS)
+        result, slope = gelu_slope(pre[rows, :])
+        rounded = result.astype(jnp.bfloat16)
+        main_ref[rows, :] = rounded
+        padded[y, 8 : 8 + COLS, :] = rounded.astype(jnp.float32)
+
+        @pl.when((y > 0) & (y <= ROWS))
+        def _():
+            before = pl.ds(pl.multiple_of((y - 1) * COLS, COLS), COLS)
+            slope_ref[before, :] = slope
+
+        eight = pl.ds(pl.multiple_of(y * 8, 8), 8)
+        edge = gelu_slope(pre_side[eight, :])[0].astype(jnp.bfloat16).astype(jnp.float32)
+        pre_side[eight, :] = edge
+        padded[y, 0:8, :] = edge
+        padded[y, 8 + COLS : 16 + COLS, :] = edge
+
+    side_out_ref[...] = pre_side[...].astype(jnp.bfloat16)
+
+    def mix(y, total):
+        summed = jnp.zeros((COLS, width), jnp.float32)
+        for r in range(3):
+            for c in range(3):
+                window = padded[y + r, 7 + c : 7 + c + COLS, :]
+                summed = summed + window * taps_ref[3 * r + c : 3 * r + c + 1, :]
+        mixed, slope = gelu_slope(summed)
+        rows = pl.ds(pl.multiple_of(y * COLS, COLS), COLS)
+        mixed_ref[rows, :] = mixed
+        slope_mix_ref[rows, :] = slope
+        return total + jnp.sum(mixed.reshape(COLS // 8, 8, width), axis=0)
+
+    total = lax.fori_loop(0, ROWS, mix, jnp.zeros((8, width), jnp.float32))
+    total = jnp.sum(total, axis=0, keepdims=True)
+    for tile in range(width // 128):
+        pooled_ref[0, tile : tile + 1, :] = total[:, tile * 128 : (tile + 1) * 128]
+
+
+def expand_and_mix(tokens_in, got, w_expand, taps):
+    tokens, channels = tokens_in.shape
+    hidden = w_expand.shape[1]
+    width = 256
+    steps = hidden // width
+
+    def fixed(shape):
+        return pl.BlockSpec(shape, lambda e: (0, 0))
+
+    def moving(height):
+        return pl.BlockSpec((height, width), lambda e: (0, e))
+
+    wide = jax.ShapeDtypeStruct((tokens, hidden), jnp.float32)
+    return pl.pallas_call(
+        expand_kernel,
+        grid=(steps,),
+        out_shape=(
+            wide,
+            wide,
+            wide,
+            jax.ShapeDtypeStruct((MAIN, hidden), jnp.bfloat16),
+            jax.ShapeDtypeStruct((SIDE, hidden), jnp.bfloat16),
+            jax.ShapeDtypeStruct((steps, width // 128, 128), jnp.float32),
+        ),
+        in_specs=[fixed(tokens_in.shape), fixed(got.shape), moving(channels), moving(9)],
+        out_specs=[
+            moving(tokens),
+            moving(tokens),
+            moving(tokens),
+            moving(MAIN),
+            moving(SIDE),
+            pl.BlockSpec((1, width // 128, 128), lambda e: (e, 0, 0)),
+        ],
+        scratch_shapes=[
+            pltpu.VMEM((MAIN, channels), jnp.bfloat16),
+            pltpu.VMEM((SIDE, channels), jnp.bfloat16),
+            pltpu.VMEM((4, SIDE, 128), jnp.float32),
+            pltpu.VMEM((MAIN, width), jnp.float32),
+            pltpu.VMEM((SIDE, width), jnp.float32),
+            pltpu.VMEM((ROWS + 2, COLS + 16, width), jnp.float32),
+        ],
+        compiler_params=pltpu.CompilerParams(vmem_limit_bytes=40 * 1024 * 1024),
+    )(tokens_in, got, w_expand, taps)
+
+
+def project_kernel(
+    mixed_ref, gate_ref, x_ref, cot_ref, w_ref, scaled_ref, middle_ref, out_ref, flat, packed
+):
+    scaled = (mixed_ref[...] * gate_ref[...]).astype(jnp.bfloat16)
+    scaled_ref[...] = scaled
+    middle = x_ref[...].astype(jnp.float32) + jnp.dot(
+        scaled, w_ref[...], preferred_element_type=jnp.float32
+    )
+    middle_ref[...] = middle
+
+    def pack(values, first_row):
+        for piece in range(4):
+            flat[piece] = values[:, piece * 128 : (piece + 1) * 128]
+        for piece in range(4):
+            half, tile = piece // 2, piece % 2
+            for a in range(2):
+                for place in range(8):
+                    source = a * 64 + (place // 4) * 32 + place % 4
+                    packed[tile, pl.ds(a * 128 + half * 8 + place, 8, stride=16), :] = flat[
+                        piece, pl.ds(source, 8, stride=4), :
+                    ]
+        for tile in range(2):
+            out_ref[:, first_row : first_row + 16, tile * 128 : (tile + 1) * 128] = (
+                packed[tile].reshape(16, 16, 128).astype(jnp.bfloat16)
+            )
+
+    pack(layer_normalize(middle)[0], 0)
+    pack(cot_ref[...].astype(jnp.float32), 16)
+
+
+def project(mixed, gate, tokens_in, cotangent, w_project):
+    tokens, hidden = mixed.shape
+    channels = w_project.shape[1]
+    height = 128
+
+    def moving(width):
+        return pl.BlockSpec((height, width), lambda t: (t, 0))
+
+    def fixed(shape):
+        return pl.BlockSpec(shape, lambda t: (0, 0))
+
+    return pl.pallas_call(
+        project_kernel,
+        grid=(tokens // height,),
+        out_shape=(
+            jax.ShapeDtypeStruct((tokens, hidden), jnp.bfloat16),
+            jax.ShapeDtypeStruct((tokens, channels), jnp.float32),
+            jax.ShapeDtypeStruct((64, 32, channels // 2), jnp.bfloat16),
+        ),
+        in_specs=[
+            moving(hidden),
+            fixed((1, hidden)),
+            moving(channels),
+            moving(channels),
+            fixed(w_project.shape),
+        ],
+        out_specs=[
+            moving(hidden),
+            moving(channels),
+            pl.BlockSpec((16, 32, channels // 2), lambda t: (t, 0, 0)),
+        ],
+        scratch_shapes=[
+            pltpu.VMEM((4, height, 128), jnp.float32),
+            pltpu.VMEM((2, 256, 128), jnp.float32),
+        ],
+        compiler_params=pltpu.CompilerParams(vmem_limit_bytes=40 * 1024 * 1024),
+    )(mixed, gate, tokens_in, cotangent, w_project)
+
+
+def middle_kernel(
+    ret_ref, middle_ref, cot_ref, mixed_ref, wout_ref, wproj_ref, out_ref, grad_ref, grad_b_ref,
+    scaled_grad_ref, gate_ref, flat, packed, total
+):
+    step = pl.program_id(0)
+
+    def unpack(first_row):
+        for tile in range(2):
+            block = ret_ref[:, first_row : first_row + 16, tile * 128 : (tile + 1) * 128]
+            packed[tile] = block.astype(jnp.float32).reshape(256, 128)
+        for piece in range(4):
+            half, tile = piece // 2, piece % 2
+            for a in range(2):
+                for place in range(8):
+                    target = a * 64 + (place // 4) * 32 + place % 4
+                    flat[piece, pl.ds(target, 8, stride=4), :] = packed[
+                        tile, pl.ds(a * 128 + half * 8 + place, 8, stride=16), :
+                    ]
+        return jnp.concatenate([flat[piece] for piece in range(4)], axis=-1)
+
+    middle = middle_ref[...]
+    context = unpack(0).astype(jnp.bfloat16)
+    out_ref[...] = (
+        middle + jnp.dot(context, wout_ref[...], preferred_element_type=jnp.float32)
+    ).astype(jnp.bfloat16)
+    standard, inverse = layer_normalize(middle)
+    grad = cot_ref[...].astype(jnp.float32) + norm_backward_pass(standard, inverse, unpack(16))
+    grad_ref[...] = grad
+    grad_b = grad.astype(jnp.bfloat16)
+    grad_b_ref[...] = grad_b
+
+    @pl.when(step == 0)
+    def _():
+        total[...] = jnp.zeros_like(total)
+
+    hidden = wproj_ref.shape[0]
+    for low in range(0, hidden, 512):
+        scaled_grad = lax.dot_general(
+            grad_b, wproj_ref[low : low + 512, :], BACKWARD, preferred_element_type=jnp.float32
+        )
+        scaled_grad_ref[:, low : low + 512] = scaled_grad
+        terms = scaled_grad * mixed_ref[:, low : low + 512]
+        total[:, low : low + 512] += jnp.sum(terms.reshape(-1, 8, 512), axis=0)
+
+    @pl.when(step == pl.num_programs(0) - 1)
+    def _():
+        for tile in range(hidden // 128):
+            gate_ref[tile : tile + 1, :] = jnp.sum(
+                total[:, tile * 128 : (tile + 1) * 128], axis=0, keepdims=True
+            )
+
+
+def middle_backward(returned, middle, cotangent, mixed, w_out, w_project):
+    tokens, hidden = mixed.shape
+    channels = middle.shape[1]
+    height = 128
+
+    def moving(width):
+        return pl.BlockSpec((height, width), lambda t: (t, 0))
+
+    def fixed(shape):
+        return pl.BlockSpec(shape, lambda t: (0, 0))
+
+    return pl.pallas_call(
+        middle_kernel,
+        grid=(tokens // height,),
+        out_shape=(
+            jax.ShapeDtypeStruct((tokens, channels), jnp.bfloat16),
+            jax.ShapeDtypeStruct((tokens, channels), jnp.float32),
+            jax.ShapeDtypeStruct((tokens, channels), jnp.bfloat16),
+            jax.ShapeDtypeStruct((tokens, hidden), jnp.float32),
+            jax.ShapeDtypeStruct((hidden // 128, 128), jnp.float32),
+        ),
+        in_specs=[
+            pl.BlockSpec((16, 32, channels // 2), lambda t: (t, 0, 0)),
+            moving(channels),
+            moving(channels),
+            moving(hidden),
+            fixed(w_out.shape),
+            fixed(w_project.shape),
+        ],
+        out_specs=[
+            moving(channels),
+            moving(channels),
+            moving(channels),
+            moving(hidden),
+            fixed((hidden // 128, 128)),
+        ],
+        scratch_shapes=[
+            pltpu.VMEM((4, height, 128), jnp.float32),
+            pltpu.VMEM((2, 256, 128), jnp.float32),
+            pltpu.VMEM((8, hidden), jnp.float32),
+        ],
+        compiler_params=pltpu.CompilerParams(vmem_limit_bytes=40 * 1024 * 1024),
+    )(returned, middle, cotangent, mixed, w_out, w_project)
+
+
+def regroup(values, flat, place, first):
+    for tile in range(4):
+        flat[tile] = values[:, tile * 128 : (tile + 1) * 128]
+    for tile in range(4):
+        for r in range(4):
+            place[tile, pl.ds(first + r, 128, stride=16), :] = flat[
+                tile, pl.ds(r, 128, stride=4), :
+            ]
+
+
+def back_kernel(
+    premix_ref, got_ref, main_ref, side_in_ref, slope_ref, w_ref, taps_ref, x_ref, grad_ref,
+    out_ref, parts_ref, terms_ref, turned, side, padded, expanded, preexp, total, flat, place
+):
+    step = pl.program_id(0)
+    last = pl.num_programs(0) - 1
+
+    @pl.when(step == 0)
+    def _():
+        side[...] = jnp.zeros_like(side)
+        total[...] = jnp.zeros_like(total)
+        turned[...] = layer_normalize(x_ref[...])[0].T.astype(jnp.bfloat16)
+
+    masks = edge_masks()
+    fill_sides(got_ref, side, masks, 4)
+    padded[0, 8 : 8 + COLS, :] = got_ref[0:COLS, :].astype(jnp.float32) * masks[0]
+    padded[ROWS + 1, 8 : 8 + COLS, :] = got_ref[COLS : 2 * COLS, :].astype(jnp.float32) * masks[1]
+
+    @pl.loop(0, ROWS)
+    def _(y):
+        rows = pl.ds(pl.multiple_of(y * COLS, COLS), COLS)
+        padded[y + 1, 8 : 8 + COLS, :] = premix_ref[rows, :].astype(jnp.float32)
+
+    pairs = (ROWS + 2) // 2
+
+    @pl.loop(0, ROWS + 2)
+    def _(y):
+        rows = pl.ds(pl.multiple_of(y * COLS, COLS), COLS)
+        expanded[y, 8 : 8 + COLS, :] = main_ref[rows, :].astype(jnp.float32)
+        eight = pl.ds(pl.multiple_of(y * 8, 8), 8)
+        edge = jnp.concatenate([side[tile, eight, :] for tile in range(4)], axis=-1)
+        padded[y, 0:8, :] = edge
+        padded[y, 8 + COLS : 16 + COLS, :] = edge
+
+    @pl.loop(0, pairs)
+    def _(y):
+        both = side_in_ref[pl.ds(pl.multiple_of(y * 16, 16), 16), :].astype(jnp.float32)
+        for k in range(2):
+            edge = both[8 * k : 8 * k + 8]
+            expanded[2 * y + k, 0:8, :] = edge
+            expanded[2 * y + k, 8 + COLS : 16 + COLS, :] = edge
+
+    for low in range(0, 512, 256):
+        lanes = slice(low, low + 256)
+
+        def unmix(y, sums):
+            rows = pl.ds(pl.multiple_of(y * COLS, COLS), COLS)
+            own = padded[y + 1, 8 : 8 + COLS, lanes]
+            summed = jnp.zeros((COLS, 256), jnp.float32)
+            new = []
+            for r in range(3):
+                for c in range(3):
+                    window = padded[y + 2 - r, 9 - c : 9 - c + COLS, lanes]
+                    summed = summed + window * taps_ref[3 * r + c : 3 * r + c + 1, lanes]
+                    term = own * expanded[y + r, 7 + c : 7 + c + COLS, lanes]
+                    new.append(sums[3 * r + c] + jnp.sum(term.reshape(-1, 8, 256), axis=0))
+            preexp[rows, lanes] = (summed * slope_ref[rows, lanes]).astype(jnp.bfloat16)
+            return tuple(new)
+
+        sums = lax.fori_loop(0, ROWS, unmix, (jnp.zeros((8, 256), jnp.float32),) * 9)
+        for k in range(9):
+            terms_ref[k : k + 1, lanes] = jnp.sum(sums[k], axis=0, keepdims=True)
+
+    regroup(
+        jnp.dot(turned[...], preexp[...], preferred_element_type=jnp.float32), flat, place, step * 4
+    )
+    total[...] += lax.dot_general(
+        preexp[...], w_ref[...], BACKWARD, preferred_element_type=jnp.float32
+    )
+
+    @pl.when(step == last)
+    def _():
+        for tile in range(4):
+            parts_ref[:, :, tile * 128 : (tile + 1) * 128] = (
+                place[tile].reshape(128, 16, 128).astype(jnp.bfloat16)
+            )
+
+        @pl.loop(0, ROWS)
+        def _(y):
+            rows = pl.ds(pl.multiple_of(y * COLS, COLS), COLS)
+            standard, inverse = layer_normalize(x_ref[rows, :])
+            out_ref[rows, :] = (
+                grad_ref[rows, :] + norm_backward_pass(standard, inverse, total[rows, :])
+            ).astype(jnp.bfloat16)
+
+
+def mix_backward(premix, got, main, side, slope, w_expand, taps, tokens_in, grad):
+    tokens, hidden = premix.shape
+    channels = w_expand.shape[0]
+    width = 512
+
+    def fixed(shape):
+        return pl.BlockSpec(shape, lambda e: (0,) * len(shape))
+
+    def moving(height):
+        return pl.BlockSpec((height, width), lambda e: (0, e))
+
+    return pl.pallas_call(
+        back_kernel,
+        grid=(hidden // width,),
+        out_shape=(
+            jax.ShapeDtypeStruct((tokens, channels), jnp.bfloat16),
+            jax.ShapeDtypeStruct((128, 16, width), jnp.bfloat16),
+            jax.ShapeDtypeStruct((9, hidden), jnp.float32),
+        ),
+        in_specs=[
+            moving(tokens),
+            moving(got.shape[0]),
+            moving(MAIN),
+            moving(SIDE),
+            moving(tokens),
+            moving(channels),
+            moving(9),
+            fixed(tokens_in.shape),
+            fixed(grad.shape),
+        ],
+        out_specs=[fixed((tokens, channels)), fixed((128, 16, width)), moving(9)],
+        scratch_shapes=[
+            pltpu.VMEM((channels, tokens), jnp.bfloat16),
+            pltpu.VMEM((4, SIDE, 128), jnp.float32),
+            pltpu.VMEM((ROWS + 2, COLS + 16, width), jnp.float32),
+            pltpu.VMEM((ROWS + 2, COLS + 16, width), jnp.float32),
+            pltpu.VMEM((tokens, width), jnp.bfloat16),
+            pltpu.VMEM((tokens, channels), jnp.float32),
+            pltpu.VMEM((4, tokens, 128), jnp.float32),
+            pltpu.VMEM((4, 2048, 128), jnp.float32),
+        ],
+        compiler_params=pltpu.CompilerParams(vmem_limit_bytes=50 * 1024 * 1024),
+    )(premix, got, main, side, slope, w_expand, taps, tokens_in, grad)
 
 
 HEAD_DIM = 32
@@ -290,14 +876,17 @@
     wout_ref,
     bias_ref,
     ret_ref,
+    parts_ref,
+    table_ref,
+    spread,
+    qkv,
+    cgrad,
     normed_ref,
     proj_ref,
     context_ref,
     cot_ref,
-    table_ref,
-    spread,
-    qkv,
-    cgrad,
+    flat,
+    place,
 ):
     channels = wout_ref.shape[0]
     factor = HEAD_DIM ** (-0.5)
@@ -421,27 +1010,55 @@
             spread[tile].reshape(64, 16, 128).astype(jnp.bfloat16)
         )
 
+    for q in range(3):
+        regroup(
+            lax.dot_general(
+                normed_ref[...],
+                proj_ref[:, q * channels : (q + 1) * channels],
+                CONTRACT,
+                preferred_element_type=jnp.float32,
+            ),
+            flat,
+            place,
+            q * 4,
+        )
+    regroup(
+        lax.dot_general(
+            context_ref[...], cot_ref[...], CONTRACT, preferred_element_type=jnp.float32
+        ),
+        flat,
+        place,
+        12,
+    )
+    for tile in range(4):
+        parts_ref[:, :, tile * 128 : (tile + 1) * 128] = (
+            place[tile].reshape(128, 16, 128).astype(jnp.bfloat16)
+        )
+
 
 def attention(blocks, w_qkv, w_out, bias):
     channels = w_out.shape[0]
     tokens = GROUPS * PLACES
     shapes = (
         jax.ShapeDtypeStruct(blocks.shape, jnp.bfloat16),
-        jax.ShapeDtypeStruct((tokens, channels), jnp.bfloat16),
-        jax.ShapeDtypeStruct((tokens, 3 * channels), jnp.bfloat16),
-        jax.ShapeDtypeStruct((tokens, channels), jnp.bfloat16),
-        jax.ShapeDtypeStruct((tokens, channels), jnp.bfloat16),
+        jax.ShapeDtypeStruct((128, 16, channels), jnp.bfloat16),
         jax.ShapeDtypeStruct(bias.shape, jnp.float32),
     )
     return pl.pallas_call(
         attention_kernel,
         out_shape=shapes,
         in_specs=[pl.BlockSpec(memory_space=pltpu.VMEM)] * 4,
-        out_specs=[pl.BlockSpec(memory_space=pltpu.VMEM)] * 6,
+        out_specs=[pl.BlockSpec(memory_space=pltpu.VMEM)] * 3,
         scratch_shapes=[
             pltpu.VMEM((2, 1024, 128), jnp.float32),
             pltpu.VMEM((tokens, 3 * channels), jnp.bfloat16),
             pltpu.VMEM((tokens, channels), jnp.bfloat16),
+            pltpu.VMEM((tokens, channels), jnp.bfloat16),
+            pltpu.VMEM((tokens, 3 * channels), jnp.bfloat16),
+            pltpu.VMEM((tokens, channels), jnp.bfloat16),
+            pltpu.VMEM((tokens, channels), jnp.bfloat16),
+            pltpu.VMEM((4, tokens, 128), jnp.float32),
+            pltpu.VMEM((4, 2048, 128), jnp.float32),
         ],
         compiler_params=pltpu.CompilerParams(vmem_limit_bytes=40 * 1024 * 1024),
     )(blocks, w_qkv, w_out, bias)
@@ -466,39 +1083,21 @@
         .transpose(0, 2, 1, 3)
         .reshape(heads // QUAD, places, QUAD * places)
     )
-    first_standardized, inverse_deviation_first = layer_normalize(inputs)
-    first_normed_input = first_standardized.astype(jnp.bfloat16)
-    pre_expand = jnp.dot(
-        first_normed_input.reshape(tokens, channels), w_expand, preferred_element_type=jnp.float32
-    )
-    expanded_f, slope_expand = gelu_slope(
-        pre_expand.reshape(images, tile_rows, tile_cols, hidden_units)
-    )
-    padded = padded_2(expanded_f.astype(jnp.bfloat16), (("row", 1), ("col", 2)), 1)
-    pre_mix = depthwise(padded, dw_kernel)
-    mixed, slope_mix = gelu_slope(pre_mix)
-    pooled = small_sum(jnp.sum(mixed, axis=(1, 2)).reshape(-1, 128), 3).reshape(images, -1) / cells
+    flat_inputs = inputs.reshape(tokens, channels)
+    flattened_cotangent = out_grad.reshape(tokens, channels)
+    taps = dw_kernel.reshape(9, hidden_units)
+    mixed, slope_mix, slope_expand, main, side, pooled = expand_and_mix(
+        flat_inputs, halo(inputs[0], 5), w_expand, taps
+    )
+    pooled = small_sum(pooled.reshape(-1, 128), 3).reshape(images, -1) / cells
     squeeze_pre = jnp.dot(pooled, se_reduce, precision=HIGHEST)
     squeeze_sig = jax.nn.sigmoid(squeeze_pre)
     squeezed = squeeze_pre * squeeze_sig
     gate = jax.nn.sigmoid(jnp.dot(squeezed, se_expand, precision=HIGHEST))
-    scaled = (mixed * gate[:, None, None, :]).astype(jnp.bfloat16).reshape(tokens, hidden_units)
-    middle_activation = inputs.astype(jnp.float32).reshape(tokens, channels) + jnp.dot(
-        scaled, w_project, preferred_element_type=jnp.float32
-    )
-    second_standardized, inverse_deviation_second = layer_normalize(middle_activation)
-    second_normed_input = second_standardized.astype(jnp.bfloat16)
-    flattened_cotangent = out_grad.reshape(tokens, channels)
-    outgoing = jnp.concatenate(
-        [
-            pack_tokens(second_normed_input.reshape(tile_rows, tile_cols, channels)),
-            pack_tokens(out_grad.reshape(tile_rows, tile_cols, channels)),
-        ],
-        axis=1,
-    )
-    returned, grid_normed, grid_proj, grid_context, grid_cotangent, scores_sum = attention(
-        swap(outgoing, 1), w_qkv, w_out, bias
-    )
+    scaled, middle_activation, outgoing = project(
+        mixed, gate, flat_inputs, flattened_cotangent, w_project
+    )
+    returned, attention_parts, scores_sum = attention(swap(outgoing, 1), w_qkv, w_out, bias)
     table_part = lax.dot_general(
         scores_sum.reshape(heads // QUAD, places, QUAD, places)
         .transpose(0, 2, 1, 3)
@@ -507,24 +1106,14 @@
         BACKWARD,
         precision=HIGHEST,
     )
-    out_proj_grad = weight_grad(grid_context, grid_cotangent) * factor
-    qkv_grad = weight_grad(grid_normed, grid_proj) * factor
-    returned = swap(returned, 2)
-    context_flat = unpack_tokens(returned[:, :16])
-    second_normed_gradient = unpack_tokens(returned[:, 16:])
-    block_out = (
-        middle_activation + jnp.dot(context_flat, w_out, preferred_element_type=jnp.float32)
-    ).astype(jnp.bfloat16)
-    middle_gradient = flattened_cotangent.astype(jnp.float32) + norm_backward_pass(
-        second_standardized, inverse_deviation_second, second_normed_gradient
-    )
-    middle_b = middle_gradient.astype(jnp.bfloat16)
-    project_grad = weight_grad(scaled, middle_b) * factor
-    scaled_grad = lax.dot_general(
-        middle_b, w_project, BACKWARD, preferred_element_type=jnp.float32
-    ).reshape(images, tile_rows, tile_cols, hidden_units)
-    gate_grad = small_sum(jnp.sum(scaled_grad * mixed, axis=(1, 2)).reshape(-1, 128), 4).reshape(
-        images, -1
+    block_out, middle_gradient, middle_b, scaled_grad, gate_grad = middle_backward(
+        swap(returned, 2), middle_activation, flattened_cotangent, mixed, w_out, w_project
+    )
+    gate_grad = small_sum(gate_grad, 4).reshape(images, -1)
+    project_parts = (
+        lax.dot_general(scaled, middle_b, CONTRACT, preferred_element_type=jnp.float32)
+        .astype(jnp.bfloat16)
+        .reshape(128, 16, channels)
     )
     excite_grad = gate_grad * gate * (1.0 - gate)
     squeezed_grad = lax.dot_general(excite_grad, se_expand, BACKWARD, precision=HIGHEST)
@@ -532,31 +1121,40 @@
     pooled_grad = lax.dot_general(squeeze_grad, se_reduce, BACKWARD, precision=HIGHEST)
     se_reduce_grad = lax.dot_general(pooled, squeeze_grad, CONTRACT, precision=HIGHEST) * factor
     se_expand_grad = lax.dot_general(squeezed, excite_grad, CONTRACT, precision=HIGHEST) * factor
-    premix_grad = (
-        (scaled_grad * gate[:, None, None, :] + pooled_grad[:, None, None, :] / cells) * slope_mix
-    ).astype(jnp.bfloat16)
-    grad_padded = padded_2(premix_grad, (("row", 1), ("col", 2)), 1)
-    kernel_part = kernel_terms(padded, premix_grad)
-    expanded_grad = depthwise(grad_padded, dw_kernel[::-1, ::-1])
-    preexp_grad = (expanded_grad * slope_expand).astype(jnp.bfloat16).reshape(tokens, hidden_units)
-    expand_grad = weight_grad(first_normed_input.reshape(tokens, channels), preexp_grad) * factor
-    first_normed_gradient = lax.dot_general(
-        preexp_grad, w_expand, BACKWARD, preferred_element_type=jnp.float32
-    ).reshape(images, tile_rows, tile_cols, channels)
-    input_gradient = (
-        middle_gradient.reshape(images, tile_rows, tile_cols, channels)
-        + norm_backward_pass(first_standardized, inverse_deviation_first, first_normed_gradient)
-    ).astype(jnp.bfloat16)
+    premix_grad = ((scaled_grad * gate + pooled_grad / cells) * slope_mix).astype(jnp.bfloat16)
+    input_gradient, expand_parts, kernel_part = mix_backward(
+        premix_grad,
+        halo(premix_grad.reshape(tile_rows, tile_cols, hidden_units), 6),
+        main,
+        side,
+        slope_expand,
+        w_expand,
+        taps,
+        flat_inputs,
+        middle_gradient,
+    )
     small = jnp.concatenate([kernel_part.reshape(-1), table_part.reshape(-1)])
     unit = lax.axis_size("row") * 1024
     room = -small.shape[0] % unit
-    small = split_sum(jnp.pad(small, (0, room))).reshape(-1)
+    small = jnp.pad(small, (0, room)).reshape(lax.axis_size("row"), -1, 128)
+    parts = jnp.concatenate([project_parts, expand_parts, attention_parts], axis=1)
+    summed, small = reduce_all(parts.reshape(64, 2, 48, channels), small, 7)
+    summed = summed * factor
+    project_grad = summed[:16]
+
+    def from_blocks(blocks):
+        return blocks.reshape(-1, 4, channels).transpose(1, 0, 2).reshape(4, -1)
+
+    expand_grad = from_blocks(summed[16:32])
+    qkv_grad = from_blocks(summed[32:44])
+    out_proj_grad = summed[44:48]
+    small = small.reshape(-1)
     kernel_size = kernel_part.size
-    kernel_sum = small[:kernel_size].reshape(kernel_part.shape)
+    kernel_sum = small[:kernel_size].reshape(dw_kernel.shape)
     table_sum = small[kernel_size : kernel_size + table_part.size].reshape(table_part.shape)
     return (
         block_out.reshape(images, tile_rows, tile_cols, channels),
-        input_gradient,
+        input_gradient.reshape(images, tile_rows, tile_cols, channels),
         expand_grad,
         project_grad,
         qkv_grad,

time: 392 us -> 327 us (0.83)
  Pallas kernels: 104 us -> 253 us
  other arithmetic: 77.3 us -> 13.7 us
  starting transfers between devices: 52.1 us -> 0 us
  waiting for transfers between devices: 50.3 us -> 0 us
  matrix products: 38 us -> 10.6 us
  blocking collectives: 12.3 us -> 0 us
  local copies, waits for them, and re-layouts: 49.1 us -> 43.7 us
    pallas_call x0 -> x7, Pallas kernels: none -> 153 us  [the longest x1 63.1 us: reduce_all(): pl.pallas_call(functools.partial(reduce_kernel, rows, cols), out_shape=(j...]
    all_to_all x6 -> x0, waiting for transfers between devices: 43.1 us -> none  [the longest x4 35.6 us: exchange_all(): return lax.all_to_all(parts, AXES, 0, 0, tiled=True)]
    all_to_all x6 -> x0, starting transfers between devices: 37.1 us -> none  [the longest x4 30.2 us: exchange_all(): return lax.all_to_all(parts, AXES, 0, 0, tiled=True)]
    reduce_sum x15 -> x0, other arithmetic: 33.5 us -> none  [the longest x1 13.8 us: kernel_terms(): collected.append(jnp.sum(window * grads_wide, axis=(0, 1, 2)))]
    dot_general x9 -> x1, matrix products: 24.6 us -> 2.98 us  [on_device(): lax.dot_general(scaled, middle_b, CONTRACT, preferred_element_type=jnp.fl...]
    unnamed x128 -> x91, local copies, waits for them, and re-layouts: 11.1 us -> 32.5 us
    convert_element_type x7 -> x1, other arithmetic: 23.8 us -> 4.59 us  [on_device(): ((scaled_grad * gate + pooled_grad / cells) * slope_mix).astype(jnp.bfloa...]
    ppermute x8 -> x0, starting transfers between devices: 15 us -> none  [the longest x4 9.82 us: padded_2(): lax.ppermute(tail, axis, [(i, (i + 1) % count) for i in range(ends)])]
  transfers between devices with their start and end apart: 14 -> 0, of which waited for: 9 -> 0; matrix products, arithmetic and copies ran while one was open for 18% -> 0% of each run, Pallas kernels for 0% -> 0%
where the time goes in v1:
time: 327 us; the launch traced here: 322 us
  Pallas kernels  253 us (77%)
  local copies, waits for them, and re-layouts  43.7 us (13%)
  other arithmetic  13.7 us (4%)
  matrix products  10.6 us (3%)
    pallas_call x1, Pallas kernels, reduce_all(): pl.pallas_call(functools.partial(reduce_kernel, rows, cols), out_shape=(j...  63.1 us
    pallas_call x2, Pallas kernels, swap(): pl.pallas_call(functools.partial(swap_kernel, parity, GRID, lax.axis_size...  44.9 us
    unnamed x91, local copies, waits for them, and re-layouts  32.5 us
    pallas_call x2, Pallas kernels, small_sum(): pl.pallas_call(functools.partial(small_sum_kernel, rows, cols), out_shape...  30.4 us
    pallas_call x2, Pallas kernels, halo(): pl.pallas_call(body, out_shape=jax.ShapeDtypeStruct((total, features), ce...  27.3 us
    pallas_call x1, Pallas kernels, mix_backward(): pl.pallas_call(back_kernel, grid=(hidden // width,), out_shape=(jax.Shape...  27 us
    pallas_call x1, Pallas kernels, expand_and_mix(): pl.pallas_call(expand_kernel, grid=(steps,), out_shape=(wide, wide, wide,...  25.2 us
    pallas_call x1, Pallas kernels, attention(): pl.pallas_call(attention_kernel, out_shape=shapes, in_specs=[pl.BlockSpec...  24.5 us

profile of v1, /device:TPU:0, one launch (start us, length us, event | category | flops | bytes accessed | tf_op | source)
XLA Modules:
  0.0 321.9 jit_solution(4957077653444732406)
XLA Ops:
  0.8 1.5 slice_bitcast_fusion
  2.3 0.9 reshape.232.taps_ref
  3.3 2.0 convolution_bitcast_fusion
  5.6 1.1 copy.40
  6.7 1.4 reshape.236.bias_ref
  9.0 12.7 %shard_map.177.got_ref = bf16[160,512]{1,0:T(8,128)(2,1)} custom-call(bf16[32,512]{1,0:T(8,128)(2,1)} %get-tuple-element.61.refs_0_, bf16[32,512]{1,0:T(8,128)(2,1)} %get-tuple-element.60.refs_1_, bf16[16,512]{1,0:T(8,128)(2,1)} %get-tuple-element.59.refs_2_, bf16[16,512]{1,0:T(8,128)(2,1)} %get-tuple-element.58.refs_3_), custom_call_target="tpu_custom_call" | custom-call | tf_op jit(solution)/shard_map/pallas_call | solution.py:111
  21.8 1.6 copy-done.5
  23.4 0.9 copy-done.25
  24.3 25.2 %shard_map.178 = (f32[512,2048]{1,0:T(8,128)S(1)}, f32[512,2048]{1,0:T(8,128)S(1)}, f32[512,2048]{1,0:T(8,128)}, bf16[576,2048]{1,0:T(8,128)(2,1)S(1)}, bf16[144...) custom-call(bf16[512,512]{1,0:T(8,128)(2,1)S(1)} %bitcast.80, bf16[160,512]{1,0:T(8,128)(2,1)S(1)} %copy-done.25, ...), custom_call_target="tpu_custom_call" | custom-call | tf_op jit(solution)/shard_map/pallas_call | solution.py:528
  49.5 2.1 copy-done.2
  51.6 2.0 copy-done.8
  53.6 1.4 copy-done.13
  54.9 0.8 copy-done.26
  56.4 13.9 %shard_map.179 = f32[16,128]{1,0:T(8,128)} custom-call(f32[16,128]{1,0:T(8,128)} %bitcast.89), custom_call_target="tpu_custom_call" | custom-call | tf_op jit(solution)/shard_map/pallas_call | solution.py:348
  70.3 1.3 fusion.10
  71.6 1.2 fusion.11
  74.0 2.2 copy-done.3
  76.2 1.6 copy-done.6
  77.8 3.3 %shard_map.180 = (bf16[512,2048]{1,0:T(8,128)(2,1)S(1)}, f32[512,512]{1,0:T(8,128)S(1)}, bf16[64,32,256]{2,1,0:T(8,128)(2,1)S(1)}) custom-call(f32[512,2048]{1,0:T(8,128)S(1)} %copy-done.3, f32[1,2048]{1,0:T(1,128)S(1)} %bitcast.87, bf16[512,512]{1,0:T(8,128)(2,1)S(1)} %bitcast.81, bf16[512,512]{1,0:T(8,128)(2,1)S(1)} %bitcast.83, ...), custom_call_target="tpu_custom_call" | custom-call | tf_op jit(solution)/shard_map/pallas_call | solution.py:601
  81.1 1.0 copy-done.19
  82.1 1.0 copy-done.22
  83.0 1.3 copy-done.32
  84.4 22.1 %shard_map.181.x_ref = bf16[64,32,256]{2,1,0:T(8,128)(2,1)} custom-call(bf16[64,32,256]{2,1,0:T(8,128)(2,1)} %copy-done.22), custom_call_target="tpu_custom_call" | custom-call | tf_op jit(solution)/shard_map/pallas_call | solution.py:404
  106.5 1.2 copy-done.11
  107.7 1.4 copy-done.18
  109.1 24.5 %shard_map.182 = (bf16[64,32,256]{2,1,0:T(8,128)(2,1)S(1)}, bf16[128,16,512]{2,1,0:T(8,128)(2,1)S(1)}, f32[4,64,256]{2,1,0:T(8,128)S(1)}) custom-call(bf16[64,32,256]{2,1,0:T(8,128)(2,1)S(1)} %copy-done.11, bf16[512,1536]{1,0:T(8,128)(2,1)S(1)} %copy-done.18, bf16[512,512]{1,0:T(8,128)(2,1)S(1)} %copy-done.15, f32[4,64,256]{2,1,0:T(8,128)S(1)} %reshape.236.bias_ref), custom_call_target="tpu_custom_call" | custom-call | tf_op jit(solution)/shard_map/pallas_call | solution.py:1047
  133.6 1.3 copy-done.16
  134.9 1.0 copy-done.21
  136.6 22.8 %shard_map.183.ret_ref = bf16[64,32,256]{2,1,0:T(8,128)(2,1)} custom-call(bf16[64,32,256]{2,1,0:T(8,128)(2,1)} %copy-done.21), custom_call_target="tpu_custom_call" | custom-call | tf_op jit(solution)/shard_map/pallas_call | solution.py:404
  159.4 1.6 copy-done.7
  161.0 1.2 copy-done.10
  162.2 1.2 copy-done.20
  163.5 7.1 %shard_map.184 = (bf16[512,512]{1,0:T(8,128)(2,1)}, f32[512,512]{1,0:T(8,128)S(1)}, bf16[512,512]{1,0:T(8,128)(2,1)S(1)}, f32[512,2048]{1,0:T(8,128)S(1)}, f32[16,128]{1,0:T(8,128)S(1)}) custom-call(bf16[64,32,256]{2,1,0:T(8,128)(2,1)S(1)} %copy-done.10, f32[512,512]{1,0:T(8,128)S(1)} %copy-done.20, bf16[512,512]{1,0:T(8,128)(2,1)S(1)} %bitcast.84, ...), custom_call_target="tpu_custom_call" | custom-call | tf_op jit(solution)/shard_map/pallas_call | solution.py:692
  170.6 3.0 convolution_convert_fusion
  173.6 16.5 %shard_map.185 = f32[16,128]{1,0:T(8,128)} custom-call(f32[16,128]{1,0:T(8,128)} %copy-done.30), custom_call_target="tpu_custom_call" | custom-call | tf_op jit(solution)/shard_map/pallas_call | solution.py:348
  190.8 0.9 fusion.4
  191.8 1.0 fusion.6
  192.8 4.6 %multiply_convert_fusion.premix_ref = bf16[512,2048]{1,0:T(8,128)(2,1)S(1)} fusion(f32[512,2048]{1,0:T(8,128)} %copy-done.8, f32[512,2048]{1,0:T(8,128)} %copy-done.9, f32[2048]{0:T(1024)S(1)} %broadcast_multiply_fusion.1, f32[2048]{0:T(1024)S(1)} %add_divide_fusion), kind=kLoop, calls=%fused_computation.2 | loop fusion | flops 4194304 | bytes 10502144 | tf_op jit(solution)/shard_map/convert_element_type | solution.py:1124
  197.6 1.0 copy.42
  199.9 14.6 %shard_map.186.got_ref = bf16[160,2048]{1,0:T(8,128)(2,1)} custom-call(bf16[32,2048]{1,0:T(8,128)(2,1)} %get-tuple-element.57.refs_0_, bf16[32,2048]{1,0:T(8,128)(2,1)} %get-tuple-element.56.refs_1_, bf16[16,2048]{1,0:T(8,128)(2,1)} %bitcast.97, bf16[16,2048]{1,0:T(8,128)(2,1)} %bitcast.96), custom_call_target="tpu_custom_call" | custom-call | tf_op jit(solution)/shard_map/pallas_call | solution.py:111
  214.5 1.1 copy-done.12
  215.6 27.0 %shard_map.187 = (bf16[512,512]{1,0:T(8,128)(2,1)}, bf16[128,16,512]{2,1,0:T(8,128)(2,1)}, f32[9,2048]{1,0:T(8,128)S(1)}) custom-call(bf16[512,2048]{1,0:T(8,128)(2,1)} %copy-done.34, bf16[160,2048]{1,0:T(8,128)(2,1)S(1)} %copy-done.12, bf16[576,2048]{1,0:T(8,128)(2,1)} %copy-done.13, bf16[144,2048]{1,0:T(8,128)(2,1)S(1)} %copy-done.27, ...), custom_call_target="tpu_custom_call" | custom-call | tf_op jit(solution)/shard_map/pallas_call | solution.py:833
  242.6 4.6 %pad_maximum_fusion.w_ref = bf16[64,2,48,512]{3,2,1,0:T(8,128)(2,1)} fusion(bf16[64,2,16,512]{3,2,1,0:T(8,128)(2,1)S(1)} %bitcast.85, bf16[64,2,16,512]{3,2,1,0:T(8,128)(2,1)} %bitcast.94, bf16[64,2,16,512]{3,2,1,0:T(8,128)(2,1)S(1)} %bitcast.93), kind=kLoop, calls=%fused_computation | loop fusion | flops 18874368 | bytes 12582912 | tf_op jit(solution)/shard_map/concatenate | solution.py:1140
  247.8 1.8 fusion
  249.7 2.8 copy-done.1
  252.5 63.1 %shard_map.188 = (f32[48,512]{1,0:T(8,128)S(1)}, f32[16,16,128]{2,1,0:T(8,128)S(1)}) custom-call(bf16[64,2,48,512]{3,2,1,0:T(8,128)(2,1)S(1)} %copy-done.1, f32[16,16,128]{2,1,0:T(8,128)S(1)} %bitcast.86), custom_call_target="tpu_custom_call" | custom-call | tf_op jit(solution)/shard_map/pallas_call | solution.py:260
  319.5 1.3 multiply_multiply_fusion.1
  320.8 1.1 multiply_multiply_fusion
  (97 shorter events, 10.7 us)
Async XLA Ops:
  0.6 70.9 %copy-start = (f32[2048,128]{1,0:T(8,128)S(1)}, f32[2048,128]{1,0:T(8,128)}, u32[]{:S(2)}) copy-start(f32[2048,128]{1,0:T(8,128)} %param.14) | copy-start | bytes 3145732
  0.7 7.5 %copy-start.4 = (bf16[1,16,32,512]{3,2,1,0:T(8,128)(2,1)S(1)}, bf16[1,16,32,512]{3,2,1,0:T(8,128)(2,1)}, u32[]{:S(2)}) copy-start(bf16[1,16,32,512]{3,2,1,0:T(8,128)(2,1)} %param.10) | copy-start | bytes 1572868
  0.8 2.4 copy-start.41
  5.5 67.2 %copy-start.35 = (f32[128,2048]{1,0:T(8,128)S(1)}, f32[128,2048]{1,0:T(8,128)}, u32[]{:S(2)}) copy-start(f32[128,2048]{1,0:T(8,128)} %param.15) | copy-start | bytes 3145732
  6.7 67.3 %copy-start.14 = (bf16[1,16,32,512]{3,2,1,0:T(8,128)(2,1)S(1)}, bf16[1,16,32,512]{3,2,1,0:T(8,128)(2,1)}, u32[]{:S(2)}) copy-start(bf16[1,16,32,512]{3,2,1,0:T(8,128)(2,1)} %param.11) | copy-start | bytes 1572868
  21.8 1.6 copy-start.5
  23.4 0.9 copy-start.25
  49.5 2.1 copy-start.2
  51.6 2.0 copy-start.8
  53.6 1.4 copy-start.13
  54.9 0.8 copy-start.26
  55.8 0.6 copy-start.31
  73.4 0.6 copy-start.38
  74.0 2.2 copy-start.3
  76.2 1.6 copy-start.6
  77.8 28.7 %copy-start.15 = (bf16[512,512]{1,0:T(8,128)(2,1)S(1)}, bf16[512,512]{1,0:T(8,128)(2,1)}, u32[]{:S(2)}) copy-start(bf16[512,512]{1,0:T(8,128)(2,1)} %wout_ref.3) | copy-start | bytes 1572868
  81.1 1.0 copy-start.19
  82.1 1.0 copy-start.22
  83.0 1.3 copy-start.32
  106.5 1.2 copy-start.11
  107.7 1.4 copy-start.18
  133.6 1.3 copy-start.16
  134.9 1.0 copy-start.21
  135.9 0.7 copy-start.28
  159.4 1.6 copy-start.7
  161.0 1.2 copy-start.10
  162.2 1.2 copy-start.20
  163.5 7.2 %copy-start.33 = (bf16[512,2048]{1,0:T(8,128)(2,1)S(1)}, bf16[512,2048]{1,0:T(8,128)(2,1)}, u32[]{:S(2)}) copy-start(bf16[512,2048]{1,0:T(8,128)(2,1)} %copy-done.32) | copy-start | bytes 6291460
  170.6 3.0 copy-start.9
  170.6 3.0 copy-start.23
  170.6 3.0 copy-start.30
  170.6 19.5 %copy-start.39 = (f32[1,2048]{1,0:T(1,128)S(1)}, f32[1,2048]{1,0:T(1,128)}, u32[]{:S(2)}) copy-start(f32[1,2048]{1,0:T(1,128)} %copy-done.38) | copy-start | bytes 24580
  170.6 20.2 %copy-start.36 = (f32[128,2048]{1,0:T(8,128)S(1)}, f32[128,2048]{1,0:T(8,128)}, u32[]{:S(2)}) copy-start(f32[128,2048]{1,0:T(8,128)} %param.15) | copy-start | bytes 3145732
  192.7 21.8 %copy-start.24 = (f32[512,512]{1,0:T(8,128)S(1)}, f32[512,512]{1,0:T(8,128)}, u32[]{:S(2)}) copy-start(f32[512,512]{1,0:T(8,128)} %copy-done.23) | copy-start | bytes 3145732
  192.8 21.8 %copy-start.27 = (bf16[144,2048]{1,0:T(8,128)(2,1)S(1)}, bf16[144,2048]{1,0:T(8,128)(2,1)}, u32[]{:S(2)}) copy-start(bf16[144,2048]{1,0:T(8,128)(2,1)} %copy-done.26) | copy-start | bytes 1769476
  197.4 1.9 copy-start.34
  214.5 1.1 copy-start.12
  215.6 27.0 %copy-start.17 = (bf16[128,16,512]{2,1,0:T(8,128)(2,1)S(1)}, bf16[128,16,512]{2,1,0:T(8,128)(2,1)}, u32[]{:S(2)}) copy-start(bf16[128,16,512]{2,1,0:T(8,128)(2,1)} %copy-done.16) | copy-start | bytes 6291460
  215.6 27.0 %copy-start.37 = (bf16[2048,512]{1,0:T(8,128)(2,1)S(1)}, bf16[2048,512]{1,0:T(8,128)(2,1)}, u32[]{:S(2)}) copy-start(bf16[2048,512]{1,0:T(8,128)(2,1)} %convolution_convert_fusion) | copy-start | bytes 6291460
  242.6 4.7 %copy-start.29 = (f32[4,64,256]{2,1,0:T(8,128)S(1)}, f32[4,64,256]{2,1,0:T(8,128)}, u32[]{:S(2)}) copy-start(f32[4,64,256]{2,1,0:T(8,128)} %copy-done.28) | copy-start | bytes 786436
  242.6 5.1 %copy-start.42 = (s32[4096]{0:T(1024)S(1)}, s32[4096]{0:T(1024)}, u32[]{:S(2)}) copy-start(s32[4096]{0:T(1024)} %copy-done.41) | copy-start | bytes 49156
  249.6 69.9 %copy-start.40 = (f32[2048]{0:T(1024)S(1)}, f32[2048]{0:T(1024)}, u32[]{:S(2)}) copy-start(f32[2048]{0:T(1024)} %get-tuple-element.64) | copy-start | bytes 24580
  249.7 2.8 copy-start.1
  252.5 68.3 %copy-start.43 = (f32[128]{0:T(128)S(1)}, f32[128]{0:T(128)}, u32[]{:S(2)}) copy-start(f32[128]{0:T(128)} %get-tuple-element.66) | copy-start | bytes 1540

commit v2 on v1

--- a/solution.py
+++ b/solution.py
@@ -63,10 +63,9 @@
 AXES = ("row", "col")
 
 
-def halo_kernel(rows, cols, height, width, top_ref, down_ref, left_ref, right_ref, o_ref, sems):
-    row = lax.axis_index("row")
-    col = lax.axis_index("col")
-    barrier = pltpu.get_barrier_semaphore()
+def halo_sends(rows, cols, row, col, parts, o_ref, sems):
+    top_ref, down_ref, left_ref, right_ref = parts
+    width, height = top_ref.shape[0], left_ref.shape[0]
     up, down = lax.rem(row + rows - 1, rows), lax.rem(row + 1, rows)
     left, right = lax.rem(col + cols - 1, cols), lax.rem(col + 1, cols)
     last = width - 16
@@ -80,22 +79,32 @@
         (top_ref.at[pl.ds(last, 16)], 2 * (width + height) + 32, 16, (up, right)),
         (top_ref.at[pl.ds(0, 16)], 2 * (width + height) + 48, 16, (up, left)),
     )
-    for _, _, _, device in sends:
+    copies = [
+        pltpu.make_async_remote_copy(
+            src_ref=source,
+            dst_ref=o_ref.at[pl.ds(start, size)],
+            send_sem=sems.at[0, number],
+            recv_sem=sems.at[1, number],
+            device_id=device,
+            device_id_type=MESH,
+        )
+        for number, (source, start, size, device) in enumerate(sends)
+    ]
+    return copies, [device for _, _, _, device in sends]
+
+
+def halo_kernel(rows, cols, top_ref, down_ref, left_ref, right_ref, o_ref, sems):
+    row = lax.axis_index("row")
+    col = lax.axis_index("col")
+    barrier = pltpu.get_barrier_semaphore()
+    copies, devices = halo_sends(
+        rows, cols, row, col, (top_ref, down_ref, left_ref, right_ref), o_ref, sems
+    )
+    for device in devices:
         pl.semaphore_signal(barrier, inc=1, device_id=device, device_id_type=MESH)
-    pl.semaphore_wait(barrier, len(sends))
-    copies = []
-    for number, (source, start, size, device) in enumerate(sends):
-        copies.append(
-            pltpu.make_async_remote_copy(
-                src_ref=source,
-                dst_ref=o_ref.at[pl.ds(start, size)],
-                send_sem=sems.at[0, number],
-                recv_sem=sems.at[1, number],
-                device_id=device,
-                device_id_type=MESH,
-            )
-        )
-        copies[-1].start()
+    pl.semaphore_wait(barrier, len(devices))
+    for copy in copies:
+        copy.start()
     for copy in copies:
         copy.wait()
 
@@ -106,7 +115,7 @@
     total = 2 * (width + height) + 64
 
     def body(*refs):
-        halo_kernel(rows, cols, height, width, *refs)
+        halo_kernel(rows, cols, *refs)
 
     return pl.pallas_call(
         body,
@@ -114,176 +123,249 @@
         in_specs=[pl.BlockSpec(memory_space=pltpu.VMEM)] * 4,
         out_specs=pl.BlockSpec(memory_space=pltpu.VMEM),
         scratch_shapes=[pltpu.SemaphoreType.DMA((2, 8))],
-        compiler_params=pltpu.CompilerParams(collective_id=number, has_side_effects=True),
+        compiler_params=pltpu.CompilerParams(
+            collective_id=number, has_side_effects=True, vmem_limit_bytes=60 * 1024 * 1024
+        ),
     )(cells[0], cells[-1], cells[:, 0], cells[:, -1])
 
 
-def reduce_kernel(rows, cols, w_ref, s_ref, o_ref, so_ref, half, got, rs_buf, own_buf, col_buf, sems):
+def reduce_kernel(
+    rows, cols, factor, w0_ref, w1_ref, w2_ref, s_ref, project_ref, expand_ref, qkv_ref, out_ref,
+    so_ref, half, buf1, buf2, buf3, sum1, sum2, rs_buf, own_buf, col_buf, sems, pair_sems, axis_sems
+):
     row = lax.axis_index("row")
     col = lax.axis_index("col")
-    depth = cols // 2
     core = lax.rem(col, 2)
-    count = rows * depth
-    me = row * depth + col // 2
-    steps = 4
-    span = count // steps
+    me = (row // 4, lax.rem(row, 4), col // 2)
+    w_refs = (w0_ref, w1_ref, w2_ref)
+    pair = (row, col + 1 - 2 * core)
     barrier = pltpu.get_barrier_semaphore()
-    pair = (row, col - core + (1 - core))
-
-    def place(k):
-        peer = lax.rem(me + k, count)
-        return peer, (peer // depth, lax.rem(peer, depth) * 2 + core)
-
-    def signal(device):
-        pl.semaphore_signal(barrier, inc=1, device_id=device, device_id_type=MESH)
+
+    def device(axis, place):
+        if axis == 0:
+            return (place * 4 + me[1], col)
+        if axis == 1:
+            return (me[0] * 4 + place, col)
+        return (row, place * 2 + core)
+
+    def signal(target):
+        pl.semaphore_signal(barrier, inc=1, device_id=target, device_id_type=MESH)
 
     def wait_like(ref, sem):
         pltpu.make_async_copy(ref, ref, sem).wait()
 
-    @pl.loop(1, count)
+    def send(source, target, send_sem, recv_sem, to):
+        pltpu.make_async_remote_copy(
+            src_ref=source,
+            dst_ref=target,
+            send_sem=send_sem,
+            recv_sem=recv_sem,
+            device_id=to,
+            device_id_type=MESH,
+        ).start()
+
+    signal(pair)
+    for axis in range(3):
+        for k in range(1, 4):
+            signal(device(axis, lax.rem(me[axis] + k, 4)))
+
+    @pl.loop(1, rows)
     def _(k):
-        signal(place(k)[1])
-
-    @pl.loop(0, depth)
+        signal((lax.rem(row + k, rows), col))
+
+    @pl.loop(1, cols)
     def _(k):
-        signal((row, lax.rem(col // 2 + k, depth) * 2 + (1 - core)))
+        signal((row, lax.rem(col + k, cols)))
 
     rs_buf[row] = s_ref[row]
-    pl.semaphore_wait(barrier, count - 1 + depth)
-
-    for step in range(steps):
-
-        @pl.loop(step * span, (step + 1) * span)
-        def _(k):
-            peer = lax.rem(me + k, count)
-            pltpu.make_async_remote_copy(
-                src_ref=w_ref.at[peer, 1 - core],
-                dst_ref=half.at[step, k - step * span],
-                send_sem=sems.at[0],
-                recv_sem=sems.at[1 + step],
-                device_id=pair,
-                device_id_type=MESH,
-            ).start()
+    pl.semaphore_wait(barrier, 10 + rows - 1 + cols - 1)
+
+    for p in range(3):
+        send(
+            w_refs[p].at[:, :, :, 1 - core], half.at[p], pair_sems.at[0, p], pair_sems.at[1, p], pair
+        )
 
     @pl.loop(1, rows)
     def _(k):
         other = lax.rem(row + k, rows)
-        pltpu.make_async_remote_copy(
-            src_ref=s_ref.at[other],
-            dst_ref=rs_buf.at[row],
-            send_sem=sems.at[5],
-            recv_sem=sems.at[6],
-            device_id=(other, col),
-            device_id_type=MESH,
-        ).start()
-
-    for step in range(steps):
-        wait_like(half.at[step], sems.at[1 + step])
-
-        @pl.loop(0, span)
-        def _(k):
-            peer, device = place(k + step * span)
-            mine = w_ref[peer, core].astype(jnp.float32) + half[step, k].astype(jnp.float32)
-            half[step, k] = mine.astype(jnp.bfloat16)
-
-            @pl.when(k + step * span > 0)
-            def _():
-                pltpu.make_async_remote_copy(
-                    src_ref=half.at[step, k],
-                    dst_ref=got.at[me],
-                    send_sem=sems.at[7],
-                    recv_sem=sems.at[8],
-                    device_id=device,
-                    device_id_type=MESH,
-                ).start()
-
-        if step == 0:
-            got[me] = half[0, 0]
-            wait_like(rs_buf.at[pl.ds(0, rows - 1)], sems.at[6])
-            total = rs_buf[0]
-            for k in range(1, rows):
-                total = total + rs_buf[k]
-            own_buf[...] = total
-            col_buf[col] = total
-
-            @pl.loop(1, cols)
-            def _(k):
-                pltpu.make_async_remote_copy(
-                    src_ref=own_buf,
-                    dst_ref=col_buf.at[col],
-                    send_sem=sems.at[9],
-                    recv_sem=sems.at[10],
-                    device_id=(row, lax.rem(col + k, cols)),
-                    device_id_type=MESH,
-                ).start()
-
-        if step == 2:
-            wait_like(col_buf.at[pl.ds(0, cols - 1)], sems.at[10])
-            total = col_buf[0]
-            for k in range(1, cols):
-                total = total + col_buf[k]
-            so_ref[row] = total
-
-            @pl.loop(1, rows)
-            def _(k):
-                pltpu.make_async_remote_copy(
-                    src_ref=so_ref.at[row],
-                    dst_ref=so_ref.at[row],
-                    send_sem=sems.at[11],
-                    recv_sem=sems.at[12],
-                    device_id=(lax.rem(row + k, rows), col),
-                    device_id_type=MESH,
-                ).start()
-
-    wait_like(got.at[pl.ds(0, count - 1)], sems.at[8])
-    height = o_ref.shape[0]
-    for low in range(0, height, 16):
-
-        def add(k, total):
-            return total + got[k, low : low + 16, :].astype(jnp.float32)
-
-        o_ref[low : low + 16, :] = lax.fori_loop(
-            0, count, add, jnp.zeros((16, o_ref.shape[1]), jnp.float32)
-        )
-    wait_like(so_ref.at[pl.ds(0, rows - 1)], sems.at[12])
-    wait_like(so_ref.at[pl.ds(0, rows - 1)], sems.at[11])
-    wait_like(col_buf.at[pl.ds(0, cols - 1)], sems.at[9])
-    wait_like(rs_buf.at[pl.ds(0, rows - 1)], sems.at[5])
-    wait_like(half, sems.at[0])
-    wait_like(got.at[pl.ds(0, count - 1)], sems.at[7])
-
-
-def reduce_all(parts, small, number):
+        send(s_ref.at[other], rs_buf.at[row], sems.at[0], sems.at[1], (other, col))
+
+    def at_axis(ref, axis, place):
+        if axis == 0:
+            return ref.at[place]
+        if axis == 1:
+            return ref.at[:, place]
+        return ref.at[:, :, place]
+
+    orders = ((0, 1, 2), (1, 2, 0), (2, 0, 1))
+    for p in range(3):
+        first = orders[p][0]
+        wait_like(half.at[p], pair_sems.at[1, p])
+        w_ref = w_refs[p]
+
+        @pl.loop(0, 16)
+        def _(i):
+            y, x = i // 4, lax.rem(i, 4)
+            for z in range(4):
+                mine = w_ref[y, x, z, core].astype(jnp.float32) + half[p, y, x, z].astype(jnp.float32)
+                half[p, y, x, z] = mine.astype(jnp.bfloat16)
+
+        for k in range(1, 4):
+            place = lax.rem(me[first] + k, 4)
+            send(
+                at_axis(half.at[p], first, place),
+                buf1.at[p, me[first]],
+                axis_sems.at[0, 0, p],
+                axis_sems.at[1, 0, p],
+                device(first, place),
+            )
+
+    wait_like(rs_buf.at[pl.ds(0, rows - 1)], sems.at[1])
+    total = rs_buf[0]
+    for k in range(1, rows):
+        total = total + rs_buf[k]
+    own_buf[...] = total
+    col_buf[col] = total
+
+    @pl.loop(1, cols)
+    def _(k):
+        send(own_buf, col_buf.at[col], sems.at[2], sems.at[3], (row, lax.rem(col + k, cols)))
+
+    for p in range(3):
+        first, second, third = orders[p]
+        wait_like(buf1.at[p, pl.ds(0, 3)], axis_sems.at[1, 0, p])
+        own = at_axis(half.at[p], first, me[first])
+
+        @pl.loop(0, 16)
+        def _(i):
+            u, v = i // 4, lax.rem(i, 4)
+            total = own[u, v].astype(jnp.float32)
+            for k in range(1, 4):
+                total = total + buf1[p, lax.rem(me[first] + k, 4), u, v].astype(jnp.float32)
+            sum1[p, u, v] = total.astype(jnp.bfloat16)
+
+        for k in range(1, 4):
+            place = lax.rem(me[second] + k, 4)
+            send(
+                at_axis(sum1.at[p], 0 if second < third else 1, place),
+                buf2.at[p, me[second]],
+                axis_sems.at[0, 1, p],
+                axis_sems.at[1, 1, p],
+                device(second, place),
+            )
+
+    wait_like(col_buf.at[pl.ds(0, cols - 1)], sems.at[3])
+    total = col_buf[0]
+    for k in range(1, cols):
+        total = total + col_buf[k]
+    so_ref[row] = total
+
+    @pl.loop(1, rows)
+    def _(k):
+        send(so_ref.at[row], so_ref.at[row], sems.at[4], sems.at[5], (lax.rem(row + k, rows), col))
+
+    for p in range(3):
+        first, second, third = orders[p]
+        wait_like(buf2.at[p, pl.ds(0, 3)], axis_sems.at[1, 1, p])
+        own = at_axis(sum1.at[p], 0 if second < third else 1, me[second])
+
+        @pl.loop(0, 4)
+        def _(u):
+            total = own[u].astype(jnp.float32)
+            for k in range(1, 4):
+                total = total + buf2[p, lax.rem(me[second] + k, 4), u].astype(jnp.float32)
+            sum2[p, u] = total.astype(jnp.bfloat16)
+
+        for k in range(1, 4):
+            place = lax.rem(me[third] + k, 4)
+            send(
+                sum2.at[p, place],
+                buf3.at[p, me[third]],
+                axis_sems.at[0, 2, p],
+                axis_sems.at[1, 2, p],
+                device(third, place),
+            )
+
+    for p in range(3):
+        third = orders[p][2]
+        wait_like(buf3.at[p, pl.ds(0, 3)], axis_sems.at[1, 2, p])
+        total = sum2[p, me[third]].astype(jnp.float32)
+        for k in range(1, 4):
+            total = total + buf3[p, lax.rem(me[third] + k, 4)].astype(jnp.float32)
+        total = total * factor
+        if p == 0:
+            project_ref[...] = total
+        elif p == 1:
+            for q in range(4):
+                expand_ref[:, q * 512 : (q + 1) * 512] = total[q * 4 : (q + 1) * 4]
+        else:
+            for q in range(3):
+                qkv_ref[:, q * 512 : (q + 1) * 512] = total[q * 4 : (q + 1) * 4]
+            out_ref[...] = total[12:16]
+
+    wait_like(so_ref.at[pl.ds(0, rows - 1)], sems.at[5])
+    wait_like(so_ref.at[pl.ds(0, rows - 1)], sems.at[4])
+    wait_like(col_buf.at[pl.ds(0, cols - 1)], sems.at[2])
+    wait_like(rs_buf.at[pl.ds(0, rows - 1)], sems.at[0])
+    for p in range(3):
+        wait_like(half.at[p], pair_sems.at[0, p])
+        wait_like(buf1.at[p, pl.ds(0, 3)], axis_sems.at[0, 0, p])
+        wait_like(buf2.at[p, pl.ds(0, 3)], axis_sems.at[0, 1, p])
+        wait_like(buf3.at[p, pl.ds(0, 3)], axis_sems.at[0, 2, p])
+
+
+def reduce_all(parts, small, factor, number):
     rows, cols = lax.axis_size("row"), lax.axis_size("col")
-    count, _, height, width = parts.shape
     block = small.shape[1:]
+    chunk = parts[0].shape[1:]
+    vmem = pl.BlockSpec(memory_space=pltpu.VMEM)
+
+    def held(*lead):
+        return pltpu.VMEM((3,) + lead + chunk, jnp.bfloat16)
+
     return pl.pallas_call(
-        functools.partial(reduce_kernel, rows, cols),
+        functools.partial(reduce_kernel, rows, cols, factor),
         out_shape=(
-            jax.ShapeDtypeStruct((height, width), jnp.float32),
+            jax.ShapeDtypeStruct((16, 512), jnp.float32),
+            jax.ShapeDtypeStruct((4, 2048), jnp.float32),
+            jax.ShapeDtypeStruct((4, 1536), jnp.float32),
+            jax.ShapeDtypeStruct((4, 512), jnp.float32),
             jax.ShapeDtypeStruct(small.shape, jnp.float32),
         ),
-        in_specs=[pl.BlockSpec(memory_space=pltpu.VMEM)] * 2,
-        out_specs=[pl.BlockSpec(memory_space=pltpu.VMEM)] * 2,
+        in_specs=[vmem] * 4,
+        out_specs=[vmem] * 5,
         scratch_shapes=[
-            pltpu.VMEM((4, count // 4, height, width), jnp.bfloat16),
-            pltpu.VMEM((count, height, width), jnp.bfloat16),
+            held(4, 4, 4),
+            held(4, 4, 4),
+            held(4, 4),
+            held(4),
+            held(4, 4),
+            held(4),
             pltpu.VMEM(small.shape, jnp.float32),
             pltpu.VMEM(block, jnp.float32),
             pltpu.VMEM((cols,) + block, jnp.float32),
-            pltpu.SemaphoreType.DMA((13,)),
+            pltpu.SemaphoreType.DMA((6,)),
+            pltpu.SemaphoreType.DMA((2, 3)),
+            pltpu.SemaphoreType.DMA((2, 3, 3)),
         ],
         compiler_params=pltpu.CompilerParams(
-            collective_id=number, has_side_effects=True, vmem_limit_bytes=40 * 1024 * 1024
+            collective_id=number, has_side_effects=True, vmem_limit_bytes=60 * 1024 * 1024
         ),
-    )(parts, small)
-
-
-def small_sum_kernel(rows, cols, x_ref, o_ref, row_buf, sum_buf, col_buf, sems):
+    )(*(part.reshape((4, 4, 4, 2) + chunk) for part in parts), small)
+
+
+def sum_halo_kernel(
+    rows, cols, x_ref, edge_ref, o_ref, got_ref, row_buf, sum_buf, col_buf, sems, halo_sems
+):
     row = lax.axis_index("row")
     col = lax.axis_index("col")
     barrier = pltpu.get_barrier_semaphore()
 
+    parts = [edge_ref.at[pl.ds(low, size)] for low, size in ((0, 32), (32, 32), (64, 16), (80, 16))]
+    copies, devices = halo_sends(rows, cols, row, col, parts, got_ref, halo_sems)
+    for device in devices:
+        pl.semaphore_signal(barrier, inc=1, device_id=device, device_id_type=MESH)
+
     def row_peer(k):
         return lax.rem(row + k, rows)
 
@@ -299,7 +381,7 @@
         pl.semaphore_signal(barrier, inc=1, device_id=(row, col_peer(k)), device_id_type=MESH)
 
     row_buf[row] = x_ref[...]
-    pl.semaphore_wait(barrier, rows + cols - 2)
+    pl.semaphore_wait(barrier, rows + cols - 2 + len(devices))
 
     @pl.loop(1, rows)
     def _(k):
@@ -312,6 +394,8 @@
             device_id_type=MESH,
         ).start()
 
+    for copy in copies:
+        copy.start()
     arrived = row_buf.at[pl.ds(0, rows - 1)]
     pltpu.make_async_copy(arrived, arrived, sems.at[1]).wait()
     total = row_buf[0]
@@ -339,25 +423,34 @@
     o_ref[...] = total
     pltpu.make_async_copy(arrived, arrived, sems.at[0]).wait()
     pltpu.make_async_copy(other, other, sems.at[2]).wait()
-
-
-def small_sum(values, number):
+    for copy in copies:
+        copy.wait()
+
+
+def sum_and_halo(values, edges, number):
     rows = lax.axis_size("row")
     cols = lax.axis_size("col")
     shape = values.shape
+    vmem = pl.BlockSpec(memory_space=pltpu.VMEM)
     return pl.pallas_call(
-        functools.partial(small_sum_kernel, rows, cols),
-        out_shape=jax.ShapeDtypeStruct(shape, jnp.float32),
-        in_specs=[pl.BlockSpec(memory_space=pltpu.VMEM)],
-        out_specs=pl.BlockSpec(memory_space=pltpu.VMEM),
+        functools.partial(sum_halo_kernel, rows, cols),
+        out_shape=(
+            jax.ShapeDtypeStruct(shape, jnp.float32),
+            jax.ShapeDtypeStruct((edges.shape[0] + 64, edges.shape[1]), edges.dtype),
+        ),
+        in_specs=[vmem, vmem],
+        out_specs=[vmem, vmem],
         scratch_shapes=[
             pltpu.VMEM((rows,) + shape, jnp.float32),
             pltpu.VMEM(shape, jnp.float32),
             pltpu.VMEM((cols,) + shape, jnp.float32),
             pltpu.SemaphoreType.DMA((4,)),
+            pltpu.SemaphoreType.DMA((2, 8)),
         ],
-        compiler_params=pltpu.CompilerParams(collective_id=number, has_side_effects=True),
-    )(values)
+        compiler_params=pltpu.CompilerParams(
+            collective_id=number, has_side_effects=True, vmem_limit_bytes=60 * 1024 * 1024
+        ),
+    )(values, edges)
 
 
 def swap_kernel(parity, side, cols, x_ref, o_ref, sems):
@@ -407,7 +500,9 @@
         in_specs=[pl.BlockSpec(memory_space=pltpu.VMEM)],
         out_specs=pl.BlockSpec(memory_space=pltpu.VMEM),
         scratch_shapes=[pltpu.SemaphoreType.DMA((3,))],
-        compiler_params=pltpu.CompilerParams(collective_id=number, has_side_effects=True),
+        compiler_params=pltpu.CompilerParams(
+            collective_id=number, has_side_effects=True, vmem_limit_bytes=60 * 1024 * 1024
+        ),
     )(parts)
 
 
@@ -415,6 +510,7 @@
 COLS = 32
 MAIN = (ROWS + 2) * COLS
 SIDE = (ROWS + 2) * 8
+EDGE = 2 * (ROWS + COLS)
 
 
 def edge_masks():
@@ -445,7 +541,7 @@
 
 def expand_kernel(
     x_ref, got_ref, w_ref, taps_ref, mixed_ref, slope_mix_ref, slope_ref, main_ref, side_out_ref,
-    pooled_ref, normed, normed_side, side, pre, pre_side, padded
+    pooled_ref, edge_ref, normed, normed_side, side, pre, pre_side, padded, ends
 ):
     step = pl.program_id(0)
 
@@ -504,9 +600,16 @@
         rows = pl.ds(pl.multiple_of(y * COLS, COLS), COLS)
         mixed_ref[rows, :] = mixed
         slope_mix_ref[rows, :] = slope
+        ends[0, pl.ds(y, 1), :] = slope[0:1]
+        ends[1, pl.ds(y, 1), :] = slope[COLS - 1 : COLS]
         return total + jnp.sum(mixed.reshape(COLS // 8, 8, width), axis=0)
 
     total = lax.fori_loop(0, ROWS, mix, jnp.zeros((8, width), jnp.float32))
+    tokens = ROWS * COLS
+    edge_ref[0:COLS, :] = slope_mix_ref[0:COLS, :].astype(jnp.bfloat16)
+    edge_ref[COLS : 2 * COLS, :] = slope_mix_ref[tokens - COLS : tokens, :].astype(jnp.bfloat16)
+    edge_ref[2 * COLS : 2 * COLS + ROWS, :] = ends[0].astype(jnp.bfloat16)
+    edge_ref[2 * COLS + ROWS : EDGE, :] = ends[1].astype(jnp.bfloat16)
     total = jnp.sum(total, axis=0, keepdims=True)
     for tile in range(width // 128):
         pooled_ref[0, tile : tile + 1, :] = total[:, tile * 128 : (tile + 1) * 128]
@@ -535,6 +638,7 @@
             jax.ShapeDtypeStruct((MAIN, hidden), jnp.bfloat16),
             jax.ShapeDtypeStruct((SIDE, hidden), jnp.bfloat16),
             jax.ShapeDtypeStruct((steps, width // 128, 128), jnp.float32),
+            jax.ShapeDtypeStruct((EDGE, hidden), jnp.bfloat16),
         ),
         in_specs=[fixed(tokens_in.shape), fixed(got.shape), moving(channels), moving(9)],
         out_specs=[
@@ -544,6 +648,7 @@
             moving(MAIN),
             moving(SIDE),
             pl.BlockSpec((1, width // 128, 128), lambda e: (e, 0, 0)),
+            moving(EDGE),
         ],
         scratch_shapes=[
             pltpu.VMEM((MAIN, channels), jnp.bfloat16),
@@ -552,8 +657,9 @@
             pltpu.VMEM((MAIN, width), jnp.float32),
             pltpu.VMEM((SIDE, width), jnp.float32),
             pltpu.VMEM((ROWS + 2, COLS + 16, width), jnp.float32),
+            pltpu.VMEM((2, ROWS, width), jnp.float32),
         ],
-        compiler_params=pltpu.CompilerParams(vmem_limit_bytes=40 * 1024 * 1024),
+        compiler_params=pltpu.CompilerParams(vmem_limit_bytes=60 * 1024 * 1024),
     )(tokens_in, got, w_expand, taps)
 
 
@@ -622,13 +728,13 @@
             pltpu.VMEM((4, height, 128), jnp.float32),
             pltpu.VMEM((2, 256, 128), jnp.float32),
         ],
-        compiler_params=pltpu.CompilerParams(vmem_limit_bytes=40 * 1024 * 1024),
+        compiler_params=pltpu.CompilerParams(vmem_limit_bytes=60 * 1024 * 1024),
     )(mixed, gate, tokens_in, cotangent, w_project)
 
 
 def middle_kernel(
     ret_ref, middle_ref, cot_ref, mixed_ref, wout_ref, wproj_ref, out_ref, grad_ref, grad_b_ref,
-    scaled_grad_ref, gate_ref, flat, packed, total
+    scaled_grad_ref, gate_ref, edge_ref, flat, packed, total, ends
 ):
     step = pl.program_id(0)
 
@@ -656,10 +762,16 @@
     grad_ref[...] = grad
     grad_b = grad.astype(jnp.bfloat16)
     grad_b_ref[...] = grad_b
+    height = grad.shape[0]
+    lines = height // COLS
+    for k in range(lines):
+        ends[0, pl.ds(step * lines + k, 1), :] = grad[k * COLS : k * COLS + 1]
+        ends[1, pl.ds(step * lines + k, 1), :] = grad[(k + 1) * COLS - 1 : (k + 1) * COLS]
 
     @pl.when(step == 0)
     def _():
         total[...] = jnp.zeros_like(total)
+        edge_ref[0:COLS, :] = grad_b[0:COLS]
 
     hidden = wproj_ref.shape[0]
     for low in range(0, hidden, 512):
@@ -672,6 +784,9 @@
 
     @pl.when(step == pl.num_programs(0) - 1)
     def _():
+        edge_ref[COLS : 2 * COLS, :] = grad_b[height - COLS : height]
+        edge_ref[2 * COLS : 2 * COLS + ROWS, :] = ends[0].astype(jnp.bfloat16)
+        edge_ref[2 * COLS + ROWS : EDGE, :] = ends[1].astype(jnp.bfloat16)
         for tile in range(hidden // 128):
             gate_ref[tile : tile + 1, :] = jnp.sum(
                 total[:, tile * 128 : (tile + 1) * 128], axis=0, keepdims=True
@@ -698,6 +813,7 @@
             jax.ShapeDtypeStruct((tokens, channels), jnp.bfloat16),
             jax.ShapeDtypeStruct((tokens, hidden), jnp.float32),
             jax.ShapeDtypeStruct((hidden // 128, 128), jnp.float32),
+            jax.ShapeDtypeStruct((EDGE, channels), jnp.bfloat16),
         ),
         in_specs=[
             pl.BlockSpec((16, 32, channels // 2), lambda t: (t, 0, 0)),
@@ -713,13 +829,15 @@
             moving(channels),
             moving(hidden),
             fixed((hidden // 128, 128)),
+            fixed((EDGE, channels)),
         ],
         scratch_shapes=[
             pltpu.VMEM((4, height, 128), jnp.float32),
             pltpu.VMEM((2, 256, 128), jnp.float32),
             pltpu.VMEM((8, hidden), jnp.float32),
+            pltpu.VMEM((2, ROWS, channels), jnp.float32),
         ],
-        compiler_params=pltpu.CompilerParams(vmem_limit_bytes=40 * 1024 * 1024),
+        compiler_params=pltpu.CompilerParams(vmem_limit_bytes=60 * 1024 * 1024),
     )(returned, middle, cotangent, mixed, w_out, w_project)
 
 
@@ -734,8 +852,9 @@
 
 
 def back_kernel(
-    premix_ref, got_ref, main_ref, side_in_ref, slope_ref, w_ref, taps_ref, x_ref, grad_ref,
-    out_ref, parts_ref, terms_ref, turned, side, padded, expanded, preexp, total, flat, place
+    scaled_grad_ref, slope_mix_ref, slope_got_ref, grad_got_ref, gate_ref, pooled_ref, project_ref,
+    main_ref, side_in_ref, slope_ref, w_ref, taps_ref, x_ref, grad_ref,
+    out_ref, parts_ref, terms_ref, got_ref, turned, side, padded, expanded, preexp, total, flat, place
 ):
     step = pl.program_id(0)
     last = pl.num_programs(0) - 1
@@ -746,6 +865,16 @@
         total[...] = jnp.zeros_like(total)
         turned[...] = layer_normalize(x_ref[...])[0].T.astype(jnp.bfloat16)
 
+    def premix(scaled_grad, slope):
+        grads = (scaled_grad * gate_ref[...] + pooled_ref[...]) * slope
+        return grads.astype(jnp.bfloat16).astype(jnp.float32)
+
+    got_ref[...] = premix(
+        lax.dot_general(
+            grad_got_ref[...], project_ref[...], BACKWARD, preferred_element_type=jnp.float32
+        ),
+        slope_got_ref[...].astype(jnp.float32),
+    )
     masks = edge_masks()
     fill_sides(got_ref, side, masks, 4)
     padded[0, 8 : 8 + COLS, :] = got_ref[0:COLS, :].astype(jnp.float32) * masks[0]
@@ -754,7 +883,7 @@
     @pl.loop(0, ROWS)
     def _(y):
         rows = pl.ds(pl.multiple_of(y * COLS, COLS), COLS)
-        padded[y + 1, 8 : 8 + COLS, :] = premix_ref[rows, :].astype(jnp.float32)
+        padded[y + 1, 8 : 8 + COLS, :] = premix(scaled_grad_ref[rows, :], slope_mix_ref[rows, :])
 
     pairs = (ROWS + 2) // 2
 
@@ -819,8 +948,11 @@
             ).astype(jnp.bfloat16)
 
 
-def mix_backward(premix, got, main, side, slope, w_expand, taps, tokens_in, grad):
-    tokens, hidden = premix.shape
+def mix_backward(
+    scaled_grad, slope_mix, slope_got, grad_got, gate, pooled_grad, w_project, main, side, slope,
+    w_expand, taps, tokens_in, grad
+):
+    tokens, hidden = scaled_grad.shape
     channels = w_expand.shape[0]
     width = 512
 
@@ -840,7 +972,12 @@
         ),
         in_specs=[
             moving(tokens),
-            moving(got.shape[0]),
+            moving(tokens),
+            moving(slope_got.shape[0]),
+            fixed(grad_got.shape),
+            moving(1),
+            moving(1),
+            pl.BlockSpec((width, channels), lambda e: (e, 0)),
             moving(MAIN),
             moving(SIDE),
             moving(tokens),
@@ -851,6 +988,7 @@
         ],
         out_specs=[fixed((tokens, channels)), fixed((128, 16, width)), moving(9)],
         scratch_shapes=[
+            pltpu.VMEM(slope_got.shape[:1] + (width,), jnp.float32),
             pltpu.VMEM((channels, tokens), jnp.bfloat16),
             pltpu.VMEM((4, SIDE, 128), jnp.float32),
             pltpu.VMEM((ROWS + 2, COLS + 16, width), jnp.float32),
@@ -860,8 +998,11 @@
             pltpu.VMEM((4, tokens, 128), jnp.float32),
             pltpu.VMEM((4, 2048, 128), jnp.float32),
         ],
-        compiler_params=pltpu.CompilerParams(vmem_limit_bytes=50 * 1024 * 1024),
-    )(premix, got, main, side, slope, w_expand, taps, tokens_in, grad)
+        compiler_params=pltpu.CompilerParams(vmem_limit_bytes=60 * 1024 * 1024),
+    )(
+        scaled_grad, slope_mix, slope_got, grad_got, gate, pooled_grad, w_project, main, side, slope,
+        w_expand, taps, tokens_in, grad
+    )
 
 
 HEAD_DIM = 32
@@ -1060,7 +1201,7 @@
             pltpu.VMEM((4, tokens, 128), jnp.float32),
             pltpu.VMEM((4, 2048, 128), jnp.float32),
         ],
-        compiler_params=pltpu.CompilerParams(vmem_limit_bytes=40 * 1024 * 1024),
+        compiler_params=pltpu.CompilerParams(vmem_limit_bytes=60 * 1024 * 1024),
     )(blocks, w_qkv, w_out, bias)
 
 
@@ -1086,10 +1227,11 @@
     flat_inputs = inputs.reshape(tokens, channels)
     flattened_cotangent = out_grad.reshape(tokens, channels)
     taps = dw_kernel.reshape(9, hidden_units)
-    mixed, slope_mix, slope_expand, main, side, pooled = expand_and_mix(
+    mixed, slope_mix, slope_expand, main, side, pooled, slope_edges = expand_and_mix(
         flat_inputs, halo(inputs[0], 5), w_expand, taps
     )
-    pooled = small_sum(pooled.reshape(-1, 128), 3).reshape(images, -1) / cells
+    pooled, slope_got = sum_and_halo(pooled.reshape(-1, 128), slope_edges, 3)
+    pooled = pooled.reshape(images, -1) / cells
     squeeze_pre = jnp.dot(pooled, se_reduce, precision=HIGHEST)
     squeeze_sig = jax.nn.sigmoid(squeeze_pre)
     squeezed = squeeze_pre * squeeze_sig
@@ -1106,10 +1248,11 @@
         BACKWARD,
         precision=HIGHEST,
     )
-    block_out, middle_gradient, middle_b, scaled_grad, gate_grad = middle_backward(
+    block_out, middle_gradient, middle_b, scaled_grad, gate_grad, grad_edges = middle_backward(
         swap(returned, 2), middle_activation, flattened_cotangent, mixed, w_out, w_project
     )
-    gate_grad = small_sum(gate_grad, 4).reshape(images, -1)
+    gate_grad, grad_got = sum_and_halo(gate_grad, grad_edges, 4)
+    gate_grad = gate_grad.reshape(images, -1)
     project_parts = (
         lax.dot_general(scaled, middle_b, CONTRACT, preferred_element_type=jnp.float32)
         .astype(jnp.bfloat16)
@@ -1121,10 +1264,14 @@
     pooled_grad = lax.dot_general(squeeze_grad, se_reduce, BACKWARD, precision=HIGHEST)
     se_reduce_grad = lax.dot_general(pooled, squeeze_grad, CONTRACT, precision=HIGHEST) * factor
     se_expand_grad = lax.dot_general(squeezed, excite_grad, CONTRACT, precision=HIGHEST) * factor
-    premix_grad = ((scaled_grad * gate + pooled_grad / cells) * slope_mix).astype(jnp.bfloat16)
     input_gradient, expand_parts, kernel_part = mix_backward(
-        premix_grad,
-        halo(premix_grad.reshape(tile_rows, tile_cols, hidden_units), 6),
+        scaled_grad,
+        slope_mix,
+        slope_got,
+        grad_got,
+        gate,
+        pooled_grad / cells,
+        w_project,
         main,
         side,
         slope_expand,
@@ -1137,17 +1284,9 @@
     unit = lax.axis_size("row") * 1024
     room = -small.shape[0] % unit
     small = jnp.pad(small, (0, room)).reshape(lax.axis_size("row"), -1, 128)
-    parts = jnp.concatenate([project_parts, expand_parts, attention_parts], axis=1)
-    summed, small = reduce_all(parts.reshape(64, 2, 48, channels), small, 7)
-    summed = summed * factor
-    project_grad = summed[:16]
-
-    def from_blocks(blocks):
-        return blocks.reshape(-1, 4, channels).transpose(1, 0, 2).reshape(4, -1)
-
-    expand_grad = from_blocks(summed[16:32])
-    qkv_grad = from_blocks(summed[32:44])
-    out_proj_grad = summed[44:48]
+    project_grad, expand_grad, qkv_grad, out_proj_grad, small = reduce_all(
+        (project_parts, expand_parts, attention_parts), small, factor, 7
+    )
     small = small.reshape(-1)
     kernel_size = kernel_part.size
     kernel_sum = small[:kernel_size].reshape(dw_kernel.shape)

time: 327 us -> 265 us (0.81); the launches traced: 322 us -> 264 us
  local copies, waits for them, and re-layouts: 43.7 us -> 11 us
  Pallas kernels: 253 us -> 233 us
  other arithmetic: 13.7 us -> 7.45 us
    unnamed x91 -> x21, local copies, waits for them, and re-layouts: 32.5 us -> 2.78 us
    pallas_call x3, Pallas kernels: 93.5 us -> 71.5 us  [the longest x1 38.1 us: reduce_all(): pl.pallas_call(functools.partial(reduce_kernel, rows, cols, factor), out_...]
    pallas_call x2 -> x1, Pallas kernels: 27.3 us -> 12.7 us  [halo(): pl.pallas_call(body, out_shape=jax.ShapeDtypeStruct((total, features), ce...]
    concatenate x1 -> x0, other arithmetic: 4.61 us -> none  [on_device(): jnp.concatenate([project_parts, expand_parts, attention_parts], axis=1)]
    convert_element_type x1 -> x0, other arithmetic: 4.59 us -> none  [on_device(): ((scaled_grad * gate + pooled_grad / cells) * slope_mix).astype(jnp.bfloa...]
    pallas_call x1, Pallas kernels: 27 us -> 31 us  [mix_backward(): pl.pallas_call(back_kernel, grid=(hidden // width,), out_shape=(jax.Shape...]
    pallas_call x1, Pallas kernels: 3.32 us -> 6.99 us  [project(): pl.pallas_call(project_kernel, grid=(tokens // height,), out_shape=(jax.S...]
    pallas_call x1, Pallas kernels: 24.5 us -> 27.9 us  [attention(): pl.pallas_call(attention_kernel, out_shape=shapes, in_specs=[pl.BlockSpec...]
where the time goes in v2:
time: 265 us; the launch traced here: 264 us
  Pallas kernels  233 us (88%)
  matrix products  11.3 us (4%)
  local copies, waits for them, and re-layouts  11 us (4%)
  other arithmetic  7.45 us (3%)
    pallas_call x2, Pallas kernels, swap(): pl.pallas_call(functools.partial(swap_kernel, parity, GRID, lax.axis_size...  47.2 us
    pallas_call x1, Pallas kernels, reduce_all(): pl.pallas_call(functools.partial(reduce_kernel, rows, cols, factor), out_...  38.1 us
    pallas_call x2, Pallas kernels, sum_and_halo(): pl.pallas_call(functools.partial(sum_halo_kernel, rows, cols), out_shape=...  33.4 us
    pallas_call x1, Pallas kernels, mix_backward(): pl.pallas_call(back_kernel, grid=(hidden // width,), out_shape=(jax.Shape...  31 us
    pallas_call x1, Pallas kernels, attention(): pl.pallas_call(attention_kernel, out_shape=shapes, in_specs=[pl.BlockSpec...  27.9 us
    pallas_call x1, Pallas kernels, expand_and_mix(): pl.pallas_call(expand_kernel, grid=(steps,), out_shape=(wide, wide, wide,...  26.5 us
    pallas_call x1, Pallas kernels, halo(): pl.pallas_call(body, out_shape=jax.ShapeDtypeStruct((total, features), ce...  12.7 us
    pallas_call x1, Pallas kernels, middle_backward(): pl.pallas_call(middle_kernel, grid=(tokens // height,), out_shape=(jax.Sh...  9.59 us

profile of v2, /device:TPU:0, one launch (start us, length us, event | category | flops | bytes accessed | tf_op | source)
XLA Modules:
  0.0 264.0 jit_solution(3446040620164091161)
XLA Ops:
  0.6 0.0 copy-start
  0.7 0.1 subtract_add_fusion
  0.8 0.1 reshape.229
  0.8 1.5 slice_bitcast_fusion
  2.3 1.6 reshape.211.taps_ref
  3.9 2.0 convolution_bitcast_fusion
  6.0 0.2 reshape.214
  6.2 0.3 copy.29
  6.5 1.0 reshape.215.bias_ref
  7.6 0.3 copy.30
  7.9 0.6 slice_bitcast_fusion.2
  8.5 12.7 %shard_map.177.got_ref = bf16[160,512]{1,0:T(8,128)(2,1)} custom-call(bf16[32,512]{1,0:T(8,128)(2,1)} %get-tuple-element.75.refs_0_, bf16[32,512]{1,0:T(8,128)(2,1)} %get-tuple-element.74.refs_1_, bf16[16,512]{1,0:T(8,128)(2,1)} %get-tuple-element.73.refs_2_, bf16[16,512]{1,0:T(8,128)(2,1)} %get-tuple-element.72.refs_3_), custom_call_target="tpu_custom_call" | custom-call | tf_op jit(solution)/shard_map/pallas_call | solution.py:120
  21.2 26.5 %shard_map.178 = (f32[512,2048]{1,0:T(8,128)}, f32[512,2048]{1,0:T(8,128)}, f32[512,2048]{1,0:T(8,128)}, bf16[576,2048]{1,0:T(8,128)(2,1)}, bf16[144,2048]{1,0:T...) custom-call(bf16[512,512]{1,0:T(8,128)(2,1)} %bitcast.68, bf16[160,512]{1,0:T(8,128)(2,1)} %shard_map.177.got_ref, ...), custom_call_target="tpu_custom_call" | custom-call | tf_op jit(solution)/shard_map/pallas_call | solution.py:631
  47.7 16.3 %shard_map.179 = (f32[16,128]{1,0:T(8,128)}, bf16[160,2048]{1,0:T(8,128)(2,1)}) custom-call(f32[16,128]{1,0:T(8,128)} %bitcast.89, bf16[96,2048]{1,0:T(8,128)(2,1)} %get-tuple-element.43.edge_ref), custom_call_target="tpu_custom_call" | custom-call | tf_op jit(solution)/shard_map/pallas_call | solution.py:435
  64.0 0.7 fusion.10
  64.7 0.6 fusion.11
  65.3 0.6 fusion.8
  65.9 0.6 add_divide_fusion
  66.5 7.0 %shard_map.180 = (bf16[512,2048]{1,0:T(8,128)(2,1)}, f32[512,512]{1,0:T(8,128)}, bf16[64,32,256]{2,1,0:T(8,128)(2,1)}) custom-call(f32[512,2048]{1,0:T(8,128)} %get-tuple-element.41.mixed_ref, f32[1,2048]{1,0:T(1,128)} %bitcast.83, bf16[512,512]{1,0:T(8,128)(2,1)} %bitcast.69, bf16[512,512]{1,0:T(8,128)(2,1)} %bitcast.74, bf16[2048,512]{1,0:T(8,128)(2,1)} %project_ref.1), custom_call_target="tpu_custom_call" | custom-call | tf_op jit(solution)/shard_map/pallas_call | solution.py:707
  73.5 24.7 %shard_map.181.x_ref = bf16[64,32,256]{2,1,0:T(8,128)(2,1)} custom-call(bf16[64,32,256]{2,1,0:T(8,128)(2,1)} %get-tuple-element.45.x_ref), custom_call_target="tpu_custom_call" | custom-call | tf_op jit(solution)/shard_map/pallas_call | solution.py:497
  98.2 27.9 %shard_map.182 = (bf16[64,32,256]{2,1,0:T(8,128)(2,1)}, bf16[128,16,512]{2,1,0:T(8,128)(2,1)}, f32[4,64,256]{2,1,0:T(8,128)}) custom-call(bf16[64,32,256]{2,1,0:T(8,128)(2,1)} %shard_map.181.x_ref, bf16[512,1536]{1,0:T(8,128)(2,1)} %wqkv_ref.1, bf16[512,512]{1,0:T(8,128)(2,1)} %wout_ref.3, f32[4,64,256]{2,1,0:T(8,128)} %reshape.215.bias_ref), custom_call_target="tpu_custom_call" | custom-call | tf_op jit(solution)/shard_map/pallas_call | solution.py:1188
  126.1 22.5 %shard_map.183.ret_ref = bf16[64,32,256]{2,1,0:T(8,128)(2,1)} custom-call(bf16[64,32,256]{2,1,0:T(8,128)(2,1)} %get-tuple-element.46.x_ref), custom_call_target="tpu_custom_call" | custom-call | tf_op jit(solution)/shard_map/pallas_call | solution.py:497
  148.6 9.6 %shard_map.184 = (bf16[512,512]{1,0:T(8,128)(2,1)}, f32[512,512]{1,0:T(8,128)}, bf16[512,512]{1,0:T(8,128)(2,1)}, f32[512,2048]{1,0:T(8,128)}, f32[16,128]{1,0:T(8,128)}, /*index=5*/bf16[96,512]{1,0:T(8,128)(2,1)}) custom-call(bf16[64,32,256]{2,1,0:T(8,128)(2,1)} %shard_map.183.ret_ref, f32[512,512]{1,0:T(8,128)} %get-tuple-element.47.middle_ref, ...), custom_call_target="tpu_custom_call" | custom-call | tf_op jit(solution)/shard_map/pallas_call | solution.py:807
  158.2 4.4 %convolution_convert_fusion = bf16[2048,512]{1,0:T(8,128)(2,1)} fusion(bf16[512,2048]{1,0:T(8,128)(2,1)} %get-tuple-element.61, bf16[512,512]{1,0:T(8,128)(2,1)} %get-tuple-element.62), kind=kOutput, calls=%fused_computation.3 | convolution fusion | flops 1074790400 | bytes 4718592 | tf_op jit(solution)/shard_map/dot_general | solution.py:1257
  162.5 17.1 %shard_map.185 = (f32[16,128]{1,0:T(8,128)}, bf16[160,512]{1,0:T(8,128)(2,1)}) custom-call(f32[16,128]{1,0:T(8,128)} %get-tuple-element.52.x_ref, bf16[96,512]{1,0:T(8,128)(2,1)} %get-tuple-element.53.edge_ref), custom_call_target="tpu_custom_call" | custom-call | tf_op jit(solution)/shard_map/pallas_call | solution.py:435
  179.7 0.7 fusion.5
  180.4 0.9 fusion.4
  181.3 1.0 fusion.6
  182.3 0.6 broadcast_multiply_fusion
  182.9 31.0 %shard_map.186 = (bf16[512,512]{1,0:T(8,128)(2,1)}, bf16[128,16,512]{2,1,0:T(8,128)(2,1)}, f32[9,2048]{1,0:T(8,128)}) custom-call(f32[512,2048]{1,0:T(8,128)} %get-tuple-element.49.scaled_grad_ref, f32[512,2048]{1,0:T(8,128)} %get-tuple-element.50.slope_mix_ref, bf16[160,2048]{1,0:T(8,128)(2,1)} %get-tuple-element.51.slope_got_ref, ...), custom_call_target="tpu_custom_call" | custom-call | tf_op jit(solution)/shard_map/pallas_call | solution.py:965
  213.9 0.9 reshape.221
  214.9 0.2 reshape.222
  215.1 0.1 copy.28
  215.2 0.2 reshape.223
  215.4 1.8 fusion
  217.2 0.1 reshape.224
  217.3 0.7 select_maximum_fusion
  218.0 38.1 %shard_map.187 = (f32[16,512]{1,0:T(8,128)}, f32[4,2048]{1,0:T(4,128)}, f32[4,1536]{1,0:T(4,128)}, f32[4,512]{1,0:T(4,128)}, f32[16,16,128]{2,1,0:T(8,128)}) custom-call(bf16[4,4,4,2,16,512]{5,4,3,2,1,0:T(8,128)(2,1)} %bitcast.72, bf16[4,4,4,2,16,512]{5,4,3,2,1,0:T(8,128)(2,1)} %bitcast.73, bf16[4,4,4,2,16,512]{5,4,3,2,1,0:T(8,128)(2,1)} %bitcast.71, ...), custom_call_target="tpu_custom_call" | custom-call | tf_op jit(solution)/shard_map/pallas_call | solution.py:326
  256.1 0.7 slice_multiply_fusion.1
  256.9 0.7 mul.84
  257.6 0.9 slice_multiply_fusion
  258.4 0.7 mul.77
  259.1 1.3 multiply_multiply_fusion.1
  260.4 1.1 multiply_multiply_fusion
  261.5 0.6 copy.35
  262.2 0.6 copy.36
  262.8 0.6 copy.37
  263.4 0.6 copy.38
  (16 shorter events, 0.0 us)
Async XLA Ops:
  0.6 64.0 %copy-start = (f32[2048,128]{1,0:T(8,128)S(1)}, f32[2048,128]{1,0:T(8,128)}, u32[]{:S(2)}) copy-start(f32[2048,128]{1,0:T(8,128)} %param.14) | copy-start | bytes 3145732
  0.7 6.9 %copy-start.1 = (bf16[1,16,32,512]{3,2,1,0:T(8,128)(2,1)S(1)}, bf16[1,16,32,512]{3,2,1,0:T(8,128)(2,1)}, u32[]{:S(2)}) copy-start(bf16[1,16,32,512]{3,2,1,0:T(8,128)(2,1)} %param.10) | copy-start | bytes 1572868
  21.2 44.1 %copy-start.2 = (f32[128,2048]{1,0:T(8,128)S(1)}, f32[128,2048]{1,0:T(8,128)}, u32[]{:S(2)}) copy-start(f32[128,2048]{1,0:T(8,128)} %param.15) | copy-start | bytes 3145732
  182.9 32.0 %copy-start.3 = (f32[4,64,256]{2,1,0:T(8,128)S(1)}, f32[4,64,256]{2,1,0:T(8,128)}, u32[]{:S(2)}) copy-start(f32[4,64,256]{2,1,0:T(8,128)} %get-tuple-element.66) | copy-start | bytes 786436
  256.1 5.5 %copy-start.5 = (f32[4,2048]{1,0:T(4,128)S(1)}, f32[4,2048]{1,0:T(4,128)}, u32[]{:S(2)}) copy-start(f32[4,2048]{1,0:T(4,128)} %get-tuple-element.94) | copy-start | bytes 98308
  256.1 6.1 %copy-start.4 = (f32[16,512]{1,0:T(8,128)S(1)}, f32[16,512]{1,0:T(8,128)}, u32[]{:S(2)}) copy-start(f32[16,512]{1,0:T(8,128)} %get-tuple-element.95) | copy-start | bytes 98308
  256.1 6.7 %copy-start.6 = (f32[4,1536]{1,0:T(4,128)S(1)}, f32[4,1536]{1,0:T(4,128)}, u32[]{:S(2)}) copy-start(f32[4,1536]{1,0:T(4,128)} %get-tuple-element.96) | copy-start | bytes 73732
  256.1 7.3 %copy-start.7 = (f32[4,512]{1,0:T(4,128)S(1)}, f32[4,512]{1,0:T(4,128)}, u32[]{:S(2)}) copy-start(f32[4,512]{1,0:T(4,128)} %get-tuple-element.97) | copy-start | bytes 24580

commit v3 on v2

--- a/solution.py
+++ b/solution.py
@@ -540,8 +540,8 @@
 
 
 def expand_kernel(
-    x_ref, got_ref, w_ref, taps_ref, mixed_ref, slope_mix_ref, slope_ref, main_ref, side_out_ref,
-    pooled_ref, edge_ref, normed, normed_side, side, pre, pre_side, padded, ends
+    x_ref, got_ref, w_ref, taps_ref, mixed_ref, slope_mix_ref, slope_ref, main_ref,
+    pooled_ref, edge_ref, normed, normed_side, side, pre, pre_side, padded, ends, slopes, mains, shifted
 ):
     step = pl.program_id(0)
 
@@ -559,7 +559,7 @@
             layer_normalize(got_ref[COLS : 2 * COLS, :])[0] * masks[1]
         ).astype(jnp.bfloat16)
 
-        @pl.loop(0, ROWS)
+        @pl.loop(0, ROWS, unroll=2)
         def _(y):
             rows = pl.ds(pl.multiple_of(y * COLS, COLS), COLS)
             after = pl.ds(pl.multiple_of((y + 1) * COLS, COLS), COLS)
@@ -569,33 +569,31 @@
     pre[...] = jnp.dot(normed[...], w_ref[...], preferred_element_type=jnp.float32)
     pre_side[...] = jnp.dot(normed_side[...], w_ref[...], preferred_element_type=jnp.float32)
 
-    @pl.loop(0, ROWS + 2)
+    @pl.loop(0, ROWS + 2, unroll=3)
     def _(y):
         rows = pl.ds(pl.multiple_of(y * COLS, COLS), COLS)
         result, slope = gelu_slope(pre[rows, :])
         rounded = result.astype(jnp.bfloat16)
-        main_ref[rows, :] = rounded
-        padded[y, 8 : 8 + COLS, :] = rounded.astype(jnp.float32)
-
-        @pl.when((y > 0) & (y <= ROWS))
-        def _():
-            before = pl.ds(pl.multiple_of((y - 1) * COLS, COLS), COLS)
-            slope_ref[before, :] = slope
-
+        mains[rows, :] = rounded
+        wide = rounded.astype(jnp.float32)
+        padded[y, 8 : 8 + COLS, :] = wide
+        shifted[1, y] = wide
+        slopes[rows, :] = slope
         eight = pl.ds(pl.multiple_of(y * 8, 8), 8)
         edge = gelu_slope(pre_side[eight, :])[0].astype(jnp.bfloat16).astype(jnp.float32)
-        pre_side[eight, :] = edge
         padded[y, 0:8, :] = edge
         padded[y, 8 + COLS : 16 + COLS, :] = edge
-
-    side_out_ref[...] = pre_side[...].astype(jnp.bfloat16)
+        shifted[0, y] = padded[y, 7 : 7 + COLS, :]
+        shifted[2, y] = padded[y, 9 : 9 + COLS, :]
+
+    slope_ref[...] = slopes[COLS : MAIN - COLS, :]
+    main_ref[...] = mains[COLS : MAIN - COLS, :]
 
     def mix(y, total):
         summed = jnp.zeros((COLS, width), jnp.float32)
         for r in range(3):
             for c in range(3):
-                window = padded[y + r, 7 + c : 7 + c + COLS, :]
-                summed = summed + window * taps_ref[3 * r + c : 3 * r + c + 1, :]
+                summed = summed + shifted[c, y + r] * taps_ref[3 * r + c : 3 * r + c + 1, :]
         mixed, slope = gelu_slope(summed)
         rows = pl.ds(pl.multiple_of(y * COLS, COLS), COLS)
         mixed_ref[rows, :] = mixed
@@ -635,8 +633,7 @@
             wide,
             wide,
             wide,
-            jax.ShapeDtypeStruct((MAIN, hidden), jnp.bfloat16),
-            jax.ShapeDtypeStruct((SIDE, hidden), jnp.bfloat16),
+            jax.ShapeDtypeStruct((tokens, hidden), jnp.bfloat16),
             jax.ShapeDtypeStruct((steps, width // 128, 128), jnp.float32),
             jax.ShapeDtypeStruct((EDGE, hidden), jnp.bfloat16),
         ),
@@ -645,8 +642,7 @@
             moving(tokens),
             moving(tokens),
             moving(tokens),
-            moving(MAIN),
-            moving(SIDE),
+            moving(tokens),
             pl.BlockSpec((1, width // 128, 128), lambda e: (e, 0, 0)),
             moving(EDGE),
         ],
@@ -658,6 +654,9 @@
             pltpu.VMEM((SIDE, width), jnp.float32),
             pltpu.VMEM((ROWS + 2, COLS + 16, width), jnp.float32),
             pltpu.VMEM((2, ROWS, width), jnp.float32),
+            pltpu.VMEM((MAIN, width), jnp.float32),
+            pltpu.VMEM((MAIN, width), jnp.bfloat16),
+            pltpu.VMEM((3, ROWS + 2, COLS, width), jnp.float32),
         ],
         compiler_params=pltpu.CompilerParams(vmem_limit_bytes=60 * 1024 * 1024),
     )(tokens_in, got, w_expand, taps)
@@ -853,8 +852,8 @@
 
 def back_kernel(
     scaled_grad_ref, slope_mix_ref, slope_got_ref, grad_got_ref, gate_ref, pooled_ref, project_ref,
-    main_ref, side_in_ref, slope_ref, w_ref, taps_ref, x_ref, grad_ref,
-    out_ref, parts_ref, terms_ref, got_ref, turned, side, padded, expanded, preexp, total, flat, place
+    main_ref, slope_ref, w_ref, taps_ref, x_ref, grad_ref,
+    out_ref, parts_ref, terms_ref, got_ref, turned, side, padded, shifted, preexp, total, flat, place
 ):
     step = pl.program_id(0)
     last = pl.num_programs(0) - 1
@@ -877,51 +876,42 @@
     )
     masks = edge_masks()
     fill_sides(got_ref, side, masks, 4)
-    padded[0, 8 : 8 + COLS, :] = got_ref[0:COLS, :].astype(jnp.float32) * masks[0]
-    padded[ROWS + 1, 8 : 8 + COLS, :] = got_ref[COLS : 2 * COLS, :].astype(jnp.float32) * masks[1]
-
-    @pl.loop(0, ROWS)
+    padded[0, 8 : 8 + COLS, :] = got_ref[0:COLS, :] * masks[0]
+    padded[ROWS + 1, 8 : 8 + COLS, :] = got_ref[COLS : 2 * COLS, :] * masks[1]
+
+    @pl.loop(0, ROWS, unroll=2)
     def _(y):
         rows = pl.ds(pl.multiple_of(y * COLS, COLS), COLS)
         padded[y + 1, 8 : 8 + COLS, :] = premix(scaled_grad_ref[rows, :], slope_mix_ref[rows, :])
 
-    pairs = (ROWS + 2) // 2
-
-    @pl.loop(0, ROWS + 2)
+    @pl.loop(0, ROWS + 2, unroll=3)
     def _(y):
-        rows = pl.ds(pl.multiple_of(y * COLS, COLS), COLS)
-        expanded[y, 8 : 8 + COLS, :] = main_ref[rows, :].astype(jnp.float32)
         eight = pl.ds(pl.multiple_of(y * 8, 8), 8)
         edge = jnp.concatenate([side[tile, eight, :] for tile in range(4)], axis=-1)
         padded[y, 0:8, :] = edge
         padded[y, 8 + COLS : 16 + COLS, :] = edge
-
-    @pl.loop(0, pairs)
-    def _(y):
-        both = side_in_ref[pl.ds(pl.multiple_of(y * 16, 16), 16), :].astype(jnp.float32)
-        for k in range(2):
-            edge = both[8 * k : 8 * k + 8]
-            expanded[2 * y + k, 0:8, :] = edge
-            expanded[2 * y + k, 8 + COLS : 16 + COLS, :] = edge
+        shifted[0, y] = padded[y, 7 : 7 + COLS, :]
+        shifted[1, y] = padded[y, 8 : 8 + COLS, :]
+        shifted[2, y] = padded[y, 9 : 9 + COLS, :]
 
     for low in range(0, 512, 256):
         lanes = slice(low, low + 256)
 
         def unmix(y, sums):
             rows = pl.ds(pl.multiple_of(y * COLS, COLS), COLS)
-            own = padded[y + 1, 8 : 8 + COLS, lanes]
+            own = main_ref[rows, lanes].astype(jnp.float32)
             summed = jnp.zeros((COLS, 256), jnp.float32)
             new = []
             for r in range(3):
                 for c in range(3):
-                    window = padded[y + 2 - r, 9 - c : 9 - c + COLS, lanes]
+                    window = shifted[2 - c, y + 2 - r, :, lanes]
                     summed = summed + window * taps_ref[3 * r + c : 3 * r + c + 1, lanes]
-                    term = own * expanded[y + r, 7 + c : 7 + c + COLS, lanes]
+                    term = own * window
                     new.append(sums[3 * r + c] + jnp.sum(term.reshape(-1, 8, 256), axis=0))
             preexp[rows, lanes] = (summed * slope_ref[rows, lanes]).astype(jnp.bfloat16)
             return tuple(new)
 
-        sums = lax.fori_loop(0, ROWS, unmix, (jnp.zeros((8, 256), jnp.float32),) * 9)
+        sums = lax.fori_loop(0, ROWS, unmix, (jnp.zeros((8, 256), jnp.float32),) * 9, unroll=2)
         for k in range(9):
             terms_ref[k : k + 1, lanes] = jnp.sum(sums[k], axis=0, keepdims=True)
 
@@ -939,7 +929,7 @@
                 place[tile].reshape(128, 16, 128).astype(jnp.bfloat16)
             )
 
-        @pl.loop(0, ROWS)
+        @pl.loop(0, ROWS, unroll=2)
         def _(y):
             rows = pl.ds(pl.multiple_of(y * COLS, COLS), COLS)
             standard, inverse = layer_normalize(x_ref[rows, :])
@@ -949,7 +939,7 @@
 
 
 def mix_backward(
-    scaled_grad, slope_mix, slope_got, grad_got, gate, pooled_grad, w_project, main, side, slope,
+    scaled_grad, slope_mix, slope_got, grad_got, gate, pooled_grad, w_project, main, slope,
     w_expand, taps, tokens_in, grad
 ):
     tokens, hidden = scaled_grad.shape
@@ -978,8 +968,7 @@
             moving(1),
             moving(1),
             pl.BlockSpec((width, channels), lambda e: (e, 0)),
-            moving(MAIN),
-            moving(SIDE),
+            moving(tokens),
             moving(tokens),
             moving(channels),
             moving(9),
@@ -992,7 +981,7 @@
             pltpu.VMEM((channels, tokens), jnp.bfloat16),
             pltpu.VMEM((4, SIDE, 128), jnp.float32),
             pltpu.VMEM((ROWS + 2, COLS + 16, width), jnp.float32),
-            pltpu.VMEM((ROWS + 2, COLS + 16, width), jnp.float32),
+            pltpu.VMEM((3, ROWS + 2, COLS, width), jnp.float32),
             pltpu.VMEM((tokens, width), jnp.bfloat16),
             pltpu.VMEM((tokens, channels), jnp.float32),
             pltpu.VMEM((4, tokens, 128), jnp.float32),
@@ -1000,7 +989,7 @@
         ],
         compiler_params=pltpu.CompilerParams(vmem_limit_bytes=60 * 1024 * 1024),
     )(
-        scaled_grad, slope_mix, slope_got, grad_got, gate, pooled_grad, w_project, main, side, slope,
+        scaled_grad, slope_mix, slope_got, grad_got, gate, pooled_grad, w_project, main, slope,
         w_expand, taps, tokens_in, grad
     )
 
@@ -1009,6 +998,7 @@
 QUAD = 4
 PLACES = 64
 GROUPS = 8
+STAGE = 4
 
 
 def attention_kernel(
@@ -1028,6 +1018,7 @@
     cot_ref,
     flat,
     place,
+    turned,
 ):
     channels = wout_ref.shape[0]
     factor = HEAD_DIM ** (-0.5)
@@ -1078,44 +1069,48 @@
     @pl.loop(0, GROUPS)
     def _(group):
         rows = pl.ds(pl.multiple_of(group * PLACES, PLACES), PLACES)
-        for quad in range(4):
-            low = quad * 128
-            queries = qkv[rows, low : low + 128]
-            keys_in = qkv[rows, channels + low : channels + low + 128]
-            values_in = qkv[rows, 2 * channels + low : 2 * channels + low + 128]
-            grads = cgrad[rows, low : low + 128]
-            queries_wide = widen(queries)
-            grads_wide = widen(grads)
-            scores = (
-                lax.dot_general(keys_in, queries_wide, BACKWARD, preferred_element_type=jnp.float32)
-                * factor
-                + bias_ref[quad]
-            )
-            scores = jnp.exp(scores - jnp.max(scores, axis=0, keepdims=True))
-            weights = scores * (1.0 / jnp.sum(scores, axis=0, keepdims=True))
-            weights_b = weights.astype(jnp.bfloat16)
-            context = narrow(
-                lax.dot_general(weights_b, values_in, CONTRACT, preferred_element_type=jnp.float32)
-            )
-            context_ref[rows, low : low + 128] = context.astype(jnp.bfloat16)
-            weights_grad = lax.dot_general(
-                values_in, grads_wide, BACKWARD, preferred_element_type=jnp.float32
-            )
-            values_grad = jnp.dot(weights_b, grads_wide, preferred_element_type=jnp.float32)
-            scores_grad = weights * (
-                weights_grad - jnp.sum(weights * weights_grad, axis=0, keepdims=True)
-            )
-            table_ref[quad] += scores_grad
-            scores_b = (scores_grad * factor).astype(jnp.bfloat16)
-            queries_grad = narrow(
-                lax.dot_general(scores_b, keys_in, CONTRACT, preferred_element_type=jnp.float32)
-            )
-            keys_grad = jnp.dot(scores_b, queries_wide, preferred_element_type=jnp.float32)
-            proj_ref[rows, low : low + 128] = queries_grad.astype(jnp.bfloat16)
-            proj_ref[rows, channels + low : channels + low + 128] = keys_grad.astype(jnp.bfloat16)
-            proj_ref[rows, 2 * channels + low : 2 * channels + low + 128] = values_grad.astype(
-                jnp.bfloat16
-            )
+        for first in range(0, 4, STAGE):
+            quads = range(first, first + STAGE)
+            lows = [quad * 128 for quad in quads]
+            queries = [qkv[rows, low : low + 128] for low in lows]
+            keys_in = [qkv[rows, channels + low : channels + low + 128] for low in lows]
+            values_in = [qkv[rows, 2 * channels + low : 2 * channels + low + 128] for low in lows]
+            grads = [cgrad[rows, low : low + 128] for low in lows]
+            queries_wide = [widen(block) for block in queries]
+            grads_wide = [widen(block) for block in grads]
+
+            def product(left, right, dims):
+                return [
+                    lax.dot_general(x, y, dims, preferred_element_type=jnp.float32)
+                    for x, y in zip(left, right)
+                ]
+
+            plain = (((1,), (0,)), ((), ()))
+            scores = product(keys_in, queries_wide, BACKWARD)
+            weights_grad = product(values_in, grads_wide, BACKWARD)
+            scores = [x * factor + bias_ref[quad] for x, quad in zip(scores, quads)]
+            scores = [jnp.exp(x - jnp.max(x, axis=0, keepdims=True)) for x in scores]
+            weights = [x * (1.0 / jnp.sum(x, axis=0, keepdims=True)) for x in scores]
+            weights_b = [x.astype(jnp.bfloat16) for x in weights]
+            context = product(weights_b, values_in, CONTRACT)
+            values_grad = product(weights_b, grads_wide, plain)
+            scores_grad = [
+                x * (y - jnp.sum(x * y, axis=0, keepdims=True))
+                for x, y in zip(weights, weights_grad)
+            ]
+            scores_b = [(x * factor).astype(jnp.bfloat16) for x in scores_grad]
+            queries_grad = product(scores_b, keys_in, CONTRACT)
+            keys_grad = product(scores_b, queries_wide, plain)
+            for k, (quad, low) in enumerate(zip(quads, lows)):
+                table_ref[quad] += scores_grad[k]
+                context_ref[rows, low : low + 128] = narrow(context[k]).astype(jnp.bfloat16)
+                proj_ref[rows, low : low + 128] = narrow(queries_grad[k]).astype(jnp.bfloat16)
+                proj_ref[rows, channels + low : channels + low + 128] = keys_grad[k].astype(
+                    jnp.bfloat16
+                )
+                proj_ref[rows, 2 * channels + low : 2 * channels + low + 128] = values_grad[
+                    k
+                ].astype(jnp.bfloat16)
 
     def scatter(read, first_row):
         for group in range(GROUPS):
@@ -1151,12 +1146,12 @@
             spread[tile].reshape(64, 16, 128).astype(jnp.bfloat16)
         )
 
+    turned[...] = normed_ref[...].T
     for q in range(3):
         regroup(
-            lax.dot_general(
-                normed_ref[...],
+            jnp.dot(
+                turned[...],
                 proj_ref[:, q * channels : (q + 1) * channels],
-                CONTRACT,
                 preferred_element_type=jnp.float32,
             ),
             flat,
@@ -1200,6 +1195,7 @@
             pltpu.VMEM((tokens, channels), jnp.bfloat16),
             pltpu.VMEM((4, tokens, 128), jnp.float32),
             pltpu.VMEM((4, 2048, 128), jnp.float32),
+            pltpu.VMEM((channels, tokens), jnp.bfloat16),
         ],
         compiler_params=pltpu.CompilerParams(vmem_limit_bytes=60 * 1024 * 1024),
     )(blocks, w_qkv, w_out, bias)
@@ -1227,7 +1223,7 @@
     flat_inputs = inputs.reshape(tokens, channels)
     flattened_cotangent = out_grad.reshape(tokens, channels)
     taps = dw_kernel.reshape(9, hidden_units)
-    mixed, slope_mix, slope_expand, main, side, pooled, slope_edges = expand_and_mix(
+    mixed, slope_mix, slope_expand, main, pooled, slope_edges = expand_and_mix(
         flat_inputs, halo(inputs[0], 5), w_expand, taps
     )
     pooled, slope_got = sum_and_halo(pooled.reshape(-1, 128), slope_edges, 3)
@@ -1273,7 +1269,6 @@
         pooled_grad / cells,
         w_project,
         main,
-        side,
         slope_expand,
         w_expand,
         taps,

time: 265 us -> 240 us (0.906)
  Pallas kernels: 233 us -> 208 us
    pallas_call x1, Pallas kernels: 27.9 us -> 16.2 us  [attention(): pl.pallas_call(attention_kernel, out_shape=shapes, in_specs=[pl.BlockSpec...]
    pallas_call x1, Pallas kernels: 31 us -> 22.4 us  [mix_backward(): pl.pallas_call(back_kernel, grid=(hidden // width,), out_shape=(jax.Shape...]
    pallas_call x1, Pallas kernels: 26.5 us -> 21.4 us  [expand_and_mix(): pl.pallas_call(expand_kernel, grid=(steps,), out_shape=(wide, wide, wide,...]
where the time goes in v3:
time: 240 us; the launch traced here: 239 us
  Pallas kernels  208 us (87%)
  matrix products  11.3 us (5%)
  local copies, waits for them, and re-layouts  11 us (5%)
  other arithmetic  7.45 us (3%)
    pallas_call x2, Pallas kernels, swap(): pl.pallas_call(functools.partial(swap_kernel, parity, GRID, lax.axis_size...  47.2 us
    pallas_call x1, Pallas kernels, reduce_all(): pl.pallas_call(functools.partial(reduce_kernel, rows, cols, factor), out_...  38.2 us
    pallas_call x2, Pallas kernels, sum_and_halo(): pl.pallas_call(functools.partial(sum_halo_kernel, rows, cols), out_shape=...  33.4 us
    pallas_call x1, Pallas kernels, mix_backward(): pl.pallas_call(back_kernel, grid=(hidden // width,), out_shape=(jax.Shape...  22.4 us
    pallas_call x1, Pallas kernels, expand_and_mix(): pl.pallas_call(expand_kernel, grid=(steps,), out_shape=(wide, wide, wide,...  21.4 us
    pallas_call x1, Pallas kernels, attention(): pl.pallas_call(attention_kernel, out_shape=shapes, in_specs=[pl.BlockSpec...  16.2 us
    pallas_call x1, Pallas kernels, halo(): pl.pallas_call(body, out_shape=jax.ShapeDtypeStruct((total, features), ce...  12.7 us
    pallas_call x1, Pallas kernels, middle_backward(): pl.pallas_call(middle_kernel, grid=(tokens // height,), out_shape=(jax.Sh...  9.58 us

profile of v3, /device:TPU:0, one launch (start us, length us, event | category | flops | bytes accessed | tf_op | source)
XLA Modules:
  0.0 238.7 jit_solution(1612302788764047951)
XLA Ops:
  0.7 0.1 subtract_add_fusion
  0.8 0.1 reshape.229
  0.8 1.5 slice_bitcast_fusion
  2.3 1.6 reshape.211.taps_ref
  3.9 2.0 convolution_bitcast_fusion
  6.0 0.2 reshape.214
  6.2 0.3 copy.29
  6.5 1.0 reshape.215.bias_ref
  7.6 0.3 copy.30
  7.9 0.6 slice_bitcast_fusion.2
  8.5 12.7 %shard_map.177.got_ref = bf16[160,512]{1,0:T(8,128)(2,1)} custom-call(bf16[32,512]{1,0:T(8,128)(2,1)} %get-tuple-element.73.refs_0_, bf16[32,512]{1,0:T(8,128)(2,1)} %get-tuple-element.72.refs_1_, bf16[16,512]{1,0:T(8,128)(2,1)} %get-tuple-element.71.refs_2_, bf16[16,512]{1,0:T(8,128)(2,1)} %get-tuple-element.70.refs_3_), custom_call_target="tpu_custom_call" | custom-call | tf_op jit(solution)/shard_map/pallas_call | solution.py:120
  21.2 21.4 %shard_map.178 = (f32[512,2048]{1,0:T(8,128)}, f32[512,2048]{1,0:T(8,128)}, f32[512,2048]{1,0:T(8,128)}, bf16[512,2048]{1,0:T(8,128)(2,1)}, f32[8,2,128]{2,1,0:T(2,128)}, /*index=5*/bf16[96,2048]{1,0:T(8,128)(2,1)}) custom-call(bf16[512,512]{1,0:T(8,128)(2,1)} %bitcast.68, bf16[160,512]{1,0:T(8,128)(2,1)} %shard_map.177.got_ref, bf16[512,2048]{1,0:T(8,128)(2,1)} %w_ref.5, ...), custom_call_target="tpu_custom_call" | custom-call | tf_op jit(solution)/shard_map/pallas_call | solution.py:629
  42.6 16.2 %shard_map.179 = (f32[16,128]{1,0:T(8,128)}, bf16[160,2048]{1,0:T(8,128)(2,1)}) custom-call(f32[16,128]{1,0:T(8,128)} %bitcast.89, bf16[96,2048]{1,0:T(8,128)(2,1)} %get-tuple-element.42.edge_ref), custom_call_target="tpu_custom_call" | custom-call | tf_op jit(solution)/shard_map/pallas_call | solution.py:435
  58.9 0.7 fusion.10
  59.6 0.6 fusion.11
  60.2 0.0 copy-done.2
  60.2 0.6 fusion.8
  60.8 0.6 add_divide_fusion
  61.4 7.0 %shard_map.180 = (bf16[512,2048]{1,0:T(8,128)(2,1)}, f32[512,512]{1,0:T(8,128)}, bf16[64,32,256]{2,1,0:T(8,128)(2,1)}) custom-call(f32[512,2048]{1,0:T(8,128)} %get-tuple-element.40.mixed_ref, f32[1,2048]{1,0:T(1,128)} %bitcast.83, bf16[512,512]{1,0:T(8,128)(2,1)} %bitcast.69, bf16[512,512]{1,0:T(8,128)(2,1)} %bitcast.74, bf16[2048,512]{1,0:T(8,128)(2,1)} %project_ref.1), custom_call_target="tpu_custom_call" | custom-call | tf_op jit(solution)/shard_map/pallas_call | solution.py:706
  68.4 24.7 %shard_map.181.x_ref = bf16[64,32,256]{2,1,0:T(8,128)(2,1)} custom-call(bf16[64,32,256]{2,1,0:T(8,128)(2,1)} %get-tuple-element.44.x_ref), custom_call_target="tpu_custom_call" | custom-call | tf_op jit(solution)/shard_map/pallas_call | solution.py:497
  93.1 16.2 %shard_map.182 = (bf16[64,32,256]{2,1,0:T(8,128)(2,1)}, bf16[128,16,512]{2,1,0:T(8,128)(2,1)}, f32[4,64,256]{2,1,0:T(8,128)}) custom-call(bf16[64,32,256]{2,1,0:T(8,128)(2,1)} %shard_map.181.x_ref, bf16[512,1536]{1,0:T(8,128)(2,1)} %wqkv_ref.1, bf16[512,512]{1,0:T(8,128)(2,1)} %wout_ref.3, f32[4,64,256]{2,1,0:T(8,128)} %reshape.215.bias_ref), custom_call_target="tpu_custom_call" | custom-call | tf_op jit(solution)/shard_map/pallas_call | solution.py:1183
  109.3 22.5 %shard_map.183.ret_ref = bf16[64,32,256]{2,1,0:T(8,128)(2,1)} custom-call(bf16[64,32,256]{2,1,0:T(8,128)(2,1)} %get-tuple-element.45.x_ref), custom_call_target="tpu_custom_call" | custom-call | tf_op jit(solution)/shard_map/pallas_call | solution.py:497
  131.9 9.6 %shard_map.184 = (bf16[512,512]{1,0:T(8,128)(2,1)}, f32[512,512]{1,0:T(8,128)}, bf16[512,512]{1,0:T(8,128)(2,1)}, f32[512,2048]{1,0:T(8,128)}, f32[16,128]{1,0:T(8,128)}, /*index=5*/bf16[96,512]{1,0:T(8,128)(2,1)}) custom-call(bf16[64,32,256]{2,1,0:T(8,128)(2,1)} %shard_map.183.ret_ref, f32[512,512]{1,0:T(8,128)} %get-tuple-element.46.middle_ref, ...), custom_call_target="tpu_custom_call" | custom-call | tf_op jit(solution)/shard_map/pallas_call | solution.py:806
  141.4 4.4 %convolution_convert_fusion = bf16[2048,512]{1,0:T(8,128)(2,1)} fusion(bf16[512,2048]{1,0:T(8,128)(2,1)} %get-tuple-element.59, bf16[512,512]{1,0:T(8,128)(2,1)} %get-tuple-element.60), kind=kOutput, calls=%fused_computation.3 | convolution fusion | flops 1074790400 | bytes 4718592 | tf_op jit(solution)/shard_map/dot_general | solution.py:1253
  145.8 17.2 %shard_map.185 = (f32[16,128]{1,0:T(8,128)}, bf16[160,512]{1,0:T(8,128)(2,1)}) custom-call(f32[16,128]{1,0:T(8,128)} %get-tuple-element.51.x_ref, bf16[96,512]{1,0:T(8,128)(2,1)} %get-tuple-element.52.edge_ref), custom_call_target="tpu_custom_call" | custom-call | tf_op jit(solution)/shard_map/pallas_call | solution.py:435
  163.0 0.7 fusion.5
  163.7 0.9 fusion.4
  164.6 1.0 fusion.6
  165.6 0.6 broadcast_multiply_fusion
  166.2 22.4 %shard_map.186 = (bf16[512,512]{1,0:T(8,128)(2,1)}, bf16[128,16,512]{2,1,0:T(8,128)(2,1)}, f32[9,2048]{1,0:T(8,128)}) custom-call(f32[512,2048]{1,0:T(8,128)} %get-tuple-element.48.scaled_grad_ref, f32[512,2048]{1,0:T(8,128)} %get-tuple-element.49.slope_mix_ref, bf16[160,2048]{1,0:T(8,128)(2,1)} %get-tuple-element.50.slope_got_ref, ...), custom_call_target="tpu_custom_call" | custom-call | tf_op jit(solution)/shard_map/pallas_call | solution.py:955
  188.6 0.9 reshape.221
  189.5 0.2 reshape.222
  189.8 0.1 copy.28
  189.8 0.2 reshape.223
  190.0 1.8 fusion
  191.8 0.1 reshape.224
  191.9 0.7 select_maximum_fusion
  192.6 38.2 %shard_map.187 = (f32[16,512]{1,0:T(8,128)}, f32[4,2048]{1,0:T(4,128)}, f32[4,1536]{1,0:T(4,128)}, f32[4,512]{1,0:T(4,128)}, f32[16,16,128]{2,1,0:T(8,128)}) custom-call(bf16[4,4,4,2,16,512]{5,4,3,2,1,0:T(8,128)(2,1)} %bitcast.72, bf16[4,4,4,2,16,512]{5,4,3,2,1,0:T(8,128)(2,1)} %bitcast.73, bf16[4,4,4,2,16,512]{5,4,3,2,1,0:T(8,128)(2,1)} %bitcast.71, ...), custom_call_target="tpu_custom_call" | custom-call | tf_op jit(solution)/shard_map/pallas_call | solution.py:326
  230.8 0.7 slice_multiply_fusion.1
  231.6 0.7 mul.84
  232.3 0.9 slice_multiply_fusion
  233.2 0.7 mul.77
  233.8 1.3 multiply_multiply_fusion.1
  235.1 1.1 multiply_multiply_fusion
  236.3 0.6 copy.35
  236.9 0.6 copy.36
  237.5 0.6 copy.37
  238.1 0.6 copy.38
  (16 shorter events, 0.0 us)
Async XLA Ops:
  0.6 58.9 %copy-start = (f32[2048,128]{1,0:T(8,128)S(1)}, f32[2048,128]{1,0:T(8,128)}, u32[]{:S(2)}) copy-start(f32[2048,128]{1,0:T(8,128)} %param.14) | copy-start | bytes 3145732
  0.7 6.9 %copy-start.1 = (bf16[1,16,32,512]{3,2,1,0:T(8,128)(2,1)S(1)}, bf16[1,16,32,512]{3,2,1,0:T(8,128)(2,1)}, u32[]{:S(2)}) copy-start(bf16[1,16,32,512]{3,2,1,0:T(8,128)(2,1)} %param.10) | copy-start | bytes 1572868
  21.2 39.0 %copy-start.2 = (f32[128,2048]{1,0:T(8,128)S(1)}, f32[128,2048]{1,0:T(8,128)}, u32[]{:S(2)}) copy-start(f32[128,2048]{1,0:T(8,128)} %param.15) | copy-start | bytes 3145732
  166.2 23.3 %copy-start.3 = (f32[4,64,256]{2,1,0:T(8,128)S(1)}, f32[4,64,256]{2,1,0:T(8,128)}, u32[]{:S(2)}) copy-start(f32[4,64,256]{2,1,0:T(8,128)} %get-tuple-element.64) | copy-start | bytes 786436
  230.8 5.5 %copy-start.5 = (f32[4,2048]{1,0:T(4,128)S(1)}, f32[4,2048]{1,0:T(4,128)}, u32[]{:S(2)}) copy-start(f32[4,2048]{1,0:T(4,128)} %get-tuple-element.92) | copy-start | bytes 98308
  230.8 6.1 %copy-start.4 = (f32[16,512]{1,0:T(8,128)S(1)}, f32[16,512]{1,0:T(8,128)}, u32[]{:S(2)}) copy-start(f32[16,512]{1,0:T(8,128)} %get-tuple-element.93) | copy-start | bytes 98308
  230.8 6.7 %copy-start.6 = (f32[4,1536]{1,0:T(4,128)S(1)}, f32[4,1536]{1,0:T(4,128)}, u32[]{:S(2)}) copy-start(f32[4,1536]{1,0:T(4,128)} %get-tuple-element.94) | copy-start | bytes 73732
  230.8 7.3 %copy-start.7 = (f32[4,512]{1,0:T(4,128)S(1)}, f32[4,512]{1,0:T(4,128)}, u32[]{:S(2)}) copy-start(f32[4,512]{1,0:T(4,128)} %get-tuple-element.95) | copy-start | bytes 24580

commit v4 on v3

--- a/solution.py
+++ b/solution.py
@@ -131,7 +131,8 @@
 
 def reduce_kernel(
     rows, cols, factor, w0_ref, w1_ref, w2_ref, s_ref, project_ref, expand_ref, qkv_ref, out_ref,
-    so_ref, half, buf1, buf2, buf3, sum1, sum2, rs_buf, own_buf, col_buf, sems, pair_sems, axis_sems
+    so_ref, mine, half, buf1, buf2, buf3, sum1, sum2, rs_buf, own_buf, col_buf, sems, pair_sems,
+    axis_sems
 ):
     row = lax.axis_index("row")
     col = lax.axis_index("col")
@@ -164,6 +165,12 @@
             device_id_type=MESH,
         ).start()
 
+    kept = [
+        pltpu.make_async_copy(w_refs[p].at[:, :, :, core], mine.at[p], pair_sems.at[2, p])
+        for p in range(3)
+    ]
+    for copy in kept:
+        copy.start()
     signal(pair)
     for axis in range(3):
         for k in range(1, 4):
@@ -200,15 +207,15 @@
     orders = ((0, 1, 2), (1, 2, 0), (2, 0, 1))
     for p in range(3):
         first = orders[p][0]
+        kept[p].wait()
         wait_like(half.at[p], pair_sems.at[1, p])
-        w_ref = w_refs[p]
 
         @pl.loop(0, 16)
         def _(i):
             y, x = i // 4, lax.rem(i, 4)
             for z in range(4):
-                mine = w_ref[y, x, z, core].astype(jnp.float32) + half[p, y, x, z].astype(jnp.float32)
-                half[p, y, x, z] = mine.astype(jnp.bfloat16)
+                both = mine[p, y, x, z].astype(jnp.float32) + half[p, y, x, z].astype(jnp.float32)
+                half[p, y, x, z] = both.astype(jnp.bfloat16)
 
         for k in range(1, 4):
             place = lax.rem(me[first] + k, 4)
@@ -332,9 +339,10 @@
             jax.ShapeDtypeStruct((4, 512), jnp.float32),
             jax.ShapeDtypeStruct(small.shape, jnp.float32),
         ),
-        in_specs=[vmem] * 4,
+        in_specs=[pl.BlockSpec(memory_space=pl.ANY)] * 3 + [vmem],
         out_specs=[vmem] * 5,
         scratch_shapes=[
+            held(4, 4, 4),
             held(4, 4, 4),
             held(4, 4, 4),
             held(4, 4),
@@ -345,7 +353,7 @@
             pltpu.VMEM(block, jnp.float32),
             pltpu.VMEM((cols,) + block, jnp.float32),
             pltpu.SemaphoreType.DMA((6,)),
-            pltpu.SemaphoreType.DMA((2, 3)),
+            pltpu.SemaphoreType.DMA((3, 3)),
             pltpu.SemaphoreType.DMA((2, 3, 3)),
         ],
         compiler_params=pltpu.CompilerParams(
@@ -497,8 +505,8 @@
     return pl.pallas_call(
         functools.partial(swap_kernel, parity, GRID, lax.axis_size("col")),
         out_shape=jax.ShapeDtypeStruct(parts.shape, parts.dtype),
-        in_specs=[pl.BlockSpec(memory_space=pltpu.VMEM)],
-        out_specs=pl.BlockSpec(memory_space=pltpu.VMEM),
+        in_specs=[pl.BlockSpec(memory_space=pl.ANY)],
+        out_specs=pl.BlockSpec(memory_space=pl.ANY),
         scratch_shapes=[pltpu.SemaphoreType.DMA((3,))],
         compiler_params=pltpu.CompilerParams(
             collective_id=number, has_side_effects=True, vmem_limit_bytes=60 * 1024 * 1024
@@ -569,7 +577,7 @@
     pre[...] = jnp.dot(normed[...], w_ref[...], preferred_element_type=jnp.float32)
     pre_side[...] = jnp.dot(normed_side[...], w_ref[...], preferred_element_type=jnp.float32)
 
-    @pl.loop(0, ROWS + 2, unroll=3)
+    @pl.loop(0, ROWS + 2, unroll=6)
     def _(y):
         rows = pl.ds(pl.multiple_of(y * COLS, COLS), COLS)
         result, slope = gelu_slope(pre[rows, :])
@@ -593,7 +601,7 @@
         summed = jnp.zeros((COLS, width), jnp.float32)
         for r in range(3):
             for c in range(3):
-                summed = summed + shifted[c, y + r] * taps_ref[3 * r + c : 3 * r + c + 1, :]
+                summed = summed + shifted[c, y + r] * taps_ref[r, c : c + 1, :]
         mixed, slope = gelu_slope(summed)
         rows = pl.ds(pl.multiple_of(y * COLS, COLS), COLS)
         mixed_ref[rows, :] = mixed
@@ -625,6 +633,7 @@
     def moving(height):
         return pl.BlockSpec((height, width), lambda e: (0, e))
 
+    taps_spec = pl.BlockSpec((3, 3, width), lambda e: (0, 0, e))
     wide = jax.ShapeDtypeStruct((tokens, hidden), jnp.float32)
     return pl.pallas_call(
         expand_kernel,
@@ -637,7 +646,7 @@
             jax.ShapeDtypeStruct((steps, width // 128, 128), jnp.float32),
             jax.ShapeDtypeStruct((EDGE, hidden), jnp.bfloat16),
         ),
-        in_specs=[fixed(tokens_in.shape), fixed(got.shape), moving(channels), moving(9)],
+        in_specs=[fixed(tokens_in.shape), fixed(got.shape), moving(channels), taps_spec],
         out_specs=[
             moving(tokens),
             moving(tokens),
@@ -852,8 +861,8 @@
 
 def back_kernel(
     scaled_grad_ref, slope_mix_ref, slope_got_ref, grad_got_ref, gate_ref, pooled_ref, project_ref,
-    main_ref, slope_ref, w_ref, taps_ref, x_ref, grad_ref,
-    out_ref, parts_ref, terms_ref, got_ref, turned, side, padded, shifted, preexp, total, flat, place
+    main_ref, slope_ref, w_ref, taps_ref, x_ref, grad_ref, scaled_ref, grad_b_ref,
+    out_ref, parts_ref, terms_ref, project_parts_ref, got_ref, turned, side, padded, shifted, preexp, total, flat, place
 ):
     step = pl.program_id(0)
     last = pl.num_programs(0) - 1
@@ -879,12 +888,12 @@
     padded[0, 8 : 8 + COLS, :] = got_ref[0:COLS, :] * masks[0]
     padded[ROWS + 1, 8 : 8 + COLS, :] = got_ref[COLS : 2 * COLS, :] * masks[1]
 
-    @pl.loop(0, ROWS, unroll=2)
+    @pl.loop(0, ROWS, unroll=4)
     def _(y):
         rows = pl.ds(pl.multiple_of(y * COLS, COLS), COLS)
         padded[y + 1, 8 : 8 + COLS, :] = premix(scaled_grad_ref[rows, :], slope_mix_ref[rows, :])
 
-    @pl.loop(0, ROWS + 2, unroll=3)
+    @pl.loop(0, ROWS + 2, unroll=6)
     def _(y):
         eight = pl.ds(pl.multiple_of(y * 8, 8), 8)
         edge = jnp.concatenate([side[tile, eight, :] for tile in range(4)], axis=-1)
@@ -905,16 +914,23 @@
             for r in range(3):
                 for c in range(3):
                     window = shifted[2 - c, y + 2 - r, :, lanes]
-                    summed = summed + window * taps_ref[3 * r + c : 3 * r + c + 1, lanes]
+                    summed = summed + window * taps_ref[r, c : c + 1, lanes]
                     term = own * window
                     new.append(sums[3 * r + c] + jnp.sum(term.reshape(-1, 8, 256), axis=0))
             preexp[rows, lanes] = (summed * slope_ref[rows, lanes]).astype(jnp.bfloat16)
             return tuple(new)
 
-        sums = lax.fori_loop(0, ROWS, unmix, (jnp.zeros((8, 256), jnp.float32),) * 9, unroll=2)
+        sums = lax.fori_loop(0, ROWS, unmix, (jnp.zeros((8, 256), jnp.float32),) * 9, unroll=4)
         for k in range(9):
             terms_ref[k : k + 1, lanes] = jnp.sum(sums[k], axis=0, keepdims=True)
 
+    project_parts_ref[...] = (
+        lax.dot_general(
+            scaled_ref[...], grad_b_ref[...], CONTRACT, preferred_element_type=jnp.float32
+        )
+        .astype(jnp.bfloat16)
+        .reshape(project_parts_ref.shape)
+    )
     regroup(
         jnp.dot(turned[...], preexp[...], preferred_element_type=jnp.float32), flat, place, step * 4
     )
@@ -929,7 +945,7 @@
                 place[tile].reshape(128, 16, 128).astype(jnp.bfloat16)
             )
 
-        @pl.loop(0, ROWS, unroll=2)
+        @pl.loop(0, ROWS, unroll=4)
         def _(y):
             rows = pl.ds(pl.multiple_of(y * COLS, COLS), COLS)
             standard, inverse = layer_normalize(x_ref[rows, :])
@@ -940,7 +956,7 @@
 
 def mix_backward(
     scaled_grad, slope_mix, slope_got, grad_got, gate, pooled_grad, w_project, main, slope,
-    w_expand, taps, tokens_in, grad
+    w_expand, taps, tokens_in, grad, scaled, grad_b
 ):
     tokens, hidden = scaled_grad.shape
     channels = w_expand.shape[0]
@@ -959,6 +975,7 @@
             jax.ShapeDtypeStruct((tokens, channels), jnp.bfloat16),
             jax.ShapeDtypeStruct((128, 16, width), jnp.bfloat16),
             jax.ShapeDtypeStruct((9, hidden), jnp.float32),
+            jax.ShapeDtypeStruct((hidden // 16, 16, channels), jnp.bfloat16),
         ),
         in_specs=[
             moving(tokens),
@@ -971,11 +988,18 @@
             moving(tokens),
             moving(tokens),
             moving(channels),
-            moving(9),
+            pl.BlockSpec((3, 3, width), lambda e: (0, 0, e)),
             fixed(tokens_in.shape),
             fixed(grad.shape),
+            moving(tokens),
+            fixed(grad_b.shape),
         ],
-        out_specs=[fixed((tokens, channels)), fixed((128, 16, width)), moving(9)],
+        out_specs=[
+            fixed((tokens, channels)),
+            fixed((128, 16, width)),
+            moving(9),
+            pl.BlockSpec((width // 16, 16, channels), lambda e: (e, 0, 0)),
+        ],
         scratch_shapes=[
             pltpu.VMEM(slope_got.shape[:1] + (width,), jnp.float32),
             pltpu.VMEM((channels, tokens), jnp.bfloat16),
@@ -990,7 +1014,7 @@
         compiler_params=pltpu.CompilerParams(vmem_limit_bytes=60 * 1024 * 1024),
     )(
         scaled_grad, slope_mix, slope_got, grad_got, gate, pooled_grad, w_project, main, slope,
-        w_expand, taps, tokens_in, grad
+        w_expand, taps, tokens_in, grad, scaled, grad_b
     )
 
 
@@ -1222,9 +1246,8 @@
     )
     flat_inputs = inputs.reshape(tokens, channels)
     flattened_cotangent = out_grad.reshape(tokens, channels)
-    taps = dw_kernel.reshape(9, hidden_units)
     mixed, slope_mix, slope_expand, main, pooled, slope_edges = expand_and_mix(
-        flat_inputs, halo(inputs[0], 5), w_expand, taps
+        flat_inputs, halo(inputs[0], 5), w_expand, dw_kernel
     )
     pooled, slope_got = sum_and_halo(pooled.reshape(-1, 128), slope_edges, 3)
     pooled = pooled.reshape(images, -1) / cells
@@ -1249,18 +1272,13 @@
     )
     gate_grad, grad_got = sum_and_halo(gate_grad, grad_edges, 4)
     gate_grad = gate_grad.reshape(images, -1)
-    project_parts = (
-        lax.dot_general(scaled, middle_b, CONTRACT, preferred_element_type=jnp.float32)
-        .astype(jnp.bfloat16)
-        .reshape(128, 16, channels)
-    )
     excite_grad = gate_grad * gate * (1.0 - gate)
     squeezed_grad = lax.dot_general(excite_grad, se_expand, BACKWARD, precision=HIGHEST)
     squeeze_grad = squeezed_grad * squeeze_sig * (1.0 + squeeze_pre * (1.0 - squeeze_sig))
     pooled_grad = lax.dot_general(squeeze_grad, se_reduce, BACKWARD, precision=HIGHEST)
     se_reduce_grad = lax.dot_general(pooled, squeeze_grad, CONTRACT, precision=HIGHEST) * factor
     se_expand_grad = lax.dot_general(squeezed, excite_grad, CONTRACT, precision=HIGHEST) * factor
-    input_gradient, expand_parts, kernel_part = mix_backward(
+    input_gradient, expand_parts, kernel_part, project_parts = mix_backward(
         scaled_grad,
         slope_mix,
         slope_got,
@@ -1271,9 +1289,11 @@
         main,
         slope_expand,
         w_expand,
-        taps,
+        dw_kernel,
         flat_inputs,
         middle_gradient,
+        scaled,
+        middle_b,
     )
     small = jnp.concatenate([kernel_part.reshape(-1), table_part.reshape(-1)])
     unit = lax.axis_size("row") * 1024

time: 240 us -> 233 us (0.971)
  Pallas kernels: 208 us -> 203 us
  matrix products: 11.3 us -> 6.97 us
  local copies, waits for them, and re-layouts: 11 us -> 14.2 us
    dot_general x1 -> x0, matrix products: 4.35 us -> none  [on_device(): lax.dot_general(scaled, middle_b, CONTRACT, preferred_element_type=jnp.fl...]
    pallas_call x2, Pallas kernels: 47.2 us -> 43.7 us  [swap(): pl.pallas_call(functools.partial(swap_kernel, parity, GRID, lax.axis_size...]
    unnamed x21 -> x13, local copies, waits for them, and re-layouts: 2.78 us -> 5.71 us
where the time goes in v4:
time: 233 us; the launch traced here: 232 us
  Pallas kernels  203 us (87%)
  local copies, waits for them, and re-layouts  14.2 us (6%)
  other arithmetic  7.43 us (3%)
  matrix products  6.97 us (3%)
    pallas_call x2, Pallas kernels, swap(): pl.pallas_call(functools.partial(swap_kernel, parity, GRID, lax.axis_size...  43.7 us
    pallas_call x1, Pallas kernels, reduce_all(): pl.pallas_call(functools.partial(reduce_kernel, rows, cols, factor), out_...  36.4 us
    pallas_call x2, Pallas kernels, sum_and_halo(): pl.pallas_call(functools.partial(sum_halo_kernel, rows, cols), out_shape=...  33.6 us
    pallas_call x1, Pallas kernels, mix_backward(): pl.pallas_call(back_kernel, grid=(hidden // width,), out_shape=(jax.Shape...  22.9 us
    pallas_call x1, Pallas kernels, expand_and_mix(): pl.pallas_call(expand_kernel, grid=(steps,), out_shape=(wide, wide, wide,...  20.6 us
    pallas_call x1, Pallas kernels, attention(): pl.pallas_call(attention_kernel, out_shape=shapes, in_specs=[pl.BlockSpec...  16.2 us
    pallas_call x1, Pallas kernels, halo(): pl.pallas_call(body, out_shape=jax.ShapeDtypeStruct((total, features), ce...  12.7 us
    pallas_call x1, Pallas kernels, middle_backward(): pl.pallas_call(middle_kernel, grid=(tokens // height,), out_shape=(jax.Sh...  9.58 us

profile of v4, /device:TPU:0, one launch (start us, length us, event | category | flops | bytes accessed | tf_op | source)
XLA Modules:
  0.0 232.1 jit_solution(5176854318582554790)
XLA Ops:
  0.6 0.0 copy-start
  0.7 0.1 subtract_add_fusion
  0.8 0.1 reshape.229
  0.8 1.5 slice_bitcast_fusion
  2.3 2.0 convolution_bitcast_fusion
  4.4 0.2 reshape.213
  4.6 0.0 copy-start.2
  4.6 1.1 copy.29
  5.7 2.1 reshape.214.bias_ref
  7.8 0.3 copy.30
  8.1 0.6 slice_bitcast_fusion.2
  8.7 12.7 %shard_map.177.got_ref = bf16[160,512]{1,0:T(8,128)(2,1)} custom-call(bf16[32,512]{1,0:T(8,128)(2,1)} %get-tuple-element.75.refs_0_, bf16[32,512]{1,0:T(8,128)(2,1)} %get-tuple-element.74.refs_1_, bf16[16,512]{1,0:T(8,128)(2,1)} %get-tuple-element.73.refs_2_, bf16[16,512]{1,0:T(8,128)(2,1)} %get-tuple-element.72.refs_3_), custom_call_target="tpu_custom_call" | custom-call | tf_op jit(solution)/shard_map/pallas_call | solution.py:120
  21.4 20.6 %shard_map.178 = (f32[512,2048]{1,0:T(8,128)}, f32[512,2048]{1,0:T(8,128)}, f32[512,2048]{1,0:T(8,128)}, bf16[512,2048]{1,0:T(8,128)(2,1)}, f32[8,2,128]{2,1,0:T(2,128)}, /*index=5*/bf16[96,2048]{1,0:T(8,128)(2,1)}) custom-call(bf16[512,512]{1,0:T(8,128)(2,1)} %bitcast.66, bf16[160,512]{1,0:T(8,128)(2,1)} %shard_map.177.got_ref, bf16[512,2048]{1,0:T(8,128)(2,1)} %w_ref.5, ...), custom_call_target="tpu_custom_call" | custom-call | tf_op jit(solution)/shard_map/pallas_call | solution.py:638
  42.0 16.2 %shard_map.179 = (f32[16,128]{1,0:T(8,128)}, bf16[160,2048]{1,0:T(8,128)(2,1)}) custom-call(f32[16,128]{1,0:T(8,128)} %bitcast.87, bf16[96,2048]{1,0:T(8,128)(2,1)} %get-tuple-element.43.edge_ref), custom_call_target="tpu_custom_call" | custom-call | tf_op jit(solution)/shard_map/pallas_call | solution.py:443
  58.2 0.7 fusion.10
  59.0 0.6 fusion.11
  59.6 0.0 copy-done.2
  59.6 0.6 fusion.8
  60.2 0.6 add_divide_fusion
  60.8 7.0 %shard_map.180 = (bf16[512,2048]{1,0:T(8,128)(2,1)}, f32[512,512]{1,0:T(8,128)}, bf16[64,32,256]{2,1,0:T(8,128)(2,1)}) custom-call(f32[512,2048]{1,0:T(8,128)} %get-tuple-element.41.mixed_ref, f32[1,2048]{1,0:T(1,128)} %bitcast.78, bf16[512,512]{1,0:T(8,128)(2,1)} %bitcast.67, bf16[512,512]{1,0:T(8,128)(2,1)} %bitcast.72, bf16[2048,512]{1,0:T(8,128)(2,1)} %project_ref.1), custom_call_target="tpu_custom_call" | custom-call | tf_op jit(solution)/shard_map/pallas_call | solution.py:715
  67.8 23.0 %shard_map.181.x_ref = bf16[64,32,256]{2,1,0:T(8,128)(2,1)} custom-call(bf16[64,32,256]{2,1,0:T(8,128)(2,1)} %get-tuple-element.45.x_ref), custom_call_target="tpu_custom_call" | custom-call | tf_op jit(solution)/shard_map/pallas_call | solution.py:505
  90.8 16.2 %shard_map.182 = (bf16[64,32,256]{2,1,0:T(8,128)(2,1)}, bf16[128,16,512]{2,1,0:T(8,128)(2,1)}, f32[4,64,256]{2,1,0:T(8,128)}) custom-call(bf16[64,32,256]{2,1,0:T(8,128)(2,1)} %shard_map.181.x_ref, bf16[512,1536]{1,0:T(8,128)(2,1)} %wqkv_ref.1, bf16[512,512]{1,0:T(8,128)(2,1)} %wout_ref.3, f32[4,64,256]{2,1,0:T(8,128)} %reshape.214.bias_ref), custom_call_target="tpu_custom_call" | custom-call | tf_op jit(solution)/shard_map/pallas_call | solution.py:1207
  107.0 20.7 %shard_map.183.ret_ref = bf16[64,32,256]{2,1,0:T(8,128)(2,1)} custom-call(bf16[64,32,256]{2,1,0:T(8,128)(2,1)} %get-tuple-element.46.x_ref), custom_call_target="tpu_custom_call" | custom-call | tf_op jit(solution)/shard_map/pallas_call | solution.py:505
  127.7 9.6 %shard_map.184 = (bf16[512,512]{1,0:T(8,128)(2,1)}, f32[512,512]{1,0:T(8,128)}, bf16[512,512]{1,0:T(8,128)(2,1)}, f32[512,2048]{1,0:T(8,128)}, f32[16,128]{1,0:T(8,128)}, /*index=5*/bf16[96,512]{1,0:T(8,128)(2,1)}) custom-call(bf16[64,32,256]{2,1,0:T(8,128)(2,1)} %shard_map.183.ret_ref, f32[512,512]{1,0:T(8,128)} %get-tuple-element.47.middle_ref, ...), custom_call_target="tpu_custom_call" | custom-call | tf_op jit(solution)/shard_map/pallas_call | solution.py:815
  137.3 17.4 %shard_map.185 = (f32[16,128]{1,0:T(8,128)}, bf16[160,512]{1,0:T(8,128)(2,1)}) custom-call(f32[16,128]{1,0:T(8,128)} %get-tuple-element.52.x_ref, bf16[96,512]{1,0:T(8,128)(2,1)} %get-tuple-element.53.edge_ref), custom_call_target="tpu_custom_call" | custom-call | tf_op jit(solution)/shard_map/pallas_call | solution.py:443
  154.7 0.7 fusion.5
  155.4 0.9 fusion.4
  156.4 1.0 fusion.6
  157.3 0.6 broadcast_multiply_fusion
  157.9 22.9 %shard_map.186 = (bf16[512,512]{1,0:T(8,128)(2,1)}, bf16[128,16,512]{2,1,0:T(8,128)(2,1)}, f32[9,2048]{1,0:T(8,128)}, bf16[128,16,512]{2,1,0:T(8,128)(2,1)}) custom-call(f32[512,2048]{1,0:T(8,128)} %get-tuple-element.49.scaled_grad_ref, f32[512,2048]{1,0:T(8,128)} %get-tuple-element.50.slope_mix_ref, bf16[160,2048]{1,0:T(8,128)(2,1)} %get-tuple-element.51.slope_got_ref, ...), custom_call_target="tpu_custom_call" | custom-call | tf_op jit(solution)/shard_map/pallas_call | solution.py:971
  180.8 0.9 reshape.221
  181.8 0.2 reshape.222
  182.0 0.1 copy.28
  182.1 0.2 reshape.223
  182.3 1.8 fusion
  184.1 0.1 reshape.224
  184.2 0.7 select_maximum_fusion
  184.9 36.4 %shard_map.187 = (f32[16,512]{1,0:T(8,128)}, f32[4,2048]{1,0:T(4,128)}, f32[4,1536]{1,0:T(4,128)}, f32[4,512]{1,0:T(4,128)}, f32[16,16,128]{2,1,0:T(8,128)}) custom-call(bf16[4,4,4,2,16,512]{5,4,3,2,1,0:T(8,128)(2,1)} %bitcast.71, bf16[4,4,4,2,16,512]{5,4,3,2,1,0:T(8,128)(2,1)} %bitcast.70, bf16[4,4,4,2,16,512]{5,4,3,2,1,0:T(8,128)(2,1)} %bitcast.69, ...), custom_call_target="tpu_custom_call" | custom-call | tf_op jit(solution)/shard_map/pallas_call | solution.py:333
  221.3 0.7 slice_multiply_fusion.1
  222.0 0.7 mul.84
  222.7 0.9 slice_multiply_fusion
  223.6 0.7 mul.77
  224.3 1.3 multiply_multiply_fusion.1
  225.6 1.1 multiply_multiply_fusion
  226.7 1.4 copy.35
  228.0 1.4 copy.36
  229.4 1.3 copy.37
  230.8 1.3 copy.38
  (6 shorter events, 0.0 us)
Async XLA Ops:
  0.6 58.3 %copy-start = (f32[2048,128]{1,0:T(8,128)S(1)}, f32[2048,128]{1,0:T(8,128)}, u32[]{:S(2)}) copy-start(f32[2048,128]{1,0:T(8,128)} %param.14) | copy-start | bytes 3145732
  0.7 7.2 %copy-start.1 = (bf16[1,16,32,512]{3,2,1,0:T(8,128)(2,1)S(1)}, bf16[1,16,32,512]{3,2,1,0:T(8,128)(2,1)}, u32[]{:S(2)}) copy-start(bf16[1,16,32,512]{3,2,1,0:T(8,128)(2,1)} %param.10) | copy-start | bytes 1572868
  4.6 55.0 %copy-start.2 = (f32[128,2048]{1,0:T(8,128)S(1)}, f32[128,2048]{1,0:T(8,128)}, u32[]{:S(2)}) copy-start(f32[128,2048]{1,0:T(8,128)} %param.15) | copy-start | bytes 3145732
  157.9 23.8 %copy-start.3 = (f32[4,64,256]{2,1,0:T(8,128)S(1)}, f32[4,64,256]{2,1,0:T(8,128)}, u32[]{:S(2)}) copy-start(f32[4,64,256]{2,1,0:T(8,128)} %get-tuple-element.66) | copy-start | bytes 786436

commit v5 on v4

--- a/solution.py
+++ b/solution.py
@@ -624,7 +624,7 @@
 def expand_and_mix(tokens_in, got, w_expand, taps):
     tokens, channels = tokens_in.shape
     hidden = w_expand.shape[1]
-    width = 256
+    width = 512
     steps = hidden // width
 
     def fixed(shape):

time: 233 us -> 232 us (level)
  no operation moved by 1% of the time
where the time goes in v5:
time: 232 us; the launch traced here: 231 us
  Pallas kernels  201 us (87%)
  local copies, waits for them, and re-layouts  14.2 us (6%)
  other arithmetic  7.43 us (3%)
  matrix products  6.97 us (3%)
    pallas_call x2, Pallas kernels, swap(): pl.pallas_call(functools.partial(swap_kernel, parity, GRID, lax.axis_size...  43.8 us
    pallas_call x1, Pallas kernels, reduce_all(): pl.pallas_call(functools.partial(reduce_kernel, rows, cols, factor), out_...  36.4 us
    pallas_call x2, Pallas kernels, sum_and_halo(): pl.pallas_call(functools.partial(sum_halo_kernel, rows, cols), out_shape=...  33.6 us
    pallas_call x1, Pallas kernels, mix_backward(): pl.pallas_call(back_kernel, grid=(hidden // width,), out_shape=(jax.Shape...  22.9 us
    pallas_call x1, Pallas kernels, expand_and_mix(): pl.pallas_call(expand_kernel, grid=(steps,), out_shape=(wide, wide, wide,...  19.2 us
    pallas_call x1, Pallas kernels, attention(): pl.pallas_call(attention_kernel, out_shape=shapes, in_specs=[pl.BlockSpec...  16.2 us
    pallas_call x1, Pallas kernels, halo(): pl.pallas_call(body, out_shape=jax.ShapeDtypeStruct((total, features), ce...  12.7 us
    pallas_call x1, Pallas kernels, middle_backward(): pl.pallas_call(middle_kernel, grid=(tokens // height,), out_shape=(jax.Sh...  9.58 us

profile of v5, /device:TPU:0, one launch (start us, length us, event | category | flops | bytes accessed | tf_op | source)
XLA Modules:
  0.0 230.7 jit_solution(16327033190929304609)
XLA Ops:
  0.6 0.0 copy-start
  0.7 0.1 subtract_add_fusion
  0.8 0.1 reshape.229
  0.8 1.5 slice_bitcast_fusion
  2.3 2.0 convolution_bitcast_fusion
  4.4 0.2 reshape.213
  4.6 0.0 copy-start.2
  4.6 1.1 copy.29
  5.7 2.1 reshape.214.bias_ref
  7.8 0.3 copy.30
  8.1 0.6 slice_bitcast_fusion.2
  8.7 12.7 %shard_map.177.got_ref = bf16[160,512]{1,0:T(8,128)(2,1)} custom-call(bf16[32,512]{1,0:T(8,128)(2,1)} %get-tuple-element.75.refs_0_, bf16[32,512]{1,0:T(8,128)(2,1)} %get-tuple-element.74.refs_1_, bf16[16,512]{1,0:T(8,128)(2,1)} %get-tuple-element.73.refs_2_, bf16[16,512]{1,0:T(8,128)(2,1)} %get-tuple-element.72.refs_3_), custom_call_target="tpu_custom_call" | custom-call | tf_op jit(solution)/shard_map/pallas_call | solution.py:120
  21.4 19.2 %shard_map.178 = (f32[512,2048]{1,0:T(8,128)}, f32[512,2048]{1,0:T(8,128)}, f32[512,2048]{1,0:T(8,128)}, bf16[512,2048]{1,0:T(8,128)(2,1)}, f32[4,4,128]{2,1,0:T(4,128)}, /*index=5*/bf16[96,2048]{1,0:T(8,128)(2,1)}) custom-call(bf16[512,512]{1,0:T(8,128)(2,1)} %bitcast.66, bf16[160,512]{1,0:T(8,128)(2,1)} %shard_map.177.got_ref, bf16[512,2048]{1,0:T(8,128)(2,1)} %w_ref.5, ...), custom_call_target="tpu_custom_call" | custom-call | tf_op jit(solution)/shard_map/pallas_call | solution.py:638
  40.7 16.2 %shard_map.179 = (f32[16,128]{1,0:T(8,128)}, bf16[160,2048]{1,0:T(8,128)(2,1)}) custom-call(f32[16,128]{1,0:T(8,128)} %bitcast.87, bf16[96,2048]{1,0:T(8,128)(2,1)} %get-tuple-element.43.edge_ref), custom_call_target="tpu_custom_call" | custom-call | tf_op jit(solution)/shard_map/pallas_call | solution.py:443
  56.9 0.7 fusion.10
  57.6 0.6 fusion.11
  58.3 0.0 copy-done.2
  58.3 0.6 fusion.8
  58.9 0.6 add_divide_fusion
  59.5 7.0 %shard_map.180 = (bf16[512,2048]{1,0:T(8,128)(2,1)}, f32[512,512]{1,0:T(8,128)}, bf16[64,32,256]{2,1,0:T(8,128)(2,1)}) custom-call(f32[512,2048]{1,0:T(8,128)} %get-tuple-element.41.mixed_ref, f32[1,2048]{1,0:T(1,128)} %bitcast.78, bf16[512,512]{1,0:T(8,128)(2,1)} %bitcast.67, bf16[512,512]{1,0:T(8,128)(2,1)} %bitcast.72, bf16[2048,512]{1,0:T(8,128)(2,1)} %project_ref.1), custom_call_target="tpu_custom_call" | custom-call | tf_op jit(solution)/shard_map/pallas_call | solution.py:715
  66.5 23.0 %shard_map.181.x_ref = bf16[64,32,256]{2,1,0:T(8,128)(2,1)} custom-call(bf16[64,32,256]{2,1,0:T(8,128)(2,1)} %get-tuple-element.45.x_ref), custom_call_target="tpu_custom_call" | custom-call | tf_op jit(solution)/shard_map/pallas_call | solution.py:505
  89.5 16.2 %shard_map.182 = (bf16[64,32,256]{2,1,0:T(8,128)(2,1)}, bf16[128,16,512]{2,1,0:T(8,128)(2,1)}, f32[4,64,256]{2,1,0:T(8,128)}) custom-call(bf16[64,32,256]{2,1,0:T(8,128)(2,1)} %shard_map.181.x_ref, bf16[512,1536]{1,0:T(8,128)(2,1)} %wqkv_ref.1, bf16[512,512]{1,0:T(8,128)(2,1)} %wout_ref.3, f32[4,64,256]{2,1,0:T(8,128)} %reshape.214.bias_ref), custom_call_target="tpu_custom_call" | custom-call | tf_op jit(solution)/shard_map/pallas_call | solution.py:1207
  105.7 20.7 %shard_map.183.ret_ref = bf16[64,32,256]{2,1,0:T(8,128)(2,1)} custom-call(bf16[64,32,256]{2,1,0:T(8,128)(2,1)} %get-tuple-element.46.x_ref), custom_call_target="tpu_custom_call" | custom-call | tf_op jit(solution)/shard_map/pallas_call | solution.py:505
  126.5 9.6 %shard_map.184 = (bf16[512,512]{1,0:T(8,128)(2,1)}, f32[512,512]{1,0:T(8,128)}, bf16[512,512]{1,0:T(8,128)(2,1)}, f32[512,2048]{1,0:T(8,128)}, f32[16,128]{1,0:T(8,128)}, /*index=5*/bf16[96,512]{1,0:T(8,128)(2,1)}) custom-call(bf16[64,32,256]{2,1,0:T(8,128)(2,1)} %shard_map.183.ret_ref, f32[512,512]{1,0:T(8,128)} %get-tuple-element.47.middle_ref, ...), custom_call_target="tpu_custom_call" | custom-call | tf_op jit(solution)/shard_map/pallas_call | solution.py:815
  136.0 17.3 %shard_map.185 = (f32[16,128]{1,0:T(8,128)}, bf16[160,512]{1,0:T(8,128)(2,1)}) custom-call(f32[16,128]{1,0:T(8,128)} %get-tuple-element.52.x_ref, bf16[96,512]{1,0:T(8,128)(2,1)} %get-tuple-element.53.edge_ref), custom_call_target="tpu_custom_call" | custom-call | tf_op jit(solution)/shard_map/pallas_call | solution.py:443
  153.4 0.7 fusion.5
  154.1 0.9 fusion.4
  155.0 1.0 fusion.6
  156.0 0.6 broadcast_multiply_fusion
  156.6 22.9 %shard_map.186 = (bf16[512,512]{1,0:T(8,128)(2,1)}, bf16[128,16,512]{2,1,0:T(8,128)(2,1)}, f32[9,2048]{1,0:T(8,128)}, bf16[128,16,512]{2,1,0:T(8,128)(2,1)}) custom-call(f32[512,2048]{1,0:T(8,128)} %get-tuple-element.49.scaled_grad_ref, f32[512,2048]{1,0:T(8,128)} %get-tuple-element.50.slope_mix_ref, bf16[160,2048]{1,0:T(8,128)(2,1)} %get-tuple-element.51.slope_got_ref, ...), custom_call_target="tpu_custom_call" | custom-call | tf_op jit(solution)/shard_map/pallas_call | solution.py:971
  179.5 0.9 reshape.221
  180.4 0.2 reshape.222
  180.7 0.1 copy.28
  180.7 0.2 reshape.223
  180.9 1.8 fusion
  182.7 0.1 reshape.224
  182.8 0.7 select_maximum_fusion
  183.5 36.4 %shard_map.187 = (f32[16,512]{1,0:T(8,128)}, f32[4,2048]{1,0:T(4,128)}, f32[4,1536]{1,0:T(4,128)}, f32[4,512]{1,0:T(4,128)}, f32[16,16,128]{2,1,0:T(8,128)}) custom-call(bf16[4,4,4,2,16,512]{5,4,3,2,1,0:T(8,128)(2,1)} %bitcast.71, bf16[4,4,4,2,16,512]{5,4,3,2,1,0:T(8,128)(2,1)} %bitcast.70, bf16[4,4,4,2,16,512]{5,4,3,2,1,0:T(8,128)(2,1)} %bitcast.69, ...), custom_call_target="tpu_custom_call" | custom-call | tf_op jit(solution)/shard_map/pallas_call | solution.py:333
  219.9 0.7 slice_multiply_fusion.1
  220.6 0.7 mul.84
  221.4 0.9 slice_multiply_fusion
  222.2 0.7 mul.77
  222.9 1.3 multiply_multiply_fusion.1
  224.2 1.1 multiply_multiply_fusion
  225.3 1.4 copy.35
  226.7 1.4 copy.36
  228.1 1.3 copy.37
  229.4 1.3 copy.38
  (6 shorter events, 0.0 us)
Async XLA Ops:
  0.6 57.0 %copy-start = (f32[2048,128]{1,0:T(8,128)S(1)}, f32[2048,128]{1,0:T(8,128)}, u32[]{:S(2)}) copy-start(f32[2048,128]{1,0:T(8,128)} %param.14) | copy-start | bytes 3145732
  0.7 7.2 %copy-start.1 = (bf16[1,16,32,512]{3,2,1,0:T(8,128)(2,1)S(1)}, bf16[1,16,32,512]{3,2,1,0:T(8,128)(2,1)}, u32[]{:S(2)}) copy-start(bf16[1,16,32,512]{3,2,1,0:T(8,128)(2,1)} %param.10) | copy-start | bytes 1572868
  4.6 53.7 %copy-start.2 = (f32[128,2048]{1,0:T(8,128)S(1)}, f32[128,2048]{1,0:T(8,128)}, u32[]{:S(2)}) copy-start(f32[128,2048]{1,0:T(8,128)} %param.15) | copy-start | bytes 3145732
  156.6 23.8 %copy-start.3 = (f32[4,64,256]{2,1,0:T(8,128)S(1)}, f32[4,64,256]{2,1,0:T(8,128)}, u32[]{:S(2)}) copy-start(f32[4,64,256]{2,1,0:T(8,128)} %get-tuple-element.66) | copy-start | bytes 786436
